TPU v7x, 256 devices: a whole 4x4x8 slice. The times are simulated.
256 devices in a mesh: ctx: 128 (over x, z, y), head: 2 (over core).
Axes of the slice: x: 4, y: 4, z: 8, core: 2. Of those that a mesh axis runs over, the one named last changes fastest.
Arguments:
- shared_qk: bfloat16 [16384, 2048], P('ctx', 'head'), may hold values from -6 to 6
- values: bfloat16 [16384, 2048], P('ctx', 'head'), may hold values from -12 to 12
- out_grad: bfloat16 [16384, 2048], P('ctx', 'head'), may hold values from -6 to 6
- out_weight: bfloat16 [2048, 2048], P('ctx', 'head'), may hold values from -0.125 to 0.125
- buckets: int32 [2, 16384], P(None, 'ctx'), may hold values from 0 to 127, as said below
Outputs:
- mixed: bfloat16 [16384, 2048], P('ctx', 'head')
- grad_qk: bfloat16 [16384, 2048], P('ctx', 'head')
- grad_values: bfloat16 [16384, 2048], P('ctx', 'head')
- grad_weight: float32 [2048, 2048], P('ctx', 'head')
Inputs may be any that keep to these rules, and one draw needn't show every extreme that they name: `buckets`: in each round at most 2 of the tokens of one device share a bucket, and one bucket takes exactly 2 tokens from every device.
All inputs are finite; a program needn't handle non-finite values.
Results may differ from a plain program's by a relative error of at most 0.012.
The roundings to bfloat16 on the way count: a program that leaves them out, or rounds other values in their place, can miss the bound.
Values may be sent and summed in bfloat16 or wider, within the bound.
No kernel may reach another device: no remote copies, remote signals or barrier semaphores. Data moves between devices by JAX's collectives and lax.ppermute only.
A program may use at most 128 MiB of HBM per device.

v0:
```python
import math

import jax
import jax.numpy as jnp
from jax import lax
from jax.sharding import PartitionSpec as P

HEAD_DIM = 128
SPAN = 128


self_penalty = 10000.0
masked_score = -1e30


def with_zero_row(matrix):
    return jnp.concatenate([matrix, jnp.zeros((1,) + matrix.shape[1:], matrix.dtype)], axis=0)


def key_windows(rows):
    row_count = rows.shape[0]
    leading = jnp.zeros((SPAN,) + rows.shape[1:], rows.dtype)
    earlier = jnp.concatenate([leading, rows[: row_count - SPAN]], axis=0)
    shape_out = (row_count // SPAN, SPAN) + rows.shape[1:]
    return jnp.concatenate([earlier.reshape(shape_out), rows.reshape(shape_out)], axis=1)


def fold_windows(stacked):
    current = stacked[:, SPAN:]
    earlier = stacked[:, :SPAN]
    return current + jnp.concatenate([earlier[1:], jnp.zeros_like(earlier[:1])], axis=0)


def span_probs(queries, key_rows, key_live):
    scores = jnp.einsum(
        "qhd,khd->hqk", queries, key_rows, preferred_element_type=jnp.float32
    ) * HEAD_DIM ** (-0.5)
    itself = jnp.arange(2 * SPAN)[None, :] == jnp.arange(SPAN)[:, None] + SPAN
    scores = jnp.where(itself[None], scores - self_penalty, scores)
    scores = jnp.where(key_live[None, None, :], scores, masked_score)
    largest = jnp.max(scores, axis=-1, keepdims=True)
    lifted = jnp.exp(scores - largest)
    summed = jnp.sum(lifted, axis=-1, keepdims=True)
    return (lifted / summed, (largest + jnp.log(summed))[..., 0])


def owner_forward(own_qk, own_values, occupied, local_heads):
    blocks = own_qk.shape[0] // SPAN
    queries = own_qk.reshape(blocks, SPAN, local_heads, HEAD_DIM)
    key_rows = key_windows(own_qk).reshape(blocks, 2 * SPAN, local_heads, HEAD_DIM)
    value_rows = key_windows(own_values).reshape(blocks, 2 * SPAN, local_heads, HEAD_DIM)
    live_keys = key_windows(occupied)

    def one_block(pieces):
        block_query, block_key, block_value, block_live = pieces
        probability, log_total = span_probs(block_query, block_key, block_live)
        result = jnp.einsum(
            "hqk,khd->qhd",
            probability.astype(jnp.bfloat16),
            block_value,
            preferred_element_type=jnp.float32,
        )
        return (result.astype(jnp.bfloat16).reshape(SPAN, local_heads * HEAD_DIM), log_total.T)

    outputs, log_totals = lax.map(one_block, (queries, key_rows, value_rows, live_keys))
    return (outputs.reshape(-1, local_heads * HEAD_DIM), log_totals.reshape(-1, local_heads))


def owner_backward(own_qk, own_values, occupied, own_grad, own_shift, local_heads):
    blocks = own_qk.shape[0] // SPAN
    queries = own_qk.reshape(blocks, SPAN, local_heads, HEAD_DIM)
    key_rows = key_windows(own_qk).reshape(blocks, 2 * SPAN, local_heads, HEAD_DIM)
    value_rows = key_windows(own_values).reshape(blocks, 2 * SPAN, local_heads, HEAD_DIM)
    live_keys = key_windows(occupied)
    grad_rows = own_grad.reshape(blocks, SPAN, local_heads, HEAD_DIM)
    shift_rows = own_shift.reshape(blocks, SPAN, local_heads)

    def one_block(pieces):
        block_query, block_key, block_value, block_live, block_grad, block_shift = pieces
        probability, log_total = span_probs(block_query, block_key, block_live)
        prob_grad = jnp.einsum(
            "qhd,khd->hqk", block_grad, block_value, preferred_element_type=jnp.float32
        )
        score_grad = (probability * (prob_grad - block_shift.T[:, :, None])).astype(jnp.bfloat16)
        query_grad = jnp.einsum(
            "hqk,khd->qhd", score_grad, block_key, preferred_element_type=jnp.float32
        ) * HEAD_DIM ** (-0.5)
        key_grad = jnp.einsum(
            "hqk,qhd->khd", score_grad, block_query, preferred_element_type=jnp.float32
        ) * HEAD_DIM ** (-0.5)
        value_grad = jnp.einsum(
            "hqk,qhd->khd",
            probability.astype(jnp.bfloat16),
            block_grad,
            preferred_element_type=jnp.float32,
        )
        return (query_grad, key_grad, value_grad)

    query_grad, key_grad, value_grad = lax.map(
        one_block, (queries, key_rows, value_rows, live_keys, grad_rows, shift_rows)
    )
    row_width = local_heads * HEAD_DIM
    qk_rows = (query_grad + fold_windows(key_grad)).reshape(-1, row_width).astype(jnp.bfloat16)
    value_out = fold_windows(value_grad).reshape(-1, row_width).astype(jnp.bfloat16)
    return (qk_rows, value_out)


def route_round(bucket_row, peer_count, per_peer, token_rows):
    owners = jnp.arange(peer_count, dtype=jnp.int32)
    member = (bucket_row[:, None] == owners[None, :]).astype(jnp.int32)
    earlier = jnp.cumsum(member, axis=0) - member
    position = jnp.sum(earlier * member, axis=1)
    slot_index = bucket_row * per_peer + position
    slot_token = (
        jnp.full((peer_count * per_peer,), token_rows, jnp.int32)
        .at[slot_index]
        .set(jnp.arange(token_rows, dtype=jnp.int32))
    )
    return (slot_index, slot_token)


def compact_slots(slot_marks, capacity):
    target = jnp.cumsum(slot_marks) - 1
    target = jnp.where(slot_marks > 0, target, capacity).astype(jnp.int32)
    source_slot = (
        jnp.full((capacity,), capacity, jnp.int32)
        .at[target]
        .set(jnp.arange(capacity, dtype=jnp.int32), mode="drop")
    )
    return (source_slot, target)


def per_device(shared_qk, values, out_grad, out_weight, buckets):
    token_rows, row_width = shared_qk.shape
    local_heads = row_width // HEAD_DIM
    peer_count = lax.axis_size("ctx")
    capacity = 2 * token_rows
    per_peer = capacity // peer_count
    rounds = buckets.shape[0]
    routes = [
        route_round(buckets[round_index], peer_count, per_peer, token_rows)
        for round_index in range(rounds)
    ]
    padded_qk = with_zero_row(shared_qk)
    padded_values = with_zero_row(values)
    whole_weight = lax.all_gather(out_weight, "ctx", axis=0, tiled=True)
    groups = [[round_index] for round_index in range(rounds)]

    def outgoing(matrix, round_index):
        return matrix[routes[round_index][1]].reshape((peer_count, per_peer) + matrix.shape[1:])

    def homeward(received, round_index):
        flat_rows = received.reshape((peer_count * per_peer,) + received.shape[2:])
        return flat_rows[routes[round_index][0]]

    round_outputs = [None] * rounds
    round_logs = [None] * rounds
    owner_state = [None] * rounds
    for round_group in groups:
        send_qk = jnp.stack(
            [outgoing(padded_qk, round_index) for round_index in round_group], axis=1
        )
        send_values = jnp.stack(
            [outgoing(padded_values, round_index) for round_index in round_group], axis=1
        )
        slot_marks = jnp.stack(
            [
                (routes[round_index][1] < token_rows)
                .astype(jnp.int32)
                .reshape(peer_count, per_peer)
                for round_index in round_group
            ],
            axis=1,
        )
        got_qk, got_values, got_marks = (
            lax.all_to_all(send_qk, "ctx", split_axis=0, concat_axis=0, tiled=True),
            lax.all_to_all(send_values, "ctx", split_axis=0, concat_axis=0, tiled=True),
            lax.all_to_all(slot_marks, "ctx", split_axis=0, concat_axis=0, tiled=True),
        )
        returned_rows = []
        returned_logs = []
        for member_index, round_index in enumerate(round_group):
            source_slot, target = compact_slots(got_marks[:, member_index].reshape(-1), capacity)
            own_qk = with_zero_row(got_qk[:, member_index].reshape(capacity, row_width))[
                source_slot
            ]
            own_values = with_zero_row(got_values[:, member_index].reshape(capacity, row_width))[
                source_slot
            ]
            occupied = source_slot < capacity
            rows_out, logs_out = owner_forward(own_qk, own_values, occupied, local_heads)
            owner_state[round_index] = (own_qk, own_values, occupied, source_slot, target)
            returned_rows.append(
                with_zero_row(rows_out)[target].reshape(peer_count, per_peer, row_width)
            )
            returned_logs.append(
                with_zero_row(logs_out)[target].reshape(peer_count, per_peer, local_heads)
            )
        back_rows, back_logs = (
            lax.all_to_all(
                jnp.stack(returned_rows, axis=1).astype(jnp.float32),
                "ctx",
                split_axis=0,
                concat_axis=0,
                tiled=True,
            ).astype(jnp.bfloat16),
            lax.all_to_all(
                jnp.stack(returned_logs, axis=1), "ctx", split_axis=0, concat_axis=0, tiled=True
            ),
        )
        for member_index, round_index in enumerate(round_group):
            round_outputs[round_index] = homeward(back_rows[:, member_index], round_index)
            round_logs[round_index] = homeward(back_logs[:, member_index], round_index)
    log_stack = jnp.stack(round_logs)
    largest = jnp.max(log_stack, axis=0)
    lifted = jnp.exp(log_stack - largest)
    round_weight = lifted / jnp.sum(lifted, axis=0)
    row_stack = (
        jnp.stack(round_outputs)
        .astype(jnp.float32)
        .reshape(rounds, token_rows, local_heads, HEAD_DIM)
    )
    attended = (
        jnp.sum(round_weight[..., None] * row_stack, axis=0)
        .reshape(token_rows, row_width)
        .astype(jnp.bfloat16)
    )
    partial_value = lax.dot_general(
        attended, whole_weight, (((1,), (1,)), ((), ())), preferred_element_type=jnp.float32
    )
    mixed = lax.psum_scatter(partial_value, "head", scatter_dimension=1, tiled=True).astype(
        jnp.bfloat16
    )
    full_grad = lax.all_gather(out_grad, "head", axis=1, tiled=True)
    attended_grad = jnp.dot(full_grad, whole_weight, preferred_element_type=jnp.float32)
    token_total = token_rows * peer_count
    grad_weight = lax.psum_scatter(
        lax.dot_general(
            full_grad, attended, (((0,), (0,)), ((), ())), preferred_element_type=jnp.float32
        ),
        "ctx",
        scatter_dimension=0,
        tiled=True,
    ) * (1.0 / math.sqrt(token_total))
    grad_heads = attended_grad.reshape(token_rows, local_heads, HEAD_DIM)
    inner = jnp.sum(
        grad_heads * attended.astype(jnp.float32).reshape(token_rows, local_heads, HEAD_DIM),
        axis=-1,
    )
    qk_total = jnp.zeros((token_rows, row_width), jnp.float32)
    value_total = jnp.zeros((token_rows, row_width), jnp.float32)
    for round_group in groups:
        send_grad = jnp.stack(
            [
                outgoing(
                    with_zero_row(
                        (round_weight[round_index][..., None] * grad_heads)
                        .reshape(token_rows, row_width)
                        .astype(jnp.bfloat16)
                    ),
                    round_index,
                )
                for round_index in round_group
            ],
            axis=1,
        )
        send_shift = jnp.stack(
            [
                outgoing(with_zero_row(round_weight[round_index] * inner), round_index)
                for round_index in round_group
            ],
            axis=1,
        )
        got_grad, got_shift = (
            lax.all_to_all(
                send_grad.astype(jnp.float32), "ctx", split_axis=0, concat_axis=0, tiled=True
            ).astype(send_grad.dtype),
            lax.all_to_all(send_shift, "ctx", split_axis=0, concat_axis=0, tiled=True),
        )
        returned_qk = []
        returned_values = []
        for member_index, round_index in enumerate(round_group):
            own_qk, own_values, occupied, source_slot, target = owner_state[round_index]
            own_grad = with_zero_row(got_grad[:, member_index].reshape(capacity, row_width))[
                source_slot
            ]
            own_shift = with_zero_row(got_shift[:, member_index].reshape(capacity, local_heads))[
                source_slot
            ]
            qk_rows, value_rows = owner_backward(
                own_qk, own_values, occupied, own_grad, own_shift, local_heads
            )
            returned_qk.append(
                with_zero_row(qk_rows)[target].reshape(peer_count, per_peer, row_width)
            )
            returned_values.append(
                with_zero_row(value_rows)[target].reshape(peer_count, per_peer, row_width)
            )
        back_qk, back_values = (
            lax.all_to_all(
                jnp.stack(returned_qk, axis=1), "ctx", split_axis=0, concat_axis=0, tiled=True
            ),
            lax.all_to_all(
                jnp.stack(returned_values, axis=1), "ctx", split_axis=0, concat_axis=0, tiled=True
            ),
        )
        for member_index, round_index in enumerate(round_group):
            qk_total = qk_total + homeward(back_qk[:, member_index], round_index).astype(
                jnp.float32
            )
            value_total = value_total + homeward(back_values[:, member_index], round_index).astype(
                jnp.float32
            )
    return (mixed, qk_total.astype(jnp.bfloat16), value_total.astype(jnp.bfloat16), grad_weight)


def solution(mesh):
    in_specs = (
        P("ctx", "head"),
        P("ctx", "head"),
        P("ctx", "head"),
        P("ctx", "head"),
        P(None, "ctx"),
    )
    out_specs = (P("ctx", "head"), P("ctx", "head"), P("ctx", "head"), P("ctx", "head"))
    return jax.shard_map(
        per_device, mesh=mesh, in_specs=in_specs, out_specs=out_specs, check_vma=False
    )
```

profile of v0, /device:TPU:0, one launch (start us, length us, event | category | flops | bytes accessed | tf_op | source)
XLA Modules:
  0.0 1010.5 jit_solution(8157372763770059630)
XLA Ops:
  11.9 14.1 %all-to-all-start.5 = ((s32[128,1,2]{2,1,0:T(1,128)}), s32[128,1,2]{2,1,0:T(1,128)S(1)}, u32[]{:S(2)}, u32[]{:S(2)}) async-start(s32[128,1,2]{2,1,0:T(1,128)} %bitcast.60), calls=%async_computation.5 | async-start | bytes 131072 | tf_op jit(solution)/shard_map/all_to_all | solution.py:178
  27.7 9.9 all-to-all-done.5
  47.0 8.4 all-to-all-done.1
  80.2 7.8 all-to-all-start.6
  89.5 14.9 %all-to-all-done.6 = bf16[128,1,2,1024]{3,2,1,0:T(2,128)(2,1)S(1)} async-done(((bf16[128,1,2,1024]{3,2,1,0:T(2,128)(2,1)}), bf16[128,1,2,1024]{3,2,1,0:T(2,128)(2,1)S(1)}, u32[]{:S(2)}, u32[]{:S(2)}) %all-to-all-start.6) | async-done | bytes 524320 | tf_op jit(solution)/shard_map/all_to_all | solution.py:176
  104.4 7.0 all-to-all-start
  111.6 22.1 %all-to-all-done = bf16[128,1,2,1024]{3,2,1,0:T(2,128)(2,1)S(1)} async-done(((bf16[128,1,2,1024]{3,2,1,0:T(2,128)(2,1)}), bf16[128,1,2,1024]{3,2,1,0:T(2,128)(2,1)S(1)}, u32[]{:S(2)}, u32[]{:S(2)}) %all-to-all-start) | async-done | bytes 524320 | tf_op jit(solution)/shard_map/all_to_all | solution.py:177
  133.7 8.1 all-to-all-start.2
  150.5 7.0 all-to-all-done.2
  182.9 7.0 while.61
  191.4 13.8 %all-to-all-start.7 = ((f32[128,1,2,8]{3,2,1,0:T(2,128)}), f32[128,1,2,8]{3,2,1,0:T(2,128)S(1)}, u32[]{:S(2)}, u32[]{:S(2)}) async-start(f32[128,1,2,8]{3,2,1,0:T(2,128)} %bitcast.69), calls=%async_computation.7 | async-start | bytes 262144 | tf_op jit(solution)/shard_map/all_to_all | solution.py:207
  210.3 6.9 all-to-all-done.7
  217.3 7.4 all-to-all-start.9
  229.8 9.8 all-to-all-done.9
  239.6 7.3 all-to-all-start.8
  252.6 9.2 all-to-all-done.8
  277.8 9.3 copy.192
  301.5 10.9 %all-to-all-done.14 = f32[128,1,2,8]{3,2,1,0:T(2,128)S(1)} async-done(((f32[128,1,2,8]{3,2,1,0:T(2,128)}), f32[128,1,2,8]{3,2,1,0:T(2,128)S(1)}, u32[]{:S(2)}, u32[]{:S(2)}) %all-to-all-start.14) | async-done | bytes 8224 | tf_op jit(solution)/shard_map/all_to_all | solution.py:278
  312.4 7.2 all-to-all-start.11
  321.9 9.4 all-to-all-done.11
  331.3 7.3 all-to-all-start.13
  344.7 12.4 %all-to-all-done.13 = bf16[128,1,2,1024]{3,2,1,0:T(2,128)(2,1)} async-done(((bf16[128,1,2,1024]{3,2,1,0:T(2,128)(2,1)}), bf16[128,1,2,1024]{3,2,1,0:T(2,128)(2,1)}, u32[]{:S(2)}, u32[]{:S(2)}) %all-to-all-start.13) | async-done | bytes 524320 | tf_op jit(solution)/shard_map/all_to_all | solution.py:275
  357.2 7.8 all-to-all-start.10
  375.6 24.0 %while.63 = (s32[]{:T(128)}, f32[2,128,8,128]{1,3,2,0:T(8,128)}, f32[2,256,8,128]{1,3,2,0:T(8,128)}, f32[2,256,8,128]{1,3,2,0:T(8,128)}, bf16[2,256,8,128]{3,1,2...) while((s32[]{:T(128)}, f32[2,128,8,128]{1,3,2,0:T(8,128)}, ...), condition=%wide.region_31.32_spmd, body=%wide.region_28.31_spmd.sunk | while | flops 407537280 | bytes 35519732 | solution.py:99
  405.3 14.7 %all-to-all-start.15 = ((bf16[128,1,2,1024]{3,2,1,0:T(2,128)(2,1)}), bf16[128,1,2,1024]{3,2,1,0:T(2,128)(2,1)}, u32[]{:S(2)}, u32[]{:S(2)}) async-start(bf16[128,1,2,1024]{3,2,1,0:T(2,128)(2,1)} %bitcast.89), calls=%async_computation.16 | async-start | bytes 1048576 | tf_op jit(solution)/shard_map/all_to_all | solution.py:300
  426.0 17.8 %while.62 = (s32[]{:T(128)}, f32[2,128,8,128]{1,3,2,0:T(8,128)S(1)}, f32[2,256,8,128]{1,3,2,0:T(8,128)}, f32[2,256,8,128]{1,3,2,0:T(8,128)}, bf16[2,256,8,128]{3...) while((s32[]{:T(128)}, ...), condition=%wide.region_27.28_spmd, body=%wide.region_24.27_spmd.sunk | while | flops 407537280 | bytes 27131068 | solution.py:99
  449.1 13.9 %all-to-all-start.12 = ((bf16[128,1,2,1024]{3,2,1,0:T(2,128)(2,1)}), bf16[128,1,2,1024]{3,2,1,0:T(2,128)(2,1)S(1)}, u32[]{:S(2)}, u32[]{:S(2)}) async-start(bf16[128,1,2,1024]{3,2,1,0:T(2,128)(2,1)} %bitcast.432), calls=%async_computation.13 | async-start | bytes 1048576 | tf_op jit(solution)/shard_map/all_to_all | solution.py:300
  465.9 13.4 %all-to-all-done.12 = bf16[128,1,2,1024]{3,2,1,0:T(2,128)(2,1)S(1)} async-done(((bf16[128,1,2,1024]{3,2,1,0:T(2,128)(2,1)}), bf16[128,1,2,1024]{3,2,1,0:T(2,128)(2,1)S(1)}, u32[]{:S(2)}, u32[]{:S(2)}) %all-to-all-start.12) | async-done | bytes 524320 | tf_op jit(solution)/shard_map/all_to_all | solution.py:300
  479.3 8.2 all-to-all-start.17
  492.2 12.3 %all-to-all-done.17 = bf16[128,1,2,1024]{3,2,1,0:T(2,128)(2,1)S(1)} async-done(((bf16[128,1,2,1024]{3,2,1,0:T(2,128)(2,1)}), bf16[128,1,2,1024]{3,2,1,0:T(2,128)(2,1)S(1)}, u32[]{:S(2)}, u32[]{:S(2)}) %all-to-all-start.17) | async-done | bytes 524320 | tf_op jit(solution)/shard_map/all_to_all | solution.py:303
  515.5 11.6 %all-to-all-done.16 = bf16[128,1,2,1024]{3,2,1,0:T(2,128)(2,1)S(1)} async-done(((bf16[128,1,2,1024]{3,2,1,0:T(2,128)(2,1)}), bf16[128,1,2,1024]{3,2,1,0:T(2,128)(2,1)S(1)}, u32[]{:S(2)}, u32[]{:S(2)}) %all-to-all-start.16) | async-done | bytes 524320 | tf_op jit(solution)/shard_map/all_to_all | solution.py:303
  531.6 470.2 %reduce-scatter.7.cloned.1.call-done = f32[16,1024]{1,0:T(8,128)} async-done(((f32[2048,1024]{1,0:T(8,128)}), f32[16,1024]{1,0:T(8,128)}) %reduce-scatter.7.cloned.1.call-update) | async-done | bytes 65552
  (395 shorter events, 237.8 us)
Async XLA Ops:
  7.2 258.8 %all-gather.2.cloned.1.call-start = ((), (), s32[]{:S(2)}) async-start(), calls=%async_computation.20 | async-start | bytes 4227072 | tf_op jit(solution)/shard_map/all_gather | solution.py:146
  11.9 25.7 %all-to-all-start.5 = ((s32[128,1,2]{2,1,0:T(1,128)}), s32[128,1,2]{2,1,0:T(1,128)S(1)}, u32[]{:S(2)}, u32[]{:S(2)}) async-start(s32[128,1,2]{2,1,0:T(1,128)} %bitcast.60), calls=%async_computation.5 | async-start | bytes 131072 | tf_op jit(solution)/shard_map/all_to_all | solution.py:178
  37.6 17.8 %all-to-all-start.1 = ((s32[128,1,2]{2,1,0:T(1,128)}), s32[128,1,2]{2,1,0:T(1,128)S(1)}, u32[]{:S(2)}, u32[]{:S(2)}) async-start(s32[128,1,2]{2,1,0:T(1,128)} %bitcast.43), calls=%async_computation.1 | async-start | bytes 131072 | tf_op jit(solution)/shard_map/all_to_all | solution.py:178
  43.8 248.1 %copy-start.27 = (s32[1024]{0:T(1024)}, s32[1024]{0:T(1024)S(1)}, u32[]{:S(2)}) copy-start(s32[1024]{0:T(1024)S(1)} %pad_clamp_fusion.3) | copy-start | bytes 12292
  45.9 15.8 %copy-start.12 = (bf16[128,1024]{1,0:T(8,128)(2,1)S(1)}, bf16[128,1024]{1,0:T(8,128)(2,1)}, u32[]{:S(2)}) copy-start(bf16[128,1024]{1,0:T(8,128)(2,1)} %param.13) | copy-start | bytes 786436
  55.4 24.8 %all-to-all-start.4 = ((bf16[128,1,2,1024]{3,2,1,0:T(2,128)(2,1)}), bf16[128,1,2,1024]{3,2,1,0:T(2,128)(2,1)S(1)}, u32[]{:S(2)}, u32[]{:S(2)}) async-start(bf16[128,1,2,1024]{3,2,1,0:T(2,128)(2,1)} %bitcast.59), calls=%async_computation.4 | async-start | bytes 1048576 | tf_op jit(solution)/shard_map/all_to_all | solution.py:177
  80.2 24.2 %all-to-all-start.6 = ((bf16[128,1,2,1024]{3,2,1,0:T(2,128)(2,1)}), bf16[128,1,2,1024]{3,2,1,0:T(2,128)(2,1)S(1)}, u32[]{:S(2)}, u32[]{:S(2)}) async-start(bf16[128,1,2,1024]{3,2,1,0:T(2,128)(2,1)} %bitcast.65), calls=%async_computation.6 | async-start | bytes 1048576 | tf_op jit(solution)/shard_map/all_to_all | solution.py:176
  104.4 29.3 %all-to-all-start = ((bf16[128,1,2,1024]{3,2,1,0:T(2,128)(2,1)}), bf16[128,1,2,1024]{3,2,1,0:T(2,128)(2,1)S(1)}, u32[]{:S(2)}, u32[]{:S(2)}) async-start(bf16[128,1,2,1024]{3,2,1,0:T(2,128)(2,1)} %bitcast.42), calls=%async_computation | async-start | bytes 1048576 | tf_op jit(solution)/shard_map/all_to_all | solution.py:177
  111.5 33.2 %copy-start.29 = (s32[1024]{0:T(1024)}, s32[1024]{0:T(1024)S(1)}, u32[]{:S(2)}) copy-start(s32[1024]{0:T(1024)S(1)} %pad_clamp_fusion.2) | copy-start | bytes 12292
  111.6 94.7 %copy-start.24 = (s32[1024]{0:T(1024)}, s32[1024]{0:T(1024)S(1)}, u32[]{:S(2)}) copy-start(s32[1024]{0:T(1024)S(1)} %pad_clamp_fusion.1) | copy-start | bytes 12292
  133.7 23.8 %all-to-all-start.2 = ((bf16[128,1,2,1024]{3,2,1,0:T(2,128)(2,1)}), bf16[128,1,2,1024]{3,2,1,0:T(2,128)(2,1)}, u32[]{:S(2)}, u32[]{:S(2)}) async-start(bf16[128,1,2,1024]{3,2,1,0:T(2,128)(2,1)} %bitcast.48), calls=%async_computation.2 | async-start | bytes 1048576 | tf_op jit(solution)/shard_map/all_to_all | solution.py:176
  141.9 16.9 %copy-start.26 = (s32[1024]{0:T(1024)}, s32[1024]{0:T(1024)S(1)}, u32[]{:S(2)}) copy-start(s32[1024]{0:T(1024)S(1)} %pad_clamp_fusion.6) | copy-start | bytes 12292
  141.9 83.9 %copy-start.22 = (s32[1024]{0:T(1024)}, s32[1024]{0:T(1024)S(1)}, u32[]{:S(2)}) copy-start(s32[1024]{0:T(1024)S(1)} %pad_clamp_fusion.5) | copy-start | bytes 12292
  170.6 20.8 %all-to-all-start.3 = ((f32[128,1,2,8]{3,2,1,0:T(2,128)}), f32[128,1,2,8]{3,2,1,0:T(2,128)S(1)}, u32[]{:S(2)}, u32[]{:S(2)}) async-start(f32[128,1,2,8]{3,2,1,0:T(2,128)} %bitcast.52), calls=%async_computation.3 | async-start | bytes 262144 | tf_op jit(solution)/shard_map/all_to_all | solution.py:207
  189.9 15.3 %copy-start.20 = (pred[2,256]{1,0:T(4,128)(4,1)}, pred[2,256]{1,0:T(4,128)(4,1)S(1)}, u32[]{:S(2)}) copy-start(pred[2,256]{1,0:T(4,128)(4,1)S(1)} %get-tuple-element.1069) | copy-start | bytes 1540
  191.4 25.9 %all-to-all-start.7 = ((f32[128,1,2,8]{3,2,1,0:T(2,128)}), f32[128,1,2,8]{3,2,1,0:T(2,128)S(1)}, u32[]{:S(2)}, u32[]{:S(2)}) async-start(f32[128,1,2,8]{3,2,1,0:T(2,128)} %bitcast.69), calls=%async_computation.7 | async-start | bytes 262144 | tf_op jit(solution)/shard_map/all_to_all | solution.py:207
  217.3 22.3 %all-to-all-start.9 = ((bf16[128,1,2,1024]{3,2,1,0:T(2,128)(2,1)}), bf16[128,1,2,1024]{3,2,1,0:T(2,128)(2,1)}, u32[]{:S(2)}, u32[]{:S(2)}) async-start(bf16[128,1,2,1024]{3,2,1,0:T(2,128)(2,1)} %bitcast.75), calls=%async_computation.9 | async-start | bytes 1048576 | tf_op jit(solution)/shard_map/all_to_all | solution.py:200
  239.6 22.2 %all-to-all-start.8 = ((bf16[128,1,2,1024]{3,2,1,0:T(2,128)(2,1)}), bf16[128,1,2,1024]{3,2,1,0:T(2,128)(2,1)}, u32[]{:S(2)}, u32[]{:S(2)}) async-start(bf16[128,1,2,1024]{3,2,1,0:T(2,128)(2,1)} %bitcast.73), calls=%async_computation.8 | async-start | bytes 1048576 | tf_op jit(solution)/shard_map/all_to_all | solution.py:200
  246.9 283.0 %reduce-scatter.5.cloned.1.call-start = ((), (), s32[]{:S(2)}) async-start(), calls=%async_computation.21 | async-start | bytes 1572864 | tf_op jit(solution)/shard_map/reduce_scatter | solution.py:231
  247.0 16.0 %copy-start.30 = (s32[1024]{0:T(1024)}, s32[1024]{0:T(1024)S(1)}, u32[]{:S(2)}) copy-start(s32[1024]{0:T(1024)S(1)} %pad_clamp_fusion.4) | copy-start | bytes 12292
  270.7 731.2 %reduce-scatter.7.cloned.1.call-start = ((), (), s32[]{:S(2)}) async-start(), calls=%async_computation.22 | async-start | bytes 8454144
  291.8 27.8 %copy-start.11 = (bf16[128,1024]{1,0:T(8,128)(2,1)S(1)}, bf16[128,1024]{1,0:T(8,128)(2,1)}, u32[]{:S(2)}) copy-start(bf16[128,1024]{1,0:T(8,128)(2,1)} %get-tuple-element.679) | copy-start | bytes 786436
  293.2 19.2 %all-to-all-start.14 = ((f32[128,1,2,8]{3,2,1,0:T(2,128)}), f32[128,1,2,8]{3,2,1,0:T(2,128)S(1)}, u32[]{:S(2)}, u32[]{:S(2)}) async-start(f32[128,1,2,8]{3,2,1,0:T(2,128)} %bitcast.86), calls=%async_computation.15 | async-start | bytes 262144 | tf_op jit(solution)/shard_map/all_to_all | solution.py:278
  312.4 18.9 %all-to-all-start.11 = ((f32[128,1,2,8]{3,2,1,0:T(2,128)}), f32[128,1,2,8]{3,2,1,0:T(2,128)}, u32[]{:S(2)}, u32[]{:S(2)}) async-start(f32[128,1,2,8]{3,2,1,0:T(2,128)} %bitcast.79), calls=%async_computation.12 | async-start | bytes 262144 | tf_op jit(solution)/shard_map/all_to_all | solution.py:278
  331.3 25.9 %all-to-all-start.13 = ((bf16[128,1,2,1024]{3,2,1,0:T(2,128)(2,1)}), bf16[128,1,2,1024]{3,2,1,0:T(2,128)(2,1)}, u32[]{:S(2)}, u32[]{:S(2)}) async-start(bf16[128,1,2,1024]{3,2,1,0:T(2,128)(2,1)} %bitcast.430), calls=%async_computation.14 | async-start | bytes 1048576 | tf_op jit(solution)/shard_map/all_to_all | solution.py:275
  357.2 48.1 %all-to-all-start.10 = ((bf16[128,1,2,1024]{3,2,1,0:T(2,128)(2,1)}), bf16[128,1,2,1024]{3,2,1,0:T(2,128)(2,1)}, u32[]{:S(2)}, u32[]{:S(2)}) async-start(bf16[128,1,2,1024]{3,2,1,0:T(2,128)(2,1)} %bitcast.77), calls=%async_computation.11 | async-start | bytes 1048576 | tf_op jit(solution)/shard_map/all_to_all | solution.py:275
  405.3 43.9 %all-to-all-start.15 = ((bf16[128,1,2,1024]{3,2,1,0:T(2,128)(2,1)}), bf16[128,1,2,1024]{3,2,1,0:T(2,128)(2,1)}, u32[]{:S(2)}, u32[]{:S(2)}) async-start(bf16[128,1,2,1024]{3,2,1,0:T(2,128)(2,1)} %bitcast.89), calls=%async_computation.16 | async-start | bytes 1048576 | tf_op jit(solution)/shard_map/all_to_all | solution.py:300
  448.1 15.0 %copy-start.5 = (f32[2,256,8,128]{1,3,2,0:T(8,128)S(1)}, f32[2,256,8,128]{1,3,2,0:T(8,128)}, u32[]{:S(2)}) copy-start(f32[2,256,8,128]{1,3,2,0:T(8,128)} %get-tuple-element.447) | copy-start | bytes 6291460
  449.1 30.1 %all-to-all-start.12 = ((bf16[128,1,2,1024]{3,2,1,0:T(2,128)(2,1)}), bf16[128,1,2,1024]{3,2,1,0:T(2,128)(2,1)S(1)}, u32[]{:S(2)}, u32[]{:S(2)}) async-start(bf16[128,1,2,1024]{3,2,1,0:T(2,128)(2,1)} %bitcast.432), calls=%async_computation.13 | async-start | bytes 1048576 | tf_op jit(solution)/shard_map/all_to_all | solution.py:300
  464.9 22.6 %copy-start.4 = (f32[2,256,8,128]{1,3,2,0:T(8,128)S(1)}, f32[2,256,8,128]{1,3,2,0:T(8,128)}, u32[]{:S(2)}) copy-start(f32[2,256,8,128]{1,3,2,0:T(8,128)} %get-tuple-element.446) | copy-start | bytes 6291460
  479.3 25.3 %all-to-all-start.17 = ((bf16[128,1,2,1024]{3,2,1,0:T(2,128)(2,1)}), bf16[128,1,2,1024]{3,2,1,0:T(2,128)(2,1)S(1)}, u32[]{:S(2)}, u32[]{:S(2)}) async-start(bf16[128,1,2,1024]{3,2,1,0:T(2,128)(2,1)} %bitcast.431), calls=%async_computation.18 | async-start | bytes 1048576 | tf_op jit(solution)/shard_map/all_to_all | solution.py:303
  504.5 22.6 %all-to-all-start.16 = ((bf16[128,1,2,1024]{3,2,1,0:T(2,128)(2,1)}), bf16[128,1,2,1024]{3,2,1,0:T(2,128)(2,1)S(1)}, u32[]{:S(2)}, u32[]{:S(2)}) async-start(bf16[128,1,2,1024]{3,2,1,0:T(2,128)(2,1)} %bitcast.90), calls=%async_computation.17 | async-start | bytes 1048576 | tf_op jit(solution)/shard_map/all_to_all | solution.py:303
  (29 other events, 67.9 us)
Sparse Core Ops, SparseCore 0:
  11.6 123.7 all-gather.1
  270.8 7.6 reduce-scatter.4
  287.3 714.5 reduce-scatter.6
where the time goes:
time: 1020 us; the launch traced here: 1010 us
  waiting for transfers between devices  635 us (62%)
  starting transfers between devices  157 us (15%)
  local copies, waits for them, and re-layouts  130 us (13%)
  matrix products  54.6 us (5%)
  between operations  15.3 us (2%)
  other arithmetic  14.8 us (1%)
    unnamed x4, waiting for transfers between devices  471 us
    all_to_all x2, starting transfers between devices, per_device(): lax.all_to_all(jnp.stack(returned_qk, axis=1), 'ctx', split_axis=0, conca...  28.6 us
    all_to_all x2, waiting for transfers between devices, per_device(): lax.all_to_all(send_values, 'ctx', split_axis=0, concat_axis=0, tiled=True)  28.3 us
    unnamed x77, local copies, waits for them, and re-layouts  24 us
    all_to_all x2, waiting for transfers between devices, per_device(): lax.all_to_all(jnp.stack(returned_values, axis=1), 'ctx', split_axis=0, c...  23.9 us
    all_to_all x2, waiting for transfers between devices, per_device(): lax.all_to_all(send_qk, 'ctx', split_axis=0, concat_axis=0, tiled=True)  21.9 us
    all_to_all x2, starting transfers between devices, per_device(): lax.all_to_all(jnp.stack(returned_logs, axis=1), 'ctx', split_axis=0, con...  20.7 us
  transfers between devices with their start and end apart: 21, of which 16 were waited for; matrix products, arithmetic and copies ran while one was open for 18% of the time, Pallas kernels for 0%

commit v1 on v0

v1 whole, which is shorter than its diff:
```python
import math

import jax
import jax.numpy as jnp
from jax import lax
from jax.experimental import pallas as pl
from jax.experimental.pallas import tpu as pltpu
from jax.sharding import PartitionSpec as P

NX, NZ, NY = 4, 8, 4
NG = NX * NY
TOK = 128
DIM = 128
ROUNDS = 2
BUCKETS = 8
SLOTS = 256
SCALE = DIM ** (-0.5)
SELF_PENALTY = 10000.0
MASKED = -1e30
BF = jnp.bfloat16
F32 = jnp.float32


def ctx_of(x, z, y):
    return (x * NZ + z) * NY + y


RINGS = [[ctx_of(x, z, y) for z in range(NZ)] for x in range(NX) for y in range(NY)]
PLANES = [[ctx_of(x, z, y) for x in range(NX) for y in range(NY)] for z in range(NZ)]

ROW_W = 512
ROW_LIVE = 640
ROWS_B = 656
ROW_EXTRA = 256
ROWS_C = 272
ROW_GW = 512
ROWS_E = 640
ROWS_A = 288
ROWS_F = 416


def iota(shape, dim):
    return lax.broadcasted_iota(jnp.int32, shape, dim)


def fiota(shape, dim):
    return iota(shape, dim).astype(F32)


def dot(a, b):
    return jnp.dot(a, b, preferred_element_type=F32)


def dot_nt(a, b):
    return lax.dot_general(a, b, (((1,), (1,)), ((), ())), preferred_element_type=F32)


def dot_tn(a, b):
    return lax.dot_general(a, b, (((0,), (0,)), ((), ())), preferred_element_type=F32)


def ones_where(mask):
    return jnp.where(mask, 1.0, 0.0).astype(BF)


def swap_matrix():
    dest = iota((TOK, TOK), 0)
    source = ((dest >> 1) & 7) * 16 + (dest >> 4) * 2 + (dest & 1)
    return ones_where(iota((TOK, TOK), 1) == source)


def three_parts(spread, lane):
    high = spread.astype(BF).astype(F32)
    rest = spread - high
    middle = rest.astype(BF).astype(F32)
    low = rest - middle
    return jnp.where(lane < 16, high, jnp.where(lane < 32, middle, jnp.where(lane < 48, low, 0.0)))


def split_slot(slot):
    owner = jnp.floor(slot * (1.0 / 16.0))
    inside = slot - 16.0 * owner
    bucket = jnp.floor(inside * 0.5)
    return owner, bucket, inside - 2.0 * bucket


def pack_ring(qk_ref, v_ref, w_ref, b_ref, msg_ref):
    for z in range(NZ):
        cols = slice(z * DIM, (z + 1) * DIM)
        msg_ref[z, 0:128, :] = qk_ref[:, cols]
        msg_ref[z, 128:256, :] = v_ref[:, cols]
        msg_ref[z, 256:272, :] = w_ref[:, cols]
        msg_ref[z, 272:288, :] = b_ref[...]


def route(a_ref, msg_ref, srow_ref, scol_ref, y_ref):
    sub = iota((TOK, TOK), 0)
    lane = iota((TOK, TOK), 1)
    swap = swap_matrix()
    slot_sub = fiota((SLOTS, TOK), 0)
    live = jnp.zeros((SLOTS, TOK), F32)
    scols = jnp.zeros((TOK, TOK), F32)
    for r in range(ROUNDS):
        for z in range(NZ):
            brow = a_ref[z, 272:288, :].astype(F32)[r : r + 1, :]
            bcol = jnp.sum(jnp.where(sub == lane, brow, 0.0), axis=1, keepdims=True)
            same = jnp.where(bcol == brow, 1.0, 0.0)
            prow = jnp.sum(jnp.where(sub < lane, same, 0.0), axis=0, keepdims=True)
            pcol = jnp.sum(jnp.where(lane < sub, same, 0.0), axis=1, keepdims=True)
            srow = 2.0 * brow + prow
            scol = 2.0 * bcol + pcol
            srow_ref[r * NZ + z : r * NZ + z + 1, :] = srow
            scols = jnp.where(lane == r * NZ + z, scol, scols)
            rows = jnp.concatenate([a_ref[z, 0:128, :], a_ref[z, 128:256, :]], axis=1)
            y_ref[z, :, :] = dot(ones_where(slot_sub == srow), rows).astype(BF)
            owner, _, _ = split_slot(srow)
            place = owner * 16.0 + (2.0 * z) + prow
            _, bucket, _ = split_slot(scol)
            mark = ones_where(lane.astype(F32) == bucket + (1.0 * r * BUCKETS))
            live = live + dot(ones_where(slot_sub == place), mark)
        for o in range(NG):
            block = y_ref[:, o * 16 : (o + 1) * 16, :].reshape(TOK, 2 * DIM)
            moved = dot(swap, block).astype(BF)
            msg_ref[o, r * 128 : (r + 1) * 128, :] = moved[:, :DIM]
            msg_ref[o, 256 + r * 128 : 256 + (r + 1) * 128, :] = moved[:, DIM:]
    scol_ref[...] = scols
    live = live.astype(BF)
    for o in range(NG):
        msg_ref[o, ROW_LIVE:ROWS_B, :] = live[o * 16 : (o + 1) * 16, :]
        for z in range(NZ):
            msg_ref[o, ROW_W + z * 16 : ROW_W + (z + 1) * 16, :] = a_ref[z, 256:272, :]


def raw_scores(q):
    scores = dot_nt(q, q) * SCALE
    itself = iota((SLOTS, SLOTS), 0) == iota((SLOTS, SLOTS), 1)
    return jnp.where(itself, scores - SELF_PENALTY, scores)


def bucket_rows(ref, start):
    return ref[:, start : start + 16, :].reshape(SLOTS, DIM)


def attend(b_ref, msg_ref, logs_ref, qcode_ref, kcode_ref, w_ref):
    lane = iota((SLOTS, TOK), 1)
    live = bucket_rows(b_ref, ROW_LIVE)

    def order(j):
        return (j >> 6) * 64 + ((j >> 1) & 7) * 8 + ((j >> 4) & 3) * 2 + (j & 1)

    earlier = ones_where(order(iota((SLOTS, SLOTS), 1)) < order(iota((SLOTS, SLOTS), 0)))
    rank = dot(earlier, live)
    span = jnp.where(rank >= 128.0, 1.0, 0.0)
    kcol = jnp.where(live.astype(F32) > 0.5, span, 2.0).astype(BF)
    pick = ones_where(iota((16, TOK), 0) == iota((16, TOK), 1))
    krows = dot_nt(pick, kcol)
    qcode_ref[...] = span
    kcode_ref[...] = krows
    logs = jnp.zeros((SLOTS, TOK), F32)
    for r in range(ROUNDS):
        for k in range(BUCKETS):
            n = r * BUCKETS + k
            q = bucket_rows(b_ref, r * 128 + k * 16)
            v = bucket_rows(b_ref, 256 + r * 128 + k * 16)
            scores = jnp.where(krows[n : n + 1, :] <= span[:, n : n + 1], raw_scores(q), MASKED)
            largest = jnp.max(scores, axis=1, keepdims=True)
            lifted = jnp.exp(scores - largest)
            summed = jnp.sum(lifted, axis=1, keepdims=True)
            probability = (lifted * (1.0 / summed)).astype(BF)
            out = dot(probability, v).astype(BF)
            msg_ref[:, r * 128 + k * 16 : r * 128 + (k + 1) * 16, :] = out.reshape(NG, 16, DIM)
            logs = jnp.where((lane & 15) == n, largest + jnp.log(summed), logs)
    logs_ref[...] = logs
    msg_ref[:, ROW_EXTRA:ROWS_C, :] = three_parts(logs, lane).astype(BF).reshape(NG, 16, DIM)
    for x in range(NX):
        for y in range(NY):
            for z in range(NZ):
                at = ctx_of(x, z, y) * 16
                w_ref[at : at + 16, :] = b_ref[x * NY + y, ROW_W + z * 16 : ROW_W + (z + 1) * 16, :]


def combine(c_ref, srow_ref, scol_ref, grad_ref, msg_ref, att_ref, y_ref, s_ref):
    lane = iota((TOK, TOK), 1)
    swap = swap_matrix()
    slot_sub = fiota((SLOTS, TOK), 0)
    slot_lane = fiota((TOK, SLOTS), 1)
    for r in range(ROUNDS):
        for o in range(NG):
            moved = dot(swap, c_ref[o, r * 128 : (r + 1) * 128, :]).astype(BF)
            y_ref[r, :, o * 16 : (o + 1) * 16, :] = moved.reshape(NZ, 16, DIM)
    log_rows = bucket_rows(c_ref, ROW_EXTRA)
    extra = jnp.zeros((SLOTS, TOK), F32)
    folded = lane & 15
    for z in range(NZ):
        outs, logs, marks = [], [], []
        for r in range(ROUNDS):
            n = r * NZ + z
            scol = scol_ref[:, n : n + 1]
            outs.append(dot(ones_where(slot_lane == scol), y_ref[r, z]))
            owner, bucket, place = split_slot(scol)
            parts = dot(ones_where(slot_lane == owner * 16.0 + (2.0 * z) + place), log_rows)
            mark = folded.astype(F32) == bucket + (1.0 * r * BUCKETS)
            marks.append(mark)
            logs.append(jnp.sum(jnp.where(mark, parts, 0.0), axis=1, keepdims=True))
        largest = jnp.maximum(logs[0], logs[1])
        lifted = [jnp.exp(log - largest) for log in logs]
        total = lifted[0] + lifted[1]
        weights = [one / total for one in lifted]
        att = (weights[0] * outs[0] + weights[1] * outs[1]).astype(BF)
        att_ref[z * TOK : (z + 1) * TOK, :] = att
        grad = grad_ref[z * TOK : (z + 1) * TOK, :]
        inner = jnp.sum(grad * att.astype(F32), axis=1, keepdims=True)
        for r in range(ROUNDS):
            n = r * NZ + z
            srow = srow_ref[n : n + 1, :]
            query_grad = (weights[r] * grad).astype(BF)
            s_ref[r, z] = dot(ones_where(slot_sub == srow), query_grad).astype(BF)
            owner, _, place = split_slot(srow)
            spread = jnp.where(marks[r], weights[r] * inner, 0.0)
            extra = extra + dot(
                ones_where(slot_sub == owner * 16.0 + (2.0 * z) + place),
                three_parts(spread, lane).astype(BF),
            )
    for r in range(ROUNDS):
        for o in range(NG):
            block = s_ref[r, :, o * 16 : (o + 1) * 16, :].reshape(TOK, DIM)
            msg_ref[o, r * 128 : (r + 1) * 128, :] = dot(swap, block).astype(BF)
    msg_ref[:, ROW_EXTRA:ROWS_C, :] = extra.astype(BF).reshape(NG, 16, DIM)


def attend_back(b_ref, d_ref, logs_ref, qcode_ref, kcode_ref, gw_ref, msg_ref):
    lane = iota((SLOTS, TOK), 1)
    shifts = bucket_rows(d_ref, ROW_EXTRA).astype(F32)
    for r in range(ROUNDS):
        for k in range(BUCKETS):
            n = r * BUCKETS + k
            q = bucket_rows(b_ref, r * 128 + k * 16)
            v = bucket_rows(b_ref, 256 + r * 128 + k * 16)
            g = bucket_rows(d_ref, r * 128 + k * 16)
            shift = jnp.sum(jnp.where((lane & 15) == n, shifts, 0.0), axis=1, keepdims=True)
            seen = kcode_ref[n : n + 1, :] <= qcode_ref[:, n : n + 1]
            scores = jnp.where(seen, raw_scores(q), MASKED)
            probability = jnp.exp(scores - logs_ref[:, n : n + 1])
            score_grad = (probability * (dot_nt(g, v) - shift)).astype(BF)
            qk_grad = (dot(score_grad, q) + dot_tn(score_grad, q)) * SCALE
            value_grad = dot_tn(probability.astype(BF), g)
            rows = slice(r * 128 + k * 16, r * 128 + (k + 1) * 16)
            msg_ref[:, rows, :] = qk_grad.astype(BF).reshape(NG, 16, DIM)
            rows = slice(256 + r * 128 + k * 16, 256 + r * 128 + (k + 1) * 16)
            msg_ref[:, rows, :] = value_grad.astype(BF).reshape(NG, 16, DIM)
    for x in range(NX):
        for y in range(NY):
            for z in range(NZ):
                at = ctx_of(x, z, y) * 16
                msg_ref[x * NY + y, ROW_GW + z * 16 : ROW_GW + (z + 1) * 16, :] = gw_ref[at : at + 16, :]


def gather_home(e_ref, scol_ref, att_ref, msg_ref, y_ref):
    swap = swap_matrix()
    slot_lane = fiota((TOK, SLOTS), 1)
    for r in range(ROUNDS):
        for o in range(NG):
            rows = jnp.concatenate(
                [
                    e_ref[o, r * 128 : (r + 1) * 128, :],
                    e_ref[o, 256 + r * 128 : 256 + (r + 1) * 128, :],
                ],
                axis=1,
            )
            y_ref[r, :, o * 16 : (o + 1) * 16, :] = dot(swap, rows).astype(BF).reshape(NZ, 16, 2 * DIM)
    total = jnp.zeros((TOK, DIM), F32)
    for o in range(NG):
        total = total + e_ref[o, ROW_GW:ROWS_E, :].astype(F32)
    total = total * (1.0 / math.sqrt(NX * NY * NZ * TOK))
    high = total.astype(BF)
    low = (total - high.astype(F32)).astype(BF)
    for z in range(NZ):
        rows = jnp.zeros((TOK, 2 * DIM), F32)
        for r in range(ROUNDS):
            n = r * NZ + z
            rows = rows + dot(ones_where(slot_lane == scol_ref[:, n : n + 1]), y_ref[r, z])
        rows = rows.astype(BF)
        msg_ref[z, 0:128, :] = rows[:, :DIM]
        msg_ref[z, 128:256, :] = rows[:, DIM:]
        msg_ref[z, 256:384, :] = att_ref[z * TOK : (z + 1) * TOK, :]
        msg_ref[z, 384:400, :] = high[z * 16 : (z + 1) * 16, :]
        msg_ref[z, 400:416, :] = low[z * 16 : (z + 1) * 16, :]


def unpack_ring(f_ref, qk_ref, v_ref, att_ref, gw_ref):
    for z in range(NZ):
        cols = slice(z * DIM, (z + 1) * DIM)
        qk_ref[:, cols] = f_ref[z, 0:128, :]
        v_ref[:, cols] = f_ref[z, 128:256, :]
        att_ref[:, cols] = f_ref[z, 256:384, :]
        gw_ref[:, cols] = f_ref[z, 384:400, :].astype(F32) + f_ref[z, 400:416, :].astype(F32)


def on_device(body, outs, scratch=()):
    shapes = [jax.ShapeDtypeStruct(shape, kind) for shape, kind in outs]

    def call(*operands):
        return pl.pallas_call(
            body,
            out_shape=shapes,
            in_specs=[pl.BlockSpec(memory_space=pltpu.VMEM)] * len(operands),
            out_specs=[pl.BlockSpec(memory_space=pltpu.VMEM)] * len(shapes),
            scratch_shapes=[pltpu.VMEM(shape, kind) for shape, kind in scratch],
            compiler_params=pltpu.CompilerParams(vmem_limit_bytes=40 * 1024 * 1024),
        )(*operands)

    return call


def exchange(message, groups):
    return lax.all_to_all(
        message, "ctx", split_axis=0, concat_axis=0, tiled=True, axis_index_groups=groups
    )


def per_device(shared_qk, values, out_grad, out_weight, buckets):
    core = lax.axis_index("head")
    width = shared_qk.shape[1]
    ring_grad = lax.all_gather(out_grad, "ctx", axis=0, tiled=True, axis_index_groups=RINGS)
    whole_weight = lax.all_gather(out_weight, "ctx", axis=0, tiled=True)
    other_grad = lax.ppermute(ring_grad, "head", [(0, 1), (1, 0)])

    bucket_tile = jnp.pad(buckets.astype(BF), ((0, 14), (0, 0)))
    (msg,) = on_device(pack_ring, [((NZ, ROWS_A, DIM), BF)])(
        shared_qk, values, out_weight, bucket_tile
    )
    got_a = exchange(msg, RINGS)
    msg, slot_rows, slot_cols = on_device(
        route,
        [((NG, ROWS_B, DIM), BF), ((16, TOK), F32), ((TOK, TOK), F32)],
        [((NZ, SLOTS, 2 * DIM), BF)],
    )(got_a)
    got_b = exchange(msg, PLANES)
    msg, logs, query_code, key_code, head_weight = on_device(
        attend,
        [
            ((NG, ROWS_C, DIM), BF),
            ((SLOTS, TOK), F32),
            ((SLOTS, TOK), F32),
            ((16, SLOTS), F32),
            ((2 * width, DIM), BF),
        ],
    )(got_b)
    got_c = exchange(msg, PLANES)
    own_part = lax.dynamic_slice_in_dim(head_weight, core * width, width, 0)
    other_part = lax.dynamic_slice_in_dim(head_weight, (1 - core) * width, width, 0)
    attended_grad = dot(ring_grad, own_part) + dot(other_grad, other_part)
    msg, attended = on_device(
        combine,
        [((NG, ROWS_C, DIM), BF), ((NZ * TOK, DIM), BF)],
        [((ROUNDS, NZ, SLOTS, DIM), BF), ((ROUNDS, NZ, SLOTS, DIM), BF)],
    )(got_c, slot_rows, slot_cols, attended_grad)
    got_d = exchange(msg, PLANES)
    own_gw = dot_tn(ring_grad, attended).astype(BF)
    other_gw = dot_tn(other_grad, attended).astype(BF)
    both_gw = jnp.concatenate(
        [jnp.where(core == 0, own_gw, other_gw), jnp.where(core == 0, other_gw, own_gw)], axis=0
    )
    (msg,) = on_device(attend_back, [((NG, ROWS_E, DIM), BF)])(
        got_b, got_d, logs, query_code, key_code, both_gw
    )
    got_e = exchange(msg, PLANES)
    (msg,) = on_device(
        gather_home, [((NZ, ROWS_F, DIM), BF)], [((ROUNDS, NZ, SLOTS, 2 * DIM), BF)]
    )(got_e, slot_cols, attended)
    got_f = exchange(msg, RINGS)
    grad_qk, grad_values, attended_rows, grad_weight = on_device(
        unpack_ring,
        [((TOK, width), BF), ((TOK, width), BF), ((TOK, width), BF), ((16, width), F32)],
    )(got_f)
    partial_rows = dot_nt(attended_rows, whole_weight)
    mine = lax.dynamic_slice_in_dim(partial_rows, core * width, width, 1)
    theirs = lax.dynamic_slice_in_dim(partial_rows, (1 - core) * width, width, 1)
    mixed = (mine + lax.ppermute(theirs, "head", [(0, 1), (1, 0)])).astype(BF)
    return (mixed, grad_qk, grad_values, grad_weight)


def solution(mesh):
    assert mesh.shape["ctx"] == NX * NY * NZ and mesh.shape["head"] == 2
    in_specs = (
        P("ctx", "head"),
        P("ctx", "head"),
        P("ctx", "head"),
        P("ctx", "head"),
        P(None, "ctx"),
    )
    out_specs = (P("ctx", "head"), P("ctx", "head"), P("ctx", "head"), P("ctx", "head"))
    return jax.shard_map(
        per_device, mesh=mesh, in_specs=in_specs, out_specs=out_specs, check_vma=False
    )
```

time: 1020 us -> 240 us (0.24)
  the two profiles are of different devices: /device:TPU:0 before, /device:TPU:18 now
where the time goes in v1:
time: 240 us; the launch traced here: 236 us
  blocking collectives  104 us (43%)
  waiting for transfers between devices  49.8 us (21%)
  starting transfers between devices  22.8 us (10%)
  Pallas kernels  21.1 us (9%)
  between operations  14.2 us (6%)
  matrix products  13.3 us (6%)
  local copies, waits for them, and re-layouts  9.46 us (4%)
    all_to_all x3, blocking collectives, exchange(): lax.all_to_all(message, 'ctx', split_axis=0, concat_axis=0, tiled=True, a...  104 us
    all_to_all x3, waiting for transfers between devices, exchange(): lax.all_to_all(message, 'ctx', split_axis=0, concat_axis=0, tiled=True, a...  40.5 us
    all_to_all x3, starting transfers between devices, exchange(): lax.all_to_all(message, 'ctx', split_axis=0, concat_axis=0, tiled=True, a...  22.6 us
    pallas_call x7, Pallas kernels, call(): pl.pallas_call(body, out_shape=shapes, in_specs=[pl.BlockSpec(memory_spac...  21.1 us
    unnamed x26, local copies, waits for them, and re-layouts  9.41 us
    all_gather x1, waiting for transfers between devices, per_device(): lax.all_gather(out_grad, 'ctx', axis=0, tiled=True, axis_index_groups=RINGS)  6.04 us
    dot_general x2, matrix products, dot_tn(): lax.dot_general(a, b, (((0,), (0,)), ((), ())), preferred_element_type=F32)  5.05 us
  transfers between devices with their start and end apart: 7, of which 5 were waited for; matrix products, arithmetic and copies ran while one was open for 4% of the time, Pallas kernels for 9%

profile of v1, /device:TPU:18, one launch (start us, length us, event | category | flops | bytes accessed | tf_op | source)
XLA Modules:
  0.0 236.0 jit_solution(13562760255484775974)
XLA Ops:
  8.6 0.9 copy-done.4
  9.5 0.9 copy-done.5
  10.5 0.8 copy-done.10
  11.4 32.1 %all_to_all.30.a_ref = bf16[8,288,128]{2,1,0:T(8,128)(2,1)S(1)} all-to-all(bf16[8,288,128]{2,1,0:T(8,128)(2,1)S(1)} %shard_map.84), channel_id=1, replica_groups={{0,8,16,24,32,40,48,56},{2,10,18,26,34,42,50,58},{4,12,20,28,36,44,52,6..., dimensions={0} | all-to-all | bytes 1179648 | tf_op jit(solution)/shard_map/all_to_all | solution.py:316
  43.5 1.9 shard_map.85
  45.4 1.6 copy-done
  47.6 7.3 %all-to-all-start.1 = ((bf16[16,656,128]{2,1,0:T(8,128)(2,1)}), bf16[16,656,128]{2,1,0:T(8,128)(2,1)S(1)}, u32[]{:S(2)}, u32[]{:S(2)}) async-start(bf16[16,656,128]{2,1,0:T(8,128)(2,1)} %copy-done), calls=%async_computation.1 | async-start | bytes 5373952 | tf_op jit(solution)/shard_map/all_to_all | solution.py:316
  54.9 0.7 all-gather.5.cloned.1.call-update
  55.6 6.0 %all-gather.3.cloned.1.call-done = bf16[1024,1024]{1,0:T(8,128)(2,1)} async-done(((bf16[128,1024]{1,0:T(8,128)(2,1)}), bf16[1024,1024]{1,0:T(8,128)(2,1)}) %all-gather.3.cloned.1.call-update) | async-done | bytes 2097168 | tf_op jit(solution)/shard_map/all_gather | solution.py:324
  61.6 24.1 %all-to-all-done.1.b_ref = bf16[16,656,128]{2,1,0:T(8,128)(2,1)S(1)} async-done(((bf16[16,656,128]{2,1,0:T(8,128)(2,1)}), bf16[16,656,128]{2,1,0:T(8,128)(2,1)S(1)}, u32[]{:S(2)}, u32[]{:S(2)}) %all-to-all-start.1) | async-done | bytes 2687008 | tf_op jit(solution)/shard_map/all_to_all | solution.py:316
  85.7 3.7 %shard_map.86 = (bf16[16,272,128]{2,1,0:T(8,128)(2,1)S(1)}, f32[256,128]{1,0:T(8,128)S(1)}, f32[256,128]{1,0:T(8,128)S(1)}, f32[16,256]{1,0:T(8,128)S(1)}, bf16[2048,128]{1,0:T(8,128)(2,1)S(1)}) custom-call(bf16[16,656,128]{2,1,0:T(8,128)(2,1)S(1)} %all-to-all-done.1.b_ref), custom_call_target="tpu_custom_call" | custom-call | tf_op jit(solution)/shard_map/pallas_call | solution.py:303
  89.4 1.1 copy-done.1
  90.5 7.9 %all-to-all-start.2 = ((bf16[16,272,128]{2,1,0:T(8,128)(2,1)}), bf16[16,272,128]{2,1,0:T(8,128)(2,1)}, u32[]{:S(2)}, u32[]{:S(2)}) async-start(bf16[16,272,128]{2,1,0:T(8,128)(2,1)} %copy-done.1), calls=%async_computation.2 | async-start | bytes 2228224 | tf_op jit(solution)/shard_map/all_to_all | solution.py:316
  98.3 2.3 fusion.2
  100.7 2.3 fusion.grad_ref
  103.0 8.0 %all-to-all-done.2.c_ref = bf16[16,272,128]{2,1,0:T(8,128)(2,1)} async-done(((bf16[16,272,128]{2,1,0:T(8,128)(2,1)}), bf16[16,272,128]{2,1,0:T(8,128)(2,1)}, u32[]{:S(2)}, u32[]{:S(2)}) %all-to-all-start.2) | async-done | bytes 1114144 | tf_op jit(solution)/shard_map/all_to_all | solution.py:316
  111.7 5.3 %shard_map.87 = (bf16[16,272,128]{2,1,0:T(8,128)(2,1)S(1)}, bf16[1024,128]{1,0:T(8,128)(2,1)S(1)}) custom-call(bf16[16,272,128]{2,1,0:T(8,128)(2,1)} %all-to-all-done.2.c_ref, f32[16,128]{1,0:T(8,128)S(1)} %copy-done.12, f32[128,128]{1,0:T(8,128)S(1)} %get-tuple-element.21.scol_ref, f32[1024,128]{1,0:T(8,128)S(1)} %fusion.grad_ref), custom_call_target="tpu_custom_call" | custom-call | tf_op jit(solution)/shard_map/pallas_call | solution.py:303
  117.0 1.0 copy-done.2
  118.0 7.5 %all-to-all-start.3 = ((bf16[16,272,128]{2,1,0:T(8,128)(2,1)}), bf16[16,272,128]{2,1,0:T(8,128)(2,1)}, u32[]{:S(2)}, u32[]{:S(2)}) async-start(bf16[16,272,128]{2,1,0:T(8,128)(2,1)} %copy-done.2), calls=%async_computation.3 | async-start | bytes 2228224 | tf_op jit(solution)/shard_map/all_to_all | solution.py:316
  125.5 2.5 %convolution_convert_fusion.1 = bf16[128,1024]{0,1:T(8,128)(2,1)S(1)} fusion(bf16[1024,128]{1,0:T(8,128)(2,1)S(1)} %get-tuple-element.27.att_ref, bf16[1024,1024]{1,0:T(8,128)(2,1)} %all-gather.3.cloned.1.call-done), kind=kOutput, calls=%fused_computation.3 | convolution fusion | flops 268566528 | bytes 2621440 | tf_op jit(solution)/shard_map/dot_general | solution.py:59
  128.0 2.5 %select_bitcast_fusion.1 = (bf16[1024,128]{1,0:T(8,128)(2,1)S(1)}, bf16[1024,128]{1,0:T(8,128)(2,1)S(1)}) fusion(bf16[128,1024]{0,1:T(8,128)(2,1)S(1)} %convolution_convert_fusion.1, pred[]{:T(512)S(6)} %eq.4, bf16[1024,128]{1,0:T(8,128)(2,1)S(1)} %get-tuple-element.27.att_ref, bf16[1024,1024]{1,0:T(8,128)(2,1)} %collective-permute-done), kind=kOutput, calls=%fused_computation.7 | convolution fusion | flops 268828672 | bytes 3145729 | tf_op jit(solution)/shard_map/dot_general | solution.py:59
  130.6 8.4 %all-to-all-done.3.d_ref = bf16[16,272,128]{2,1,0:T(8,128)(2,1)} async-done(((bf16[16,272,128]{2,1,0:T(8,128)(2,1)}), bf16[16,272,128]{2,1,0:T(8,128)(2,1)}, u32[]{:S(2)}, u32[]{:S(2)}) %all-to-all-start.3) | async-done | bytes 1114144 | tf_op jit(solution)/shard_map/all_to_all | solution.py:316
  139.0 0.9 copy-done.7
  139.9 0.9 copy-done.9
  140.8 8.1 %shard_map.88 = bf16[16,640,128]{2,1,0:T(8,128)(2,1)S(1)} custom-call(bf16[16,656,128]{2,1,0:T(8,128)(2,1)S(1)} %all-to-all-done.1.b_ref, bf16[16,272,128]{2,1,0:T(8,128)(2,1)} %all-to-all-done.3.d_ref, f32[256,128]{1,0:T(8,128)S(1)} %copy-done.7, f32[256,128]{1,0:T(8,128)S(1)} %copy-done.9, f32[16,256]{1,0:T(8,128)S(1)} %get-tuple-element.26.kcode_ref, ...), custom_call_target="tpu_custom_call" | custom-call | tf_op jit(solution)/shard_map/pallas_call | solution.py:303
  148.9 45.9 %all_to_all.31.e_ref = bf16[16,640,128]{2,1,0:T(8,128)(2,1)S(1)} all-to-all(bf16[16,640,128]{2,1,0:T(8,128)(2,1)S(1)} %shard_map.88), channel_id=1, replica_groups={{0,2,4,6,64,66,68,70,128,130,132,134,192,194,196,198},{8,10,12,14,72,74..., dimensions={0} | all-to-all | bytes 5242880 | tf_op jit(solution)/shard_map/all_to_all | solution.py:316
  194.8 1.2 shard_map.89
  195.9 25.7 %all_to_all.32.f_ref = bf16[8,416,128]{2,1,0:T(8,128)(2,1)S(1)} all-to-all(bf16[8,416,128]{2,1,0:T(8,128)(2,1)S(1)} %shard_map.89), channel_id=1, replica_groups={{0,8,16,24,32,40,48,56},{2,10,18,26,34,42,50,58},{4,12,20,28,36,44,52,6..., dimensions={0} | all-to-all | bytes 1703936 | tf_op jit(solution)/shard_map/all_to_all | solution.py:316
  221.7 0.9 shard_map.90
  222.6 3.7 %fusion.6 = f32[128,2048]{1,0:T(8,128)S(1)} fusion(bf16[128,1024]{1,0:T(8,128)(2,1)S(1)} %get-tuple-element.28, bf16[2048,1024]{1,0:T(8,128)(2,1)} %all-gather.5.cloned.1.call-done), kind=kOutput, calls=%fused_computation.14 | convolution fusion | flops 536870912 | bytes 5505024 | tf_op jit(solution)/shard_map/dot_general | solution.py:55
  226.5 1.9 collective-permute-done.1
  228.4 0.8 add_convert_fusion
  (30 shorter events, 3.1 us)
Async XLA Ops:
  7.2 54.4 %all-gather.3.cloned.1.call-start = ((), (), s32[]{:S(2)}) async-start(), calls=%async_computation.6 | async-start | bytes 2359296 | tf_op jit(solution)/shard_map/all_gather | solution.py:324
  8.6 0.9 copy-start.4
  9.5 0.9 copy-start.5
  10.5 0.8 copy-start.10
  45.4 1.6 copy-start
  47.0 0.6 copy-start.11
  47.6 38.2 %all-to-all-start.1 = ((bf16[16,656,128]{2,1,0:T(8,128)(2,1)}), bf16[16,656,128]{2,1,0:T(8,128)(2,1)S(1)}, u32[]{:S(2)}, u32[]{:S(2)}) async-start(bf16[16,656,128]{2,1,0:T(8,128)(2,1)} %copy-done), calls=%async_computation.1 | async-start | bytes 5373952 | tf_op jit(solution)/shard_map/all_to_all | solution.py:316
  54.8 167.8 %all-gather.5.cloned.1.call-start = ((), (), s32[]{:S(2)}) async-start(), calls=%async_computation.7 | async-start | bytes 4227072 | tf_op jit(solution)/shard_map/all_gather | solution.py:325
  61.6 39.1 %collective-permute-start = (bf16[1024,1024]{1,0:T(8,128)(2,1)}, bf16[1024,1024]{1,0:T(8,128)(2,1)}, u32[]{:S(2)}, u32[]{:S(2)}) collective-permute-start(bf16[1024,1024]{1,0:T(8,128)(2,1)} %all-gather.3.cloned.1.call-done), channel_id=1, source_target_pairs={{0,1},{1,0},{2,3},{3,2},{4,5},{5,4},{6,7},{7,6},{8,9},{9,8},{10,11... | collective-permute-start | bytes 6291464 | tf_op jit(solution)/shard_map/ppermute | solution.py:326
  89.4 1.1 copy-start.1
  90.5 10.2 %copy-start.3 = (bf16[2048,128]{1,0:T(8,128)(2,1)}, bf16[2048,128]{1,0:T(8,128)(2,1)S(1)}, u32[]{:S(2)}) copy-start(bf16[2048,128]{1,0:T(8,128)(2,1)S(1)} %get-tuple-element.22) | copy-start | bytes 1572868
  90.5 10.2 %copy-start.6 = (f32[256,128]{1,0:T(8,128)}, f32[256,128]{1,0:T(8,128)S(1)}, u32[]{:S(2)}) copy-start(f32[256,128]{1,0:T(8,128)S(1)} %get-tuple-element.24.logs_ref) | copy-start | bytes 393220
  90.5 10.2 %copy-start.8 = (f32[256,128]{1,0:T(8,128)}, f32[256,128]{1,0:T(8,128)S(1)}, u32[]{:S(2)}) copy-start(f32[256,128]{1,0:T(8,128)S(1)} %get-tuple-element.25.qcode_ref) | copy-start | bytes 393220
  90.5 20.5 %all-to-all-start.2 = ((bf16[16,272,128]{2,1,0:T(8,128)(2,1)}), bf16[16,272,128]{2,1,0:T(8,128)(2,1)}, u32[]{:S(2)}, u32[]{:S(2)}) async-start(bf16[16,272,128]{2,1,0:T(8,128)(2,1)} %copy-done.1), calls=%async_computation.2 | async-start | bytes 2228224 | tf_op jit(solution)/shard_map/all_to_all | solution.py:316
  111.0 0.7 copy-start.12
  117.0 1.0 copy-start.2
  118.0 21.0 %all-to-all-start.3 = ((bf16[16,272,128]{2,1,0:T(8,128)(2,1)}), bf16[16,272,128]{2,1,0:T(8,128)(2,1)}, u32[]{:S(2)}, u32[]{:S(2)}) async-start(bf16[16,272,128]{2,1,0:T(8,128)(2,1)} %copy-done.2), calls=%async_computation.3 | async-start | bytes 2228224 | tf_op jit(solution)/shard_map/all_to_all | solution.py:316
  139.0 0.9 copy-start.7
  139.9 0.9 copy-start.9
  226.4 2.0 collective-permute-start.1
Sparse Core Ops, SparseCore 0:
  9.8 51.7 all-gather.2
  65.2 127.5 all-gather.4

commit v2 on v1

--- a/solution.py
+++ b/solution.py
@@ -33,6 +33,8 @@
 ROWS_B = 656
 ROW_EXTRA = 256
 ROWS_C = 272
+ROW_PLANE = 272
+ROWS_D = 400
 ROW_GW = 512
 ROWS_E = 640
 ROWS_A = 288
@@ -84,16 +86,23 @@
     return owner, bucket, inside - 2.0 * bucket
 
 
-def pack_ring(qk_ref, v_ref, w_ref, b_ref, msg_ref):
+def pack_ring(qk_ref, v_ref, w_ref, b_ref, msg_ref, sems):
+    copies = []
     for z in range(NZ):
         cols = slice(z * DIM, (z + 1) * DIM)
-        msg_ref[z, 0:128, :] = qk_ref[:, cols]
-        msg_ref[z, 128:256, :] = v_ref[:, cols]
-        msg_ref[z, 256:272, :] = w_ref[:, cols]
-        msg_ref[z, 272:288, :] = b_ref[...]
-
-
-def route(a_ref, msg_ref, srow_ref, scol_ref, y_ref):
+        for i, (ref, start, rows) in enumerate(((qk_ref, 0, 128), (v_ref, 128, 128), (w_ref, 256, 16))):
+            copies.append(
+                pltpu.make_async_copy(ref.at[:, cols], msg_ref.at[z, start : start + rows, :], sems.at[z, i])
+            )
+            copies[-1].start()
+    rows = jnp.concatenate([b_ref[...].astype(F32), jnp.zeros((14, TOK), F32)], axis=0).astype(BF)
+    for z in range(NZ):
+        msg_ref[z, 272:288, :] = rows
+    for copy in copies:
+        copy.wait()
+
+
+def route(a_ref, msg_ref, slot_ref, y_ref):
     sub = iota((TOK, TOK), 0)
     lane = iota((TOK, TOK), 1)
     swap = swap_matrix()
@@ -109,7 +118,7 @@
             pcol = jnp.sum(jnp.where(lane < sub, same, 0.0), axis=1, keepdims=True)
             srow = 2.0 * brow + prow
             scol = 2.0 * bcol + pcol
-            srow_ref[r * NZ + z : r * NZ + z + 1, :] = srow
+            slot_ref[r * NZ + z : r * NZ + z + 1, :] = srow
             scols = jnp.where(lane == r * NZ + z, scol, scols)
             rows = jnp.concatenate([a_ref[z, 0:128, :], a_ref[z, 128:256, :]], axis=1)
             y_ref[z, :, :] = dot(ones_where(slot_sub == srow), rows).astype(BF)
@@ -123,7 +132,7 @@
             moved = dot(swap, block).astype(BF)
             msg_ref[o, r * 128 : (r + 1) * 128, :] = moved[:, :DIM]
             msg_ref[o, 256 + r * 128 : 256 + (r + 1) * 128, :] = moved[:, DIM:]
-    scol_ref[...] = scols
+    slot_ref[16:144, :] = scols
     live = live.astype(BF)
     for o in range(NG):
         msg_ref[o, ROW_LIVE:ROWS_B, :] = live[o * 16 : (o + 1) * 16, :]
@@ -141,7 +150,7 @@
     return ref[:, start : start + 16, :].reshape(SLOTS, DIM)
 
 
-def attend(b_ref, msg_ref, logs_ref, qcode_ref, kcode_ref, w_ref):
+def attend(b_ref, msg_ref, state_ref, w_ref):
     lane = iota((SLOTS, TOK), 1)
     live = bucket_rows(b_ref, ROW_LIVE)
 
@@ -154,8 +163,6 @@
     kcol = jnp.where(live.astype(F32) > 0.5, span, 2.0).astype(BF)
     pick = ones_where(iota((16, TOK), 0) == iota((16, TOK), 1))
     krows = dot_nt(pick, kcol)
-    qcode_ref[...] = span
-    kcode_ref[...] = krows
     logs = jnp.zeros((SLOTS, TOK), F32)
     for r in range(ROUNDS):
         for k in range(BUCKETS):
@@ -170,7 +177,10 @@
             out = dot(probability, v).astype(BF)
             msg_ref[:, r * 128 + k * 16 : r * 128 + (k + 1) * 16, :] = out.reshape(NG, 16, DIM)
             logs = jnp.where((lane & 15) == n, largest + jnp.log(summed), logs)
-    logs_ref[...] = logs
+    shifted = dot_nt(span.astype(BF), ones_where(iota((TOK, TOK), 0) == iota((TOK, TOK), 1) + 16))
+    state_ref[0:256, :] = jnp.where(lane < 16, logs, shifted)
+    state_ref[256:272, :] = krows[:, 0:128]
+    state_ref[272:288, :] = krows[:, 128:256]
     msg_ref[:, ROW_EXTRA:ROWS_C, :] = three_parts(logs, lane).astype(BF).reshape(NG, 16, DIM)
     for x in range(NX):
         for y in range(NY):
@@ -179,7 +189,7 @@
                 w_ref[at : at + 16, :] = b_ref[x * NY + y, ROW_W + z * 16 : ROW_W + (z + 1) * 16, :]
 
 
-def combine(c_ref, srow_ref, scol_ref, grad_ref, msg_ref, att_ref, y_ref, s_ref):
+def combine(z_ref, c_ref, slot_ref, grad_ref, weight_ref, msg_ref, att_ref, turned_ref, y_ref, s_ref):
     lane = iota((TOK, TOK), 1)
     swap = swap_matrix()
     slot_sub = fiota((SLOTS, TOK), 0)
@@ -195,7 +205,7 @@
         outs, logs, marks = [], [], []
         for r in range(ROUNDS):
             n = r * NZ + z
-            scol = scol_ref[:, n : n + 1]
+            scol = slot_ref[16:144, n : n + 1]
             outs.append(dot(ones_where(slot_lane == scol), y_ref[r, z]))
             owner, bucket, place = split_slot(scol)
             parts = dot(ones_where(slot_lane == owner * 16.0 + (2.0 * z) + place), log_rows)
@@ -208,11 +218,13 @@
         weights = [one / total for one in lifted]
         att = (weights[0] * outs[0] + weights[1] * outs[1]).astype(BF)
         att_ref[z * TOK : (z + 1) * TOK, :] = att
-        grad = grad_ref[z * TOK : (z + 1) * TOK, :]
+        turned = pl.ds(pl.multiple_of(lax.rem(z_ref[0] - z + NZ, NZ) * TOK, TOK), TOK)
+        turned_ref[turned, :] = att
+        grad = grad_ref[turned, :]
         inner = jnp.sum(grad * att.astype(F32), axis=1, keepdims=True)
         for r in range(ROUNDS):
             n = r * NZ + z
-            srow = srow_ref[n : n + 1, :]
+            srow = slot_ref[n : n + 1, :]
             query_grad = (weights[r] * grad).astype(BF)
             s_ref[r, z] = dot(ones_where(slot_sub == srow), query_grad).astype(BF)
             owner, _, place = split_slot(srow)
@@ -226,11 +238,17 @@
             block = s_ref[r, :, o * 16 : (o + 1) * 16, :].reshape(TOK, DIM)
             msg_ref[o, r * 128 : (r + 1) * 128, :] = dot(swap, block).astype(BF)
     msg_ref[:, ROW_EXTRA:ROWS_C, :] = extra.astype(BF).reshape(NG, 16, DIM)
-
-
-def attend_back(b_ref, d_ref, logs_ref, qcode_ref, kcode_ref, gw_ref, msg_ref):
+    for h in range(NZ):
+        part = weight_ref[:, h * DIM : (h + 1) * DIM]
+        for o in range(NG):
+            msg_ref[o, ROW_PLANE + h * 16 : ROW_PLANE + (h + 1) * 16, :] = part
+
+
+def attend_back(b_ref, d_ref, state_ref, gw_ref, msg_ref, mark_ref):
     lane = iota((SLOTS, TOK), 1)
     shifts = bucket_rows(d_ref, ROW_EXTRA).astype(F32)
+    krows = jnp.concatenate([state_ref[256:272, :], state_ref[272:288, :]], axis=1)
+    mark_ref[...] = krows[0:8, 0:128]
     for r in range(ROUNDS):
         for k in range(BUCKETS):
             n = r * BUCKETS + k
@@ -238,9 +256,9 @@
             v = bucket_rows(b_ref, 256 + r * 128 + k * 16)
             g = bucket_rows(d_ref, r * 128 + k * 16)
             shift = jnp.sum(jnp.where((lane & 15) == n, shifts, 0.0), axis=1, keepdims=True)
-            seen = kcode_ref[n : n + 1, :] <= qcode_ref[:, n : n + 1]
+            seen = krows[n : n + 1, :] <= state_ref[0:256, 16 + n : 17 + n]
             scores = jnp.where(seen, raw_scores(q), MASKED)
-            probability = jnp.exp(scores - logs_ref[:, n : n + 1])
+            probability = jnp.exp(scores - state_ref[0:256, n : n + 1])
             score_grad = (probability * (dot_nt(g, v) - shift)).astype(BF)
             qk_grad = (dot(score_grad, q) + dot_tn(score_grad, q)) * SCALE
             value_grad = dot_tn(probability.astype(BF), g)
@@ -255,7 +273,41 @@
                 msg_ref[x * NY + y, ROW_GW + z * 16 : ROW_GW + (z + 1) * 16, :] = gw_ref[at : at + 16, :]
 
 
-def gather_home(e_ref, scol_ref, att_ref, msg_ref, y_ref):
+def join(*refs):
+    out_ref, sems = refs[NZ:]
+    copies = [
+        pltpu.make_async_copy(ref, out_ref.at[n * TOK : (n + 1) * TOK, :], sems.at[n])
+        for n, ref in enumerate(refs[:NZ])
+    ]
+    for copy in copies:
+        copy.start()
+    for copy in copies:
+        copy.wait()
+
+
+def project(place_ref, d_ref, *refs):
+    own_out, other_out, plane_ref, sem = refs[NZ:]
+    fetch = pltpu.make_async_copy(d_ref.at[:, ROW_PLANE:ROWS_D, :], plane_ref, sem)
+    fetch.start()
+    fetch.wait()
+    weights = []
+    for core in (place_ref[0], 1 - place_ref[0]):
+        parts = []
+        for turn in range(NZ):
+            head = lax.rem(place_ref[1] - turn + NZ, NZ)
+            rows = pl.ds(pl.multiple_of(head * 16, 16), 16)
+            parts.append(plane_ref[pl.ds(core * (NG // 2), NG // 2), rows, :].reshape(NG * 8, DIM))
+        weights.append(jnp.concatenate(parts, axis=1))
+    weights = jnp.concatenate(weights, axis=0)
+    for z in range(NZ):
+        tokens = slice(z * TOK, (z + 1) * TOK)
+        rows = jnp.concatenate([ref[tokens, :] for ref in refs[:NZ]], axis=1)
+        both = dot_nt(rows, weights)
+        own_out[tokens, :] = both[:, :DIM]
+        other_out[tokens, :] = both[:, DIM:]
+
+
+def gather_home(e_ref, slot_ref, own_ref, other_ref, msg_ref, y_ref):
     swap = swap_matrix()
     slot_lane = fiota((TOK, SLOTS), 1)
     for r in range(ROUNDS):
@@ -278,35 +330,49 @@
         rows = jnp.zeros((TOK, 2 * DIM), F32)
         for r in range(ROUNDS):
             n = r * NZ + z
-            rows = rows + dot(ones_where(slot_lane == scol_ref[:, n : n + 1]), y_ref[r, z])
+            rows = rows + dot(ones_where(slot_lane == slot_ref[16:144, n : n + 1]), y_ref[r, z])
         rows = rows.astype(BF)
         msg_ref[z, 0:128, :] = rows[:, :DIM]
         msg_ref[z, 128:256, :] = rows[:, DIM:]
-        msg_ref[z, 256:384, :] = att_ref[z * TOK : (z + 1) * TOK, :]
+        tokens = slice(z * TOK, (z + 1) * TOK)
+        msg_ref[z, 256:384, :] = (own_ref[tokens, :] + other_ref[tokens, :]).astype(BF)
         msg_ref[z, 384:400, :] = high[z * 16 : (z + 1) * 16, :]
         msg_ref[z, 400:416, :] = low[z * 16 : (z + 1) * 16, :]
 
 
-def unpack_ring(f_ref, qk_ref, v_ref, att_ref, gw_ref):
+def unpack_ring(f_ref, qk_ref, v_ref, mixed_ref, gw_ref):
     for z in range(NZ):
         cols = slice(z * DIM, (z + 1) * DIM)
         qk_ref[:, cols] = f_ref[z, 0:128, :]
         v_ref[:, cols] = f_ref[z, 128:256, :]
-        att_ref[:, cols] = f_ref[z, 256:384, :]
         gw_ref[:, cols] = f_ref[z, 384:400, :].astype(F32) + f_ref[z, 400:416, :].astype(F32)
-
-
-def on_device(body, outs, scratch=()):
-    shapes = [jax.ShapeDtypeStruct(shape, kind) for shape, kind in outs]
+    for z in range(0, NZ, 2):
+        first, second = f_ref[z, 256:384, :], f_ref[z + 1, 256:384, :]
+        for half in range(2):
+            cols = slice(half * 512 + z * 64, half * 512 + z * 64 + 128)
+            part = slice(half * 64, half * 64 + 64)
+            mixed_ref[:, cols] = jnp.concatenate([first[:, part], second[:, part]], axis=1)
+
+
+def on_device(body, outs, scratch=(), scalars=0, hbm_in=0, hbm_out=0, vmem=24):
+    shapes = [
+        pltpu.HBM(shape, kind) if n < hbm_out else jax.ShapeDtypeStruct(shape, kind)
+        for n, (shape, kind) in enumerate(outs)
+    ]
+    scratches = [pltpu.VMEM(*one) if isinstance(one, tuple) else one for one in scratch]
 
     def call(*operands):
+        places = [pltpu.SMEM] * scalars + [pltpu.HBM] * hbm_in
+        places += [pltpu.VMEM] * (len(operands) - len(places))
         return pl.pallas_call(
             body,
             out_shape=shapes,
-            in_specs=[pl.BlockSpec(memory_space=pltpu.VMEM)] * len(operands),
-            out_specs=[pl.BlockSpec(memory_space=pltpu.VMEM)] * len(shapes),
-            scratch_shapes=[pltpu.VMEM(shape, kind) for shape, kind in scratch],
-            compiler_params=pltpu.CompilerParams(vmem_limit_bytes=40 * 1024 * 1024),
+            in_specs=[pl.BlockSpec(memory_space=place) for place in places],
+            out_specs=[
+                pl.BlockSpec(memory_space=pltpu.HBM if n < hbm_out else pltpu.VMEM) for n in range(len(shapes))
+            ],
+            scratch_shapes=scratches,
+            compiler_params=pltpu.CompilerParams(vmem_limit_bytes=vmem * 1024 * 1024),
         )(*operands)
 
     return call
@@ -318,65 +384,97 @@
     )
 
 
+def swap_cores(array):
+    return lax.ppermute(array, "head", [(0, 1), (1, 0)])
+
+
+def pass_on(block, step):
+    turn = [
+        (ctx_of(x, z, y), ctx_of(x, (z + step) % NZ, y)) for x in range(NX) for z in range(NZ) for y in range(NY)
+    ]
+    return lax.ppermute(block, "ctx", turn)
+
+
+def ring_round(forward, backward):
+    return pass_on(forward, 1), pass_on(backward, -1)
+
+
+def after(arrays, event):
+    return lax.optimization_barrier((*arrays, event))[: len(arrays)]
+
+
 def per_device(shared_qk, values, out_grad, out_weight, buckets):
     core = lax.axis_index("head")
+    z_place = lax.rem(lax.axis_index("ctx") // NY, NZ)
     width = shared_qk.shape[1]
-    ring_grad = lax.all_gather(out_grad, "ctx", axis=0, tiled=True, axis_index_groups=RINGS)
-    whole_weight = lax.all_gather(out_weight, "ctx", axis=0, tiled=True)
-    other_grad = lax.ppermute(ring_grad, "head", [(0, 1), (1, 0)])
-
-    bucket_tile = jnp.pad(buckets.astype(BF), ((0, 14), (0, 0)))
-    (msg,) = on_device(pack_ring, [((NZ, ROWS_A, DIM), BF)])(
-        shared_qk, values, out_weight, bucket_tile
-    )
+
+    (msg,) = on_device(
+        pack_ring, [((NZ, ROWS_A, DIM), BF)], [pltpu.SemaphoreType.DMA((NZ, 3))], hbm_in=3, vmem=56
+    )(shared_qk, values, out_weight, buckets)
     got_a = exchange(msg, RINGS)
-    msg, slot_rows, slot_cols = on_device(
+    msg, slots = on_device(
         route,
-        [((NG, ROWS_B, DIM), BF), ((16, TOK), F32), ((TOK, TOK), F32)],
+        [((NG, ROWS_B, DIM), BF), ((16 + TOK, TOK), F32)],
         [((NZ, SLOTS, 2 * DIM), BF)],
     )(got_a)
+    late_grad, msg = lax.optimization_barrier((out_grad, msg))
     got_b = exchange(msg, PLANES)
-    msg, logs, query_code, key_code, head_weight = on_device(
-        attend,
-        [
-            ((NG, ROWS_C, DIM), BF),
-            ((SLOTS, TOK), F32),
-            ((SLOTS, TOK), F32),
-            ((16, SLOTS), F32),
-            ((2 * width, DIM), BF),
-        ],
+    before1, after1 = ring_round(late_grad, late_grad)
+    before2, after2 = ring_round(before1, after1)
+    before3, after3 = ring_round(before2, after2)
+    before4 = pass_on(before3, 1)
+    blocks = [late_grad, before1, before2, before3, before4, after3, after2, after1]
+    (ring_grad,) = on_device(
+        join, [((NZ * TOK, width), BF)], [pltpu.SemaphoreType.DMA((NZ,))], hbm_in=NZ, hbm_out=1
+    )(*blocks)
+    msg, state, head_weight = on_device(
+        attend, [((NG, ROWS_C, DIM), BF), ((SLOTS + 32, TOK), F32), ((2 * width, DIM), BF)]
     )(got_b)
     got_c = exchange(msg, PLANES)
+    other_grad = swap_cores(ring_grad)
     own_part = lax.dynamic_slice_in_dim(head_weight, core * width, width, 0)
     other_part = lax.dynamic_slice_in_dim(head_weight, (1 - core) * width, width, 0)
     attended_grad = dot(ring_grad, own_part) + dot(other_grad, other_part)
-    msg, attended = on_device(
+    msg, attended, turned = on_device(
         combine,
-        [((NG, ROWS_C, DIM), BF), ((NZ * TOK, DIM), BF)],
+        [((NG, ROWS_D, DIM), BF), ((NZ * TOK, DIM), BF), ((NZ * TOK, DIM), BF)],
         [((ROUNDS, NZ, SLOTS, DIM), BF), ((ROUNDS, NZ, SLOTS, DIM), BF)],
-    )(got_c, slot_rows, slot_cols, attended_grad)
+        scalars=1,
+    )(z_place.reshape(1), got_c, slots, attended_grad, out_weight)
     got_d = exchange(msg, PLANES)
-    own_gw = dot_tn(ring_grad, attended).astype(BF)
-    other_gw = dot_tn(other_grad, attended).astype(BF)
+    att_before1, att_after1 = ring_round(attended, attended)
+    att_before2, att_after2 = ring_round(att_before1, att_after1)
+    own_gw = dot_tn(ring_grad, turned).astype(BF)
+    other_gw = dot_tn(other_grad, turned).astype(BF)
     both_gw = jnp.concatenate(
         [jnp.where(core == 0, own_gw, other_gw), jnp.where(core == 0, other_gw, own_gw)], axis=0
     )
-    (msg,) = on_device(attend_back, [((NG, ROWS_E, DIM), BF)])(
-        got_b, got_d, logs, query_code, key_code, both_gw
+    got_d, att_before2, att_after2 = lax.optimization_barrier((got_d, att_before2, att_after2))
+    msg, mark = on_device(attend_back, [((NG, ROWS_E, DIM), BF), ((8, TOK), F32)])(
+        got_b, got_d, state, both_gw
     )
     got_e = exchange(msg, PLANES)
+    late_before2, late_after2 = after((att_before2, att_after2), mark)
+    att_before3, att_after3 = ring_round(late_before2, late_after2)
+    att_before4 = pass_on(att_before3, 1)
+    all_attended = [attended, att_before1, att_before2, att_before3, att_before4]
+    all_attended += [att_after3, att_after2, att_after1]
+    own_rows, other_rows = on_device(
+        project,
+        [((NZ * TOK, DIM), F32), ((NZ * TOK, DIM), F32)],
+        [((NG, ROWS_D - ROW_PLANE, DIM), BF), pltpu.SemaphoreType.DMA],
+        scalars=1,
+        hbm_in=1,
+    )(jnp.stack([core, z_place]), got_d, *all_attended)
+    other_rows = swap_cores(other_rows)
     (msg,) = on_device(
         gather_home, [((NZ, ROWS_F, DIM), BF)], [((ROUNDS, NZ, SLOTS, 2 * DIM), BF)]
-    )(got_e, slot_cols, attended)
+    )(got_e, slots, own_rows, other_rows)
     got_f = exchange(msg, RINGS)
-    grad_qk, grad_values, attended_rows, grad_weight = on_device(
+    grad_qk, grad_values, mixed, grad_weight = on_device(
         unpack_ring,
         [((TOK, width), BF), ((TOK, width), BF), ((TOK, width), BF), ((16, width), F32)],
     )(got_f)
-    partial_rows = dot_nt(attended_rows, whole_weight)
-    mine = lax.dynamic_slice_in_dim(partial_rows, core * width, width, 1)
-    theirs = lax.dynamic_slice_in_dim(partial_rows, (1 - core) * width, width, 1)
-    mixed = (mine + lax.ppermute(theirs, "head", [(0, 1), (1, 0)])).astype(BF)
     return (mixed, grad_qk, grad_values, grad_weight)
 
 

time: 240 us -> 213 us (0.89); the launches traced: 236 us -> 212 us
  blocking collectives: 104 us -> 54.3 us
  starting transfers between devices: 22.8 us -> 49.2 us
  between operations: 14.2 us -> 0.87 us
  waiting for transfers between devices: 49.8 us -> 57.7 us
  Pallas kernels: 21.1 us -> 29 us
  matrix products: 13.3 us -> 7.37 us
  local copies, waits for them, and re-layouts: 9.46 us -> 13.6 us
    all_to_all x3 -> x2, blocking collectives: 104 us -> 54.3 us  [exchange(): lax.all_to_all(message, 'ctx', split_axis=0, concat_axis=0, tiled=True, a...]
    ppermute x2 -> x16, waiting for transfers between devices: 1.9 us -> 39.9 us  [the longest x14 38 us: pass_on(): return lax.ppermute(block, 'ctx', turn)]
    all_to_all x3 -> x4, waiting for transfers between devices: 40.5 us -> 17.8 us  [exchange(): lax.all_to_all(message, 'ctx', split_axis=0, concat_axis=0, tiled=True, a...]
    ppermute x2 -> x16, starting transfers between devices: 0.1 us -> 20.1 us  [the longest x14 19.9 us: pass_on(): return lax.ppermute(block, 'ctx', turn)]
    pallas_call x7 -> x9, Pallas kernels: 21.1 us -> 29 us  [call(): pl.pallas_call(body, out_shape=shapes, in_specs=[pl.BlockSpec(memory_spac...]
    all_to_all x3 -> x4, starting transfers between devices: 22.6 us -> 29.1 us  [exchange(): lax.all_to_all(message, 'ctx', split_axis=0, concat_axis=0, tiled=True, a...]
    all_gather x2 -> x0, waiting for transfers between devices: 6.04 us -> none  [the longest x1 6.04 us: per_device(): lax.all_gather(out_grad, 'ctx', axis=0, tiled=True, axis_index_groups=RINGS)]
    unnamed x26 -> x44, local copies, waits for them, and re-layouts: 9.41 us -> 13.6 us
  transfers between devices with their start and end apart: 7 -> 20, of which waited for: 5 -> 14; matrix products, arithmetic and copies ran while one was open for 4% -> 4% of each run, Pallas kernels for 9% -> 4%
where the time goes in v2:
time: 213 us; the launch traced here: 212 us
  waiting for transfers between devices  57.7 us (27%)
  blocking collectives  54.3 us (25%)
  starting transfers between devices  49.2 us (23%)
  Pallas kernels  29 us (14%)
  local copies, waits for them, and re-layouts  13.6 us (6%)
  matrix products  7.37 us (3%)
    all_to_all x2, blocking collectives, exchange(): lax.all_to_all(message, 'ctx', split_axis=0, concat_axis=0, tiled=True, a...  54.3 us
    ppermute x14, waiting for transfers between devices, pass_on(): return lax.ppermute(block, 'ctx', turn)  38 us
    all_to_all x4, starting transfers between devices, exchange(): lax.all_to_all(message, 'ctx', split_axis=0, concat_axis=0, tiled=True, a...  29.1 us
    pallas_call x9, Pallas kernels, call(): pl.pallas_call(body, out_shape=shapes, in_specs=[pl.BlockSpec(memory_spac...  29 us
    ppermute x14, starting transfers between devices, pass_on(): return lax.ppermute(block, 'ctx', turn)  19.9 us
    all_to_all x4, waiting for transfers between devices, exchange(): lax.all_to_all(message, 'ctx', split_axis=0, concat_axis=0, tiled=True, a...  17.8 us
    unnamed x44, local copies, waits for them, and re-layouts  13.6 us
  transfers between devices with their start and end apart: 20, of which 14 were waited for; matrix products, arithmetic and copies ran while one was open for 4% of the time, Pallas kernels for 4%

profile of v2, /device:TPU:18, one launch (start us, length us, event | category | flops | bytes accessed | tf_op | source)
XLA Modules:
  0.0 212.2 jit_solution(9974605218502997389)
XLA Ops:
  0.6 2.8 %shard_map.84 = bf16[8,288,128]{2,1,0:T(8,128)(2,1)} custom-call(bf16[128,1024]{1,0:T(8,128)(2,1)} %qk_ref.1, bf16[128,1024]{1,0:T(8,128)(2,1)} %v_ref.1, bf16[16,1024]{1,0:T(8,128)(2,1)} %weight_ref.1, s32[2,128]{1,0:T(2,128)} %b_ref.1), custom_call_target="tpu_custom_call" | custom-call | tf_op jit(solution)/shard_map/pallas_call | solution.py:367
  3.5 27.4 %all_to_all.30.a_ref = bf16[8,288,128]{2,1,0:T(8,128)(2,1)S(1)} all-to-all(bf16[8,288,128]{2,1,0:T(8,128)(2,1)} %shard_map.84), channel_id=1, replica_groups={{0,8,16,24,32,40,48,56},{2,10,18,26,34,42,50,58},{4,12,20,28,36,44,52,6..., dimensions={0} | all-to-all | bytes 1179648 | tf_op jit(solution)/shard_map/all_to_all | solution.py:382
  34.8 7.2 %all-to-all-start.1 = ((bf16[16,656,128]{2,1,0:T(8,128)(2,1)}), bf16[16,656,128]{2,1,0:T(8,128)(2,1)S(1)}, u32[]{:S(2)}, u32[]{:S(2)}) async-start(bf16[16,656,128]{2,1,0:T(8,128)(2,1)} %copy-done), calls=%async_computation.1 | async-start | bytes 5373952 | tf_op jit(solution)/shard_map/all_to_all | solution.py:382
  42.1 2.7 %collective-permute-start.4 = (bf16[128,1024]{1,0:T(8,128)(2,1)S(1)}, bf16[128,1024]{1,0:T(8,128)(2,1)S(1)}, u32[]{:S(2)}, u32[]{:S(2)}) collective-permute-start(bf16[128,1024]{1,0:T(8,128)(2,1)S(1)} %copy-done.7), channel_id=1, source_target_pairs={{0,56},{2,58},{4,60},{6,62},{8,0},{10,2},{12,4},{14,6},{16,8},{18,... | collective-permute-start | bytes 786440 | tf_op jit(solution)/shard_map/ppermute | solution.py:395
  44.7 4.4 %collective-permute-done.4.refs_7_ = bf16[128,1024]{1,0:T(8,128)(2,1)S(1)} collective-permute-done((bf16[128,1024]{1,0:T(8,128)(2,1)S(1)}, bf16[128,1024]{1,0:T(8,128)(2,1)S(1)}, u32[]{:S(2)}, u32[]{:S(2)}) %collective-permute-start.4) | collective-permute-done | bytes 262176 | tf_op jit(solution)/shard_map/ppermute | solution.py:395
  49.2 3.2 %collective-permute-start.5 = (bf16[128,1024]{1,0:T(8,128)(2,1)S(1)}, bf16[128,1024]{1,0:T(8,128)(2,1)S(1)}, u32[]{:S(2)}, u32[]{:S(2)}) collective-permute-start(bf16[128,1024]{1,0:T(8,128)(2,1)S(1)} %collective-permute-done.4.refs_7_), channel_id=1, source_target_pairs={{0,56},{2,58},{4,60},{6,62},{8,0},{10,2},{12,4},{14,6},{16,8},{18,... | collective-permute-start | bytes 786440 | tf_op jit(solution)/shard_map/ppermute | solution.py:395
  52.4 4.7 %collective-permute-done.5.refs_6_ = bf16[128,1024]{1,0:T(8,128)(2,1)S(1)} collective-permute-done((bf16[128,1024]{1,0:T(8,128)(2,1)S(1)}, bf16[128,1024]{1,0:T(8,128)(2,1)S(1)}, u32[]{:S(2)}, u32[]{:S(2)}) %collective-permute-start.5) | collective-permute-done | bytes 262176 | tf_op jit(solution)/shard_map/ppermute | solution.py:395
  57.1 3.7 %collective-permute-start.6 = (bf16[128,1024]{1,0:T(8,128)(2,1)S(1)}, bf16[128,1024]{1,0:T(8,128)(2,1)S(1)}, u32[]{:S(2)}, u32[]{:S(2)}) collective-permute-start(bf16[128,1024]{1,0:T(8,128)(2,1)S(1)} %collective-permute-done.5.refs_6_), channel_id=1, source_target_pairs={{0,56},{2,58},{4,60},{6,62},{8,0},{10,2},{12,4},{14,6},{16,8},{18,... | collective-permute-start | bytes 786440 | tf_op jit(solution)/shard_map/ppermute | solution.py:395
  60.8 3.9 %collective-permute-done.6.refs_5_ = bf16[128,1024]{1,0:T(8,128)(2,1)S(1)} collective-permute-done((bf16[128,1024]{1,0:T(8,128)(2,1)S(1)}, bf16[128,1024]{1,0:T(8,128)(2,1)S(1)}, u32[]{:S(2)}, u32[]{:S(2)}) %collective-permute-start.6) | collective-permute-done | bytes 262176 | tf_op jit(solution)/shard_map/ppermute | solution.py:395
  64.7 3.7 %collective-permute-done.3.refs_4_ = bf16[128,1024]{1,0:T(8,128)(2,1)S(1)} collective-permute-done((bf16[128,1024]{1,0:T(8,128)(2,1)S(1)}, bf16[128,1024]{1,0:T(8,128)(2,1)S(1)}, u32[]{:S(2)}, u32[]{:S(2)}) %collective-permute-start.3) | collective-permute-done | bytes 262176 | tf_op jit(solution)/shard_map/ppermute | solution.py:395
  69.9 3.9 %all-to-all-done.1.b_ref = bf16[16,656,128]{2,1,0:T(8,128)(2,1)S(1)} async-done(((bf16[16,656,128]{2,1,0:T(8,128)(2,1)}), bf16[16,656,128]{2,1,0:T(8,128)(2,1)S(1)}, u32[]{:S(2)}, u32[]{:S(2)}) %all-to-all-start.1) | async-done | bytes 2687008 | tf_op jit(solution)/shard_map/all_to_all | solution.py:382
  73.8 3.7 %shard_map.86 = (bf16[16,272,128]{2,1,0:T(8,128)(2,1)S(1)}, f32[288,128]{1,0:T(8,128)S(1)}, bf16[2048,128]{1,0:T(8,128)(2,1)S(1)}) custom-call(bf16[16,656,128]{2,1,0:T(8,128)(2,1)S(1)} %all-to-all-done.1.b_ref), custom_call_target="tpu_custom_call" | custom-call | tf_op jit(solution)/shard_map/pallas_call | solution.py:367
  79.2 7.1 %all-to-all-start.2 = ((bf16[16,272,128]{2,1,0:T(8,128)(2,1)}), bf16[16,272,128]{2,1,0:T(8,128)(2,1)}, u32[]{:S(2)}, u32[]{:S(2)}) async-start(bf16[16,272,128]{2,1,0:T(8,128)(2,1)} %copy-done.3), calls=%async_computation.2 | async-start | bytes 2228224 | tf_op jit(solution)/shard_map/all_to_all | solution.py:382
  86.3 2.4 %fusion = f32[1024,128]{1,0:T(8,128)S(1)} fusion(bf16[1024,1024]{1,0:T(8,128)(2,1)} %collective-permute-done.7, bf16[2048,128]{1,0:T(8,128)(2,1)S(1)} %get-tuple-element.31, s32[]{:T(128)S(6)} %select_n.25), kind=kOutput, calls=%fused_computation.4 | convolution fusion | flops 268435456 | bytes 2883588 | tf_op jit(solution)/shard_map/dot_general | solution.py:53
  90.4 9.0 %all-to-all-done.2.c_ref = bf16[16,272,128]{2,1,0:T(8,128)(2,1)} async-done(((bf16[16,272,128]{2,1,0:T(8,128)(2,1)}), bf16[16,272,128]{2,1,0:T(8,128)(2,1)}, u32[]{:S(2)}, u32[]{:S(2)}) %all-to-all-start.2) | async-done | bytes 1114144 | tf_op jit(solution)/shard_map/all_to_all | solution.py:382
  100.2 5.3 %shard_map.88 = (bf16[16,400,128]{2,1,0:T(8,128)(2,1)S(1)}, bf16[1024,128]{1,0:T(8,128)(2,1)S(1)}, bf16[1024,128]{1,0:T(8,128)(2,1)S(1)}) custom-call(s32[1]{0:T(128)} %bitcast.z_ref, bf16[16,272,128]{2,1,0:T(8,128)(2,1)} %all-to-all-done.2.c_ref, f32[144,128]{1,0:T(8,128)S(1)} %get-tuple-element.29.slot_ref, f32[1024,128]{1,0:T(8,128)S(1)} %convolution_add_fusion.grad_ref, ...), custom_call_target="tpu_custom_call" | custom-call | tf_op jit(solution)/shard_map/pallas_call | solution.py:367
  107.4 7.2 %all-to-all-start.3 = ((bf16[16,400,128]{2,1,0:T(8,128)(2,1)}), bf16[16,400,128]{2,1,0:T(8,128)(2,1)}, u32[]{:S(2)}, u32[]{:S(2)}) async-start(bf16[16,400,128]{2,1,0:T(8,128)(2,1)} %copy-done.2), calls=%async_computation.3 | async-start | bytes 3276800 | tf_op jit(solution)/shard_map/all_to_all | solution.py:382
  114.6 2.9 %collective-permute-start.10 = (bf16[1024,128]{1,0:T(8,128)(2,1)S(1)}, bf16[1024,128]{1,0:T(8,128)(2,1)S(1)}, u32[]{:S(2)}, u32[]{:S(2)}) collective-permute-start(bf16[1024,128]{1,0:T(8,128)(2,1)S(1)} %get-tuple-element.33.refs_0_), channel_id=1, source_target_pairs={{0,56},{2,58},{4,60},{6,62},{8,0},{10,2},{12,4},{14,6},{16,8},{18,... | collective-permute-start | bytes 786440 | tf_op jit(solution)/shard_map/ppermute | solution.py:395
  117.5 2.5 %convolution_convert_fusion = bf16[1024,128]{1,0:T(8,128)(2,1)S(1)} fusion(bf16[1024,1024]{1,0:T(8,128)(2,1)} %collective-permute-done.7, bf16[1024,128]{1,0:T(8,128)(2,1)S(1)} %copy-done.16), kind=kOutput, calls=%fused_computation.1 | convolution fusion | flops 268566528 | bytes 2621440 | tf_op jit(solution)/shard_map/dot_general | solution.py:61
  120.0 2.1 collective-permute-done.10.refs_7_
  122.1 3.7 %collective-permute-start.11 = (bf16[1024,128]{1,0:T(8,128)(2,1)S(1)}, bf16[1024,128]{1,0:T(8,128)(2,1)S(1)}, u32[]{:S(2)}, u32[]{:S(2)}) collective-permute-start(bf16[1024,128]{1,0:T(8,128)(2,1)S(1)} %collective-permute-done.10.refs_7_), channel_id=1, source_target_pairs={{0,56},{2,58},{4,60},{6,62},{8,0},{10,2},{12,4},{14,6},{16,8},{18,... | collective-permute-start | bytes 786440 | tf_op jit(solution)/shard_map/ppermute | solution.py:395
  126.6 3.0 %collective-permute-done.11.refs_6_ = bf16[1024,128]{1,0:T(8,128)(2,1)S(1)} collective-permute-done((bf16[1024,128]{1,0:T(8,128)(2,1)S(1)}, bf16[1024,128]{1,0:T(8,128)(2,1)S(1)}, u32[]{:S(2)}, u32[]{:S(2)}) %collective-permute-start.11) | collective-permute-done | bytes 262176 | tf_op jit(solution)/shard_map/ppermute | solution.py:395
  130.4 3.1 %collective-permute-done.9.refs_2_ = bf16[1024,128]{1,0:T(8,128)(2,1)} collective-permute-done((bf16[1024,128]{1,0:T(8,128)(2,1)S(1)}, bf16[1024,128]{1,0:T(8,128)(2,1)}, u32[]{:S(2)}, u32[]{:S(2)}) %collective-permute-start.9) | collective-permute-done | bytes 262176 | tf_op jit(solution)/shard_map/ppermute | solution.py:395
  134.8 8.1 %shard_map.89 = (bf16[16,640,128]{2,1,0:T(8,128)(2,1)S(1)}, f32[8,128]{1,0:T(8,128)}) custom-call(bf16[16,656,128]{2,1,0:T(8,128)(2,1)S(1)} %all-to-all-done.1.b_ref, bf16[16,400,128]{2,1,0:T(8,128)(2,1)} %all-to-all-done.3.d_ref, f32[288,128]{1,0:T(8,128)S(1)} %copy-done.18, bf16[2048,128]{1,0:T(8,128)(2,1)S(1)} %pad_maximum_fusion.gw_ref), custom_call_target="tpu_custom_call" | custom-call | tf_op jit(solution)/shard_map/pallas_call | solution.py:367
  144.4 7.5 %all-to-all-start.4 = ((bf16[16,640,128]{2,1,0:T(8,128)(2,1)}), bf16[16,640,128]{2,1,0:T(8,128)(2,1)S(1)}, u32[]{:S(2)}, u32[]{:S(2)}) async-start(bf16[16,640,128]{2,1,0:T(8,128)(2,1)} %copy-done.1), calls=%async_computation.4 | async-start | bytes 5242880 | tf_op jit(solution)/shard_map/all_to_all | solution.py:382
  152.0 3.2 %collective-permute-start.14 = (bf16[1024,128]{1,0:T(8,128)(2,1)S(1)}, bf16[1024,128]{1,0:T(8,128)(2,1)S(1)}, u32[]{:S(2)}, u32[]{:S(2)}) collective-permute-start(bf16[1024,128]{1,0:T(8,128)(2,1)S(1)} %copy-done.13), channel_id=1, source_target_pairs={{0,56},{2,58},{4,60},{6,62},{8,0},{10,2},{12,4},{14,6},{16,8},{18,... | collective-permute-start | bytes 786440 | tf_op jit(solution)/shard_map/ppermute | solution.py:395
  155.2 5.6 %collective-permute-done.12.refs_3_ = bf16[1024,128]{1,0:T(8,128)(2,1)S(1)} collective-permute-done((bf16[1024,128]{1,0:T(8,128)(2,1)}, bf16[1024,128]{1,0:T(8,128)(2,1)S(1)}, u32[]{:S(2)}, u32[]{:S(2)}) %collective-permute-start.12) | collective-permute-done | bytes 262176 | tf_op jit(solution)/shard_map/ppermute | solution.py:395
  160.9 7.5 %collective-permute-done.13.refs_4_ = bf16[1024,128]{1,0:T(8,128)(2,1)S(1)} collective-permute-done((bf16[1024,128]{1,0:T(8,128)(2,1)S(1)}, bf16[1024,128]{1,0:T(8,128)(2,1)S(1)}, u32[]{:S(2)}, u32[]{:S(2)}) %collective-permute-start.13) | collective-permute-done | bytes 262176 | tf_op jit(solution)/shard_map/ppermute | solution.py:395
  171.2 3.5 %shard_map.90 = (f32[1024,128]{1,0:T(8,128)S(1)}, f32[1024,128]{1,0:T(8,128)S(1)}) custom-call(s32[2]{0:T(128)S(1)} %pad_add_fusion.place_ref, bf16[16,400,128]{2,1,0:T(8,128)(2,1)} %all-to-all-done.3.d_ref, bf16[1024,128]{1,0:T(8,128)(2,1)S(1)} %get-tuple-element.33.refs_0_, bf16[1024,128]{1,0:T(8,128)(2,1)S(1)} %copy-done.11, ...), custom_call_target="tpu_custom_call" | custom-call | tf_op jit(solution)/shard_map/pallas_call | solution.py:367
  174.8 1.9 collective-permute-done.15.other_ref
  177.5 4.6 %all-to-all-done.4.e_ref = bf16[16,640,128]{2,1,0:T(8,128)(2,1)S(1)} async-done(((bf16[16,640,128]{2,1,0:T(8,128)(2,1)}), bf16[16,640,128]{2,1,0:T(8,128)(2,1)S(1)}, u32[]{:S(2)}, u32[]{:S(2)}) %all-to-all-start.4) | async-done | bytes 2621472 | tf_op jit(solution)/shard_map/all_to_all | solution.py:382
  184.3 26.9 %all_to_all.31.f_ref = bf16[8,416,128]{2,1,0:T(8,128)(2,1)S(1)} all-to-all(bf16[8,416,128]{2,1,0:T(8,128)(2,1)S(1)} %shard_map.91), channel_id=1, replica_groups={{0,8,16,24,32,40,48,56},{2,10,18,26,34,42,50,58},{4,12,20,28,36,44,52,6..., dimensions={0} | all-to-all | bytes 1703936 | tf_op jit(solution)/shard_map/all_to_all | solution.py:382
  (69 shorter events, 22.9 us)
Async XLA Ops:
  0.6 33.6 %copy-start.7 = (bf16[128,1024]{1,0:T(8,128)(2,1)S(1)}, bf16[128,1024]{1,0:T(8,128)(2,1)}, u32[]{:S(2)}) copy-start(bf16[128,1024]{1,0:T(8,128)(2,1)} %refs_0_) | copy-start | bytes 786436
  32.7 1.5 copy-start
  34.2 10.5 %collective-permute-start = (bf16[128,1024]{1,0:T(8,128)(2,1)S(1)}, bf16[128,1024]{1,0:T(8,128)(2,1)S(1)}, u32[]{:S(2)}, u32[]{:S(2)}) collective-permute-start(bf16[128,1024]{1,0:T(8,128)(2,1)S(1)} %copy-done.7), channel_id=1, source_target_pairs={{0,8},{2,10},{4,12},{6,14},{8,16},{10,18},{12,20},{14,22},{16,24},... | collective-permute-start | bytes 786440 | tf_op jit(solution)/shard_map/ppermute | solution.py:395
  34.8 39.0 %all-to-all-start.1 = ((bf16[16,656,128]{2,1,0:T(8,128)(2,1)}), bf16[16,656,128]{2,1,0:T(8,128)(2,1)S(1)}, u32[]{:S(2)}, u32[]{:S(2)}) async-start(bf16[16,656,128]{2,1,0:T(8,128)(2,1)} %copy-done), calls=%async_computation.1 | async-start | bytes 5373952 | tf_op jit(solution)/shard_map/all_to_all | solution.py:382
  42.1 7.1 %collective-permute-start.4 = (bf16[128,1024]{1,0:T(8,128)(2,1)S(1)}, bf16[128,1024]{1,0:T(8,128)(2,1)S(1)}, u32[]{:S(2)}, u32[]{:S(2)}) collective-permute-start(bf16[128,1024]{1,0:T(8,128)(2,1)S(1)} %copy-done.7), channel_id=1, source_target_pairs={{0,56},{2,58},{4,60},{6,62},{8,0},{10,2},{12,4},{14,6},{16,8},{18,... | collective-permute-start | bytes 786440 | tf_op jit(solution)/shard_map/ppermute | solution.py:395
  44.7 7.6 %collective-permute-start.1 = (bf16[128,1024]{1,0:T(8,128)(2,1)S(1)}, bf16[128,1024]{1,0:T(8,128)(2,1)S(1)}, u32[]{:S(2)}, u32[]{:S(2)}) collective-permute-start(bf16[128,1024]{1,0:T(8,128)(2,1)S(1)} %collective-permute-done.refs_1_), channel_id=1, source_target_pairs={{0,8},{2,10},{4,12},{6,14},{8,16},{10,18},{12,20},{14,22},{16,24},... | collective-permute-start | bytes 786440 | tf_op jit(solution)/shard_map/ppermute | solution.py:395
  49.2 7.9 %collective-permute-start.5 = (bf16[128,1024]{1,0:T(8,128)(2,1)S(1)}, bf16[128,1024]{1,0:T(8,128)(2,1)S(1)}, u32[]{:S(2)}, u32[]{:S(2)}) collective-permute-start(bf16[128,1024]{1,0:T(8,128)(2,1)S(1)} %collective-permute-done.4.refs_7_), channel_id=1, source_target_pairs={{0,56},{2,58},{4,60},{6,62},{8,0},{10,2},{12,4},{14,6},{16,8},{18,... | collective-permute-start | bytes 786440 | tf_op jit(solution)/shard_map/ppermute | solution.py:395
  52.4 8.4 %collective-permute-start.2 = (bf16[128,1024]{1,0:T(8,128)(2,1)S(1)}, bf16[128,1024]{1,0:T(8,128)(2,1)S(1)}, u32[]{:S(2)}, u32[]{:S(2)}) collective-permute-start(bf16[128,1024]{1,0:T(8,128)(2,1)S(1)} %collective-permute-done.1.refs_2_), channel_id=1, source_target_pairs={{0,8},{2,10},{4,12},{6,14},{8,16},{10,18},{12,20},{14,22},{16,24},... | collective-permute-start | bytes 786440 | tf_op jit(solution)/shard_map/ppermute | solution.py:395
  57.1 7.6 %collective-permute-start.6 = (bf16[128,1024]{1,0:T(8,128)(2,1)S(1)}, bf16[128,1024]{1,0:T(8,128)(2,1)S(1)}, u32[]{:S(2)}, u32[]{:S(2)}) collective-permute-start(bf16[128,1024]{1,0:T(8,128)(2,1)S(1)} %collective-permute-done.5.refs_6_), channel_id=1, source_target_pairs={{0,56},{2,58},{4,60},{6,62},{8,0},{10,2},{12,4},{14,6},{16,8},{18,... | collective-permute-start | bytes 786440 | tf_op jit(solution)/shard_map/ppermute | solution.py:395
  60.8 7.6 %collective-permute-start.3 = (bf16[128,1024]{1,0:T(8,128)(2,1)S(1)}, bf16[128,1024]{1,0:T(8,128)(2,1)S(1)}, u32[]{:S(2)}, u32[]{:S(2)}) collective-permute-start(bf16[128,1024]{1,0:T(8,128)(2,1)S(1)} %collective-permute-done.2.refs_3_), channel_id=1, source_target_pairs={{0,8},{2,10},{4,12},{6,14},{8,16},{10,18},{12,20},{14,22},{16,24},... | collective-permute-start | bytes 786440 | tf_op jit(solution)/shard_map/ppermute | solution.py:395
  69.8 16.5 %collective-permute-start.7 = (bf16[1024,1024]{1,0:T(8,128)(2,1)}, bf16[1024,1024]{1,0:T(8,128)(2,1)}, u32[]{:S(2)}, u32[]{:S(2)}) collective-permute-start(bf16[1024,1024]{1,0:T(8,128)(2,1)} %shard_map.87), channel_id=1, source_target_pairs={{0,1},{1,0},{2,3},{3,2},{4,5},{5,4},{6,7},{7,6},{8,9},{9,8},{10,11... | collective-permute-start | bytes 6291464 | tf_op jit(solution)/shard_map/ppermute | solution.py:388
  77.5 1.0 copy-start.3
  79.2 7.1 %copy-start.4 = (bf16[2048,128]{1,0:T(8,128)(2,1)}, bf16[2048,128]{1,0:T(8,128)(2,1)S(1)}, u32[]{:S(2)}) copy-start(bf16[2048,128]{1,0:T(8,128)(2,1)S(1)} %get-tuple-element.31) | copy-start | bytes 1572868
  79.2 20.2 %all-to-all-start.2 = ((bf16[16,272,128]{2,1,0:T(8,128)(2,1)}), bf16[16,272,128]{2,1,0:T(8,128)(2,1)}, u32[]{:S(2)}, u32[]{:S(2)}) async-start(bf16[16,272,128]{2,1,0:T(8,128)(2,1)} %copy-done.3), calls=%async_computation.2 | async-start | bytes 2228224 | tf_op jit(solution)/shard_map/all_to_all | solution.py:382
  86.3 2.5 %copy-start.20 = (bf16[1024,1024]{1,0:T(8,128)(2,1)S(1)}, bf16[1024,1024]{1,0:T(8,128)(2,1)}, u32[]{:S(2)}) copy-start(bf16[1024,1024]{1,0:T(8,128)(2,1)} %shard_map.87) | copy-start | bytes 6291460
  105.5 1.2 copy-start.2
  107.4 10.1 %copy-start.16 = (bf16[1024,128]{1,0:T(8,128)(2,1)S(1)}, bf16[1024,128]{1,0:T(8,128)(2,1)}, u32[]{:S(2)}) copy-start(bf16[1024,128]{1,0:T(8,128)(2,1)} %copy-done.15) | copy-start | bytes 786436
  107.4 26.5 %all-to-all-start.3 = ((bf16[16,400,128]{2,1,0:T(8,128)(2,1)}), bf16[16,400,128]{2,1,0:T(8,128)(2,1)}, u32[]{:S(2)}, u32[]{:S(2)}) async-start(bf16[16,400,128]{2,1,0:T(8,128)(2,1)} %copy-done.2), calls=%async_computation.3 | async-start | bytes 3276800 | tf_op jit(solution)/shard_map/all_to_all | solution.py:382
  114.6 7.5 %collective-permute-start.10 = (bf16[1024,128]{1,0:T(8,128)(2,1)S(1)}, bf16[1024,128]{1,0:T(8,128)(2,1)S(1)}, u32[]{:S(2)}, u32[]{:S(2)}) collective-permute-start(bf16[1024,128]{1,0:T(8,128)(2,1)S(1)} %get-tuple-element.33.refs_0_), channel_id=1, source_target_pairs={{0,56},{2,58},{4,60},{6,62},{8,0},{10,2},{12,4},{14,6},{16,8},{18,... | collective-permute-start | bytes 786440 | tf_op jit(solution)/shard_map/ppermute | solution.py:395
  117.5 8.3 %collective-permute-start.8 = (bf16[1024,128]{1,0:T(8,128)(2,1)S(1)}, bf16[1024,128]{1,0:T(8,128)(2,1)S(1)}, u32[]{:S(2)}, u32[]{:S(2)}) collective-permute-start(bf16[1024,128]{1,0:T(8,128)(2,1)S(1)} %get-tuple-element.33.refs_0_), channel_id=1, source_target_pairs={{0,8},{2,10},{4,12},{6,14},{8,16},{10,18},{12,20},{14,22},{16,24},... | collective-permute-start | bytes 786440 | tf_op jit(solution)/shard_map/ppermute | solution.py:395
  117.5 8.3 %copy-start.21 = (bf16[1024,1024]{1,0:T(8,128)(2,1)S(1)}, bf16[1024,1024]{1,0:T(8,128)(2,1)}, u32[]{:S(2)}) copy-start(bf16[1024,1024]{1,0:T(8,128)(2,1)} %shard_map.87) | copy-start | bytes 6291460
  122.1 4.5 %copy-start.8 = (bf16[1024,128]{1,0:T(8,128)(2,1)}, bf16[1024,128]{1,0:T(8,128)(2,1)S(1)}, u32[]{:S(2)}) copy-start(bf16[1024,128]{1,0:T(8,128)(2,1)S(1)} %collective-permute-done.10.refs_7_) | copy-start | bytes 786436
  122.1 7.6 %collective-permute-start.11 = (bf16[1024,128]{1,0:T(8,128)(2,1)S(1)}, bf16[1024,128]{1,0:T(8,128)(2,1)S(1)}, u32[]{:S(2)}, u32[]{:S(2)}) collective-permute-start(bf16[1024,128]{1,0:T(8,128)(2,1)S(1)} %collective-permute-done.10.refs_7_), channel_id=1, source_target_pairs={{0,56},{2,58},{4,60},{6,62},{8,0},{10,2},{12,4},{14,6},{16,8},{18,... | collective-permute-start | bytes 786440 | tf_op jit(solution)/shard_map/ppermute | solution.py:395
  125.8 7.7 %collective-permute-start.9 = (bf16[1024,128]{1,0:T(8,128)(2,1)S(1)}, bf16[1024,128]{1,0:T(8,128)(2,1)}, u32[]{:S(2)}, u32[]{:S(2)}) collective-permute-start(bf16[1024,128]{1,0:T(8,128)(2,1)S(1)} %collective-permute-done.8.refs_1_), channel_id=1, source_target_pairs={{0,8},{2,10},{4,12},{6,14},{8,16},{10,18},{12,20},{14,22},{16,24},... | collective-permute-start | bytes 786440 | tf_op jit(solution)/shard_map/ppermute | solution.py:395
  142.9 1.5 copy-start.1
  144.4 7.6 %copy-start.13 = (bf16[1024,128]{1,0:T(8,128)(2,1)S(1)}, bf16[1024,128]{1,0:T(8,128)(2,1)}, u32[]{:S(2)}) copy-start(bf16[1024,128]{1,0:T(8,128)(2,1)} %copy-done.12) | copy-start | bytes 786436
  144.4 37.6 %all-to-all-start.4 = ((bf16[16,640,128]{2,1,0:T(8,128)(2,1)}), bf16[16,640,128]{2,1,0:T(8,128)(2,1)S(1)}, u32[]{:S(2)}, u32[]{:S(2)}) async-start(bf16[16,640,128]{2,1,0:T(8,128)(2,1)} %copy-done.1), calls=%async_computation.4 | async-start | bytes 5242880 | tf_op jit(solution)/shard_map/all_to_all | solution.py:382
  152.0 8.8 %collective-permute-start.12 = (bf16[1024,128]{1,0:T(8,128)(2,1)}, bf16[1024,128]{1,0:T(8,128)(2,1)S(1)}, u32[]{:S(2)}, u32[]{:S(2)}) collective-permute-start(bf16[1024,128]{1,0:T(8,128)(2,1)} %collective-permute-done.9.refs_2_), channel_id=1, source_target_pairs={{0,8},{2,10},{4,12},{6,14},{8,16},{10,18},{12,20},{14,22},{16,24},... | collective-permute-start | bytes 786440 | tf_op jit(solution)/shard_map/ppermute | solution.py:395
  152.0 8.9 %collective-permute-start.14 = (bf16[1024,128]{1,0:T(8,128)(2,1)S(1)}, bf16[1024,128]{1,0:T(8,128)(2,1)S(1)}, u32[]{:S(2)}, u32[]{:S(2)}) collective-permute-start(bf16[1024,128]{1,0:T(8,128)(2,1)S(1)} %copy-done.13), channel_id=1, source_target_pairs={{0,56},{2,58},{4,60},{6,62},{8,0},{10,2},{12,4},{14,6},{16,8},{18,... | collective-permute-start | bytes 786440 | tf_op jit(solution)/shard_map/ppermute | solution.py:395
  160.8 7.6 %collective-permute-start.13 = (bf16[1024,128]{1,0:T(8,128)(2,1)S(1)}, bf16[1024,128]{1,0:T(8,128)(2,1)S(1)}, u32[]{:S(2)}, u32[]{:S(2)}) collective-permute-start(bf16[1024,128]{1,0:T(8,128)(2,1)S(1)} %collective-permute-done.12.refs_3_), channel_id=1, source_target_pairs={{0,8},{2,10},{4,12},{6,14},{8,16},{10,18},{12,20},{14,22},{16,24},... | collective-permute-start | bytes 786440 | tf_op jit(solution)/shard_map/ppermute | solution.py:395
  174.7 2.0 collective-permute-start.15
  182.1 1.0 copy-start.6
  (10 other events, 8.2 us)

commit v3 on v2

--- a/solution.py
+++ b/solution.py
@@ -86,31 +86,34 @@
     return owner, bucket, inside - 2.0 * bucket
 
 
-def pack_ring(qk_ref, v_ref, w_ref, b_ref, msg_ref, sems):
-    copies = []
-    for z in range(NZ):
-        cols = slice(z * DIM, (z + 1) * DIM)
-        for i, (ref, start, rows) in enumerate(((qk_ref, 0, 128), (v_ref, 128, 128), (w_ref, 256, 16))):
-            copies.append(
-                pltpu.make_async_copy(ref.at[:, cols], msg_ref.at[z, start : start + rows, :], sems.at[z, i])
-            )
-            copies[-1].start()
+def pack_ring(qk_in, v_in, w_in, b_in, msg_ref, qk_ref, v_ref, w_ref, b_ref, sems):
+    fetches = [
+        pltpu.make_async_copy(source, dest, sems.at[n])
+        for n, (source, dest) in enumerate(((qk_in, qk_ref), (v_in, v_ref), (w_in, w_ref), (b_in, b_ref)))
+    ]
+    for fetch in fetches:
+        fetch.start()
+    fetches[3].wait()
     rows = jnp.concatenate([b_ref[...].astype(F32), jnp.zeros((14, TOK), F32)], axis=0).astype(BF)
     for z in range(NZ):
         msg_ref[z, 272:288, :] = rows
-    for copy in copies:
-        copy.wait()
-
-
-def route(a_ref, msg_ref, slot_ref, y_ref):
+    for fetch, ref, span in zip(fetches, (qk_ref, v_ref, w_ref), ((0, 128), (128, 256), (256, 272))):
+        fetch.wait()
+        for z in range(NZ):
+            msg_ref[z, slice(*span), :] = ref[:, z * DIM : (z + 1) * DIM]
+
+
+def route(a_ref, slot_out, msg_out, slot_ref, y_ref, msg_ref, sems):
     sub = iota((TOK, TOK), 0)
     lane = iota((TOK, TOK), 1)
     swap = swap_matrix()
     slot_sub = fiota((SLOTS, TOK), 0)
     live = jnp.zeros((SLOTS, TOK), F32)
     scols = jnp.zeros((TOK, TOK), F32)
-    for r in range(ROUNDS):
-        for z in range(NZ):
+    for z in range(NZ):
+        rows = jnp.concatenate([a_ref[z, 0:128, :], a_ref[z, 128:256, :]], axis=1)
+        places, marks = [], []
+        for r in range(ROUNDS):
             brow = a_ref[z, 272:288, :].astype(F32)[r : r + 1, :]
             bcol = jnp.sum(jnp.where(sub == lane, brow, 0.0), axis=1, keepdims=True)
             same = jnp.where(bcol == brow, 1.0, 0.0)
@@ -120,24 +123,29 @@
             scol = 2.0 * bcol + pcol
             slot_ref[r * NZ + z : r * NZ + z + 1, :] = srow
             scols = jnp.where(lane == r * NZ + z, scol, scols)
-            rows = jnp.concatenate([a_ref[z, 0:128, :], a_ref[z, 128:256, :]], axis=1)
-            y_ref[z, :, :] = dot(ones_where(slot_sub == srow), rows).astype(BF)
+            y_ref[r, z] = dot(ones_where(slot_sub == srow), rows).astype(BF)
             owner, _, _ = split_slot(srow)
-            place = owner * 16.0 + (2.0 * z) + prow
+            places.append(ones_where(slot_sub == owner * 16.0 + (2.0 * z) + prow))
             _, bucket, _ = split_slot(scol)
-            mark = ones_where(lane.astype(F32) == bucket + (1.0 * r * BUCKETS))
-            live = live + dot(ones_where(slot_sub == place), mark)
-        for o in range(NG):
-            block = y_ref[:, o * 16 : (o + 1) * 16, :].reshape(TOK, 2 * DIM)
+            marks.append(ones_where(lane.astype(F32) == bucket + (1.0 * r * BUCKETS)))
+        live = live + dot(jnp.concatenate(places, axis=1), jnp.concatenate(marks, axis=0))
+    slot_ref[16:144, :] = scols
+    keeps = [pltpu.make_async_copy(slot_ref, slot_out, sems.at[NG])]
+    keeps[0].start()
+    live = live.astype(BF)
+    for o in range(NG):
+        for r in range(ROUNDS):
+            block = y_ref[r, :, o * 16 : (o + 1) * 16, :].reshape(TOK, 2 * DIM)
             moved = dot(swap, block).astype(BF)
             msg_ref[o, r * 128 : (r + 1) * 128, :] = moved[:, :DIM]
             msg_ref[o, 256 + r * 128 : 256 + (r + 1) * 128, :] = moved[:, DIM:]
-    slot_ref[16:144, :] = scols
-    live = live.astype(BF)
-    for o in range(NG):
         msg_ref[o, ROW_LIVE:ROWS_B, :] = live[o * 16 : (o + 1) * 16, :]
         for z in range(NZ):
             msg_ref[o, ROW_W + z * 16 : ROW_W + (z + 1) * 16, :] = a_ref[z, 256:272, :]
+        keeps.append(pltpu.make_async_copy(msg_ref.at[o], msg_out.at[o], sems.at[o]))
+        keeps[-1].start()
+    for keep in keeps:
+        keep.wait()
 
 
 def raw_scores(q):
@@ -150,7 +158,7 @@
     return ref[:, start : start + 16, :].reshape(SLOTS, DIM)
 
 
-def attend(b_ref, msg_ref, state_ref, w_ref):
+def attend(b_ref, state_out, msg_ref, w_ref, state_ref, sem):
     lane = iota((SLOTS, TOK), 1)
     live = bucket_rows(b_ref, ROW_LIVE)
 
@@ -181,37 +189,59 @@
     state_ref[0:256, :] = jnp.where(lane < 16, logs, shifted)
     state_ref[256:272, :] = krows[:, 0:128]
     state_ref[272:288, :] = krows[:, 128:256]
+    keep = pltpu.make_async_copy(state_ref, state_out, sem)
+    keep.start()
     msg_ref[:, ROW_EXTRA:ROWS_C, :] = three_parts(logs, lane).astype(BF).reshape(NG, 16, DIM)
     for x in range(NX):
         for y in range(NY):
             for z in range(NZ):
                 at = ctx_of(x, z, y) * 16
                 w_ref[at : at + 16, :] = b_ref[x * NY + y, ROW_W + z * 16 : ROW_W + (z + 1) * 16, :]
-
-
-def combine(z_ref, c_ref, slot_ref, grad_ref, weight_ref, msg_ref, att_ref, turned_ref, y_ref, s_ref):
+    keep.wait()
+
+
+def recall(b_ref, state_ref, prob_ref, turned_ref, mark_ref):
+    krows = jnp.concatenate([state_ref[256:272, :], state_ref[272:288, :]], axis=1)
+    for n in range(ROUNDS * BUCKETS):
+        q = bucket_rows(b_ref, n * 16)
+        seen = krows[n : n + 1, :] <= state_ref[0:256, 16 + n : 17 + n]
+        scores = jnp.where(seen, raw_scores(q), MASKED)
+        probability = jnp.exp(scores - state_ref[0:256, n : n + 1])
+        prob_ref[n] = probability
+        turned_ref[n] = probability.T.astype(BF)
+    mark_ref[...] = krows[0:8, 0:128]
+
+
+def combine(
+    z_ref, slot_in, weight_in, c_ref, grad_ref, turned_out, msg_out, att_ref,
+    y_ref, s_ref, slot_ref, weight_ref, turned_ref, msg_ref, sems,
+):
+    fetch = pltpu.make_async_copy(slot_in, slot_ref, sems.at[NZ])
+    fetch.start()
+    fetch_weight = pltpu.make_async_copy(weight_in, weight_ref, sems.at[NZ + 1])
+    fetch_weight.start()
+    keeps = []
     lane = iota((TOK, TOK), 1)
     swap = swap_matrix()
     slot_sub = fiota((SLOTS, TOK), 0)
     slot_lane = fiota((TOK, SLOTS), 1)
-    for r in range(ROUNDS):
-        for o in range(NG):
-            moved = dot(swap, c_ref[o, r * 128 : (r + 1) * 128, :]).astype(BF)
-            y_ref[r, :, o * 16 : (o + 1) * 16, :] = moved.reshape(NZ, 16, DIM)
+    for o in range(NG):
+        rows = jnp.concatenate([c_ref[o, 0:128, :], c_ref[o, 128:256, :]], axis=1)
+        y_ref[:, o * 16 : (o + 1) * 16, :] = dot(swap, rows).astype(BF).reshape(NZ, 16, 2 * DIM)
     log_rows = bucket_rows(c_ref, ROW_EXTRA)
     extra = jnp.zeros((SLOTS, TOK), F32)
-    folded = lane & 15
+    folded = (lane & 15).astype(F32)
+    fetch.wait()
     for z in range(NZ):
         outs, logs, marks = [], [], []
         for r in range(ROUNDS):
             n = r * NZ + z
             scol = slot_ref[16:144, n : n + 1]
-            outs.append(dot(ones_where(slot_lane == scol), y_ref[r, z]))
+            outs.append(dot(ones_where(slot_lane == scol), y_ref[z, :, r * DIM : (r + 1) * DIM]))
             owner, bucket, place = split_slot(scol)
             parts = dot(ones_where(slot_lane == owner * 16.0 + (2.0 * z) + place), log_rows)
-            mark = folded.astype(F32) == bucket + (1.0 * r * BUCKETS)
-            marks.append(mark)
-            logs.append(jnp.sum(jnp.where(mark, parts, 0.0), axis=1, keepdims=True))
+            marks.append(folded == bucket + (1.0 * r * BUCKETS))
+            logs.append(jnp.sum(jnp.where(marks[r], parts, 0.0), axis=1, keepdims=True))
         largest = jnp.maximum(logs[0], logs[1])
         lifted = [jnp.exp(log - largest) for log in logs]
         total = lifted[0] + lifted[1]
@@ -219,58 +249,69 @@
         att = (weights[0] * outs[0] + weights[1] * outs[1]).astype(BF)
         att_ref[z * TOK : (z + 1) * TOK, :] = att
         turned = pl.ds(pl.multiple_of(lax.rem(z_ref[0] - z + NZ, NZ) * TOK, TOK), TOK)
-        turned_ref[turned, :] = att
+        turned_ref[z * TOK : (z + 1) * TOK, :] = att
+        keeps.append(
+            pltpu.make_async_copy(turned_ref.at[z * TOK : (z + 1) * TOK, :], turned_out.at[turned, :], sems.at[z])
+        )
+        keeps[-1].start()
         grad = grad_ref[turned, :]
         inner = jnp.sum(grad * att.astype(F32), axis=1, keepdims=True)
         for r in range(ROUNDS):
             n = r * NZ + z
             srow = slot_ref[n : n + 1, :]
             query_grad = (weights[r] * grad).astype(BF)
-            s_ref[r, z] = dot(ones_where(slot_sub == srow), query_grad).astype(BF)
+            s_ref[z, :, r * DIM : (r + 1) * DIM] = dot(ones_where(slot_sub == srow), query_grad).astype(BF)
             owner, _, place = split_slot(srow)
             spread = jnp.where(marks[r], weights[r] * inner, 0.0)
             extra = extra + dot(
                 ones_where(slot_sub == owner * 16.0 + (2.0 * z) + place),
                 three_parts(spread, lane).astype(BF),
             )
-    for r in range(ROUNDS):
-        for o in range(NG):
-            block = s_ref[r, :, o * 16 : (o + 1) * 16, :].reshape(TOK, DIM)
-            msg_ref[o, r * 128 : (r + 1) * 128, :] = dot(swap, block).astype(BF)
-    msg_ref[:, ROW_EXTRA:ROWS_C, :] = extra.astype(BF).reshape(NG, 16, DIM)
-    for h in range(NZ):
-        part = weight_ref[:, h * DIM : (h + 1) * DIM]
-        for o in range(NG):
-            msg_ref[o, ROW_PLANE + h * 16 : ROW_PLANE + (h + 1) * 16, :] = part
-
-
-def attend_back(b_ref, d_ref, state_ref, gw_ref, msg_ref, mark_ref):
-    lane = iota((SLOTS, TOK), 1)
-    shifts = bucket_rows(d_ref, ROW_EXTRA).astype(F32)
-    krows = jnp.concatenate([state_ref[256:272, :], state_ref[272:288, :]], axis=1)
-    mark_ref[...] = krows[0:8, 0:128]
-    for r in range(ROUNDS):
-        for k in range(BUCKETS):
-            n = r * BUCKETS + k
-            q = bucket_rows(b_ref, r * 128 + k * 16)
-            v = bucket_rows(b_ref, 256 + r * 128 + k * 16)
-            g = bucket_rows(d_ref, r * 128 + k * 16)
-            shift = jnp.sum(jnp.where((lane & 15) == n, shifts, 0.0), axis=1, keepdims=True)
-            seen = krows[n : n + 1, :] <= state_ref[0:256, 16 + n : 17 + n]
-            scores = jnp.where(seen, raw_scores(q), MASKED)
-            probability = jnp.exp(scores - state_ref[0:256, n : n + 1])
-            score_grad = (probability * (dot_nt(g, v) - shift)).astype(BF)
-            qk_grad = (dot(score_grad, q) + dot_tn(score_grad, q)) * SCALE
-            value_grad = dot_tn(probability.astype(BF), g)
-            rows = slice(r * 128 + k * 16, r * 128 + (k + 1) * 16)
-            msg_ref[:, rows, :] = qk_grad.astype(BF).reshape(NG, 16, DIM)
-            rows = slice(256 + r * 128 + k * 16, 256 + r * 128 + (k + 1) * 16)
-            msg_ref[:, rows, :] = value_grad.astype(BF).reshape(NG, 16, DIM)
+    fetch_weight.wait()
+    extra = extra.astype(BF)
+    for o in range(NG):
+        moved = dot(swap, s_ref[:, o * 16 : (o + 1) * 16, :].reshape(TOK, 2 * DIM)).astype(BF)
+        msg_ref[o, 0:128, :] = moved[:, :DIM]
+        msg_ref[o, 128:256, :] = moved[:, DIM:]
+        msg_ref[o, ROW_EXTRA:ROWS_C, :] = extra[o * 16 : (o + 1) * 16, :]
+        for h in range(NZ):
+            msg_ref[o, ROW_PLANE + h * 16 : ROW_PLANE + (h + 1) * 16, :] = weight_ref[:, h * DIM : (h + 1) * DIM]
+        keeps.append(pltpu.make_async_copy(msg_ref.at[o], msg_out.at[o], sems.at[NZ + 2 + o]))
+        keeps[-1].start()
+    for keep in keeps:
+        keep.wait()
+
+
+def attend_back(d_in, b_ref, prob_ref, turned_ref, gw_ref, msg_ref, mark_ref, d_ref, sems):
+    fetches = [
+        pltpu.make_async_copy(d_in.at[:, rows, :], d_ref.at[:, rows, :], sems.at[n])
+        for n, rows in enumerate((slice(ROW_EXTRA, ROWS_C), slice(0, 128), slice(128, 256)))
+    ]
+    for fetch in fetches:
+        fetch.start()
     for x in range(NX):
         for y in range(NY):
             for z in range(NZ):
                 at = ctx_of(x, z, y) * 16
                 msg_ref[x * NY + y, ROW_GW + z * 16 : ROW_GW + (z + 1) * 16, :] = gw_ref[at : at + 16, :]
+    lane = iota((SLOTS, TOK), 1)
+    fetches[0].wait()
+    shifts = bucket_rows(d_ref, ROW_EXTRA).astype(F32)
+    for r in range(ROUNDS):
+        fetches[1 + r].wait()
+        for k in range(BUCKETS):
+            n = r * BUCKETS + k
+            q = bucket_rows(b_ref, n * 16)
+            v = bucket_rows(b_ref, 256 + n * 16)
+            g = bucket_rows(d_ref, n * 16)
+            shift = jnp.sum(jnp.where((lane & 15) == n, shifts, 0.0), axis=1, keepdims=True)
+            score_grad = (prob_ref[n] * (dot_nt(g, v) - shift)).astype(BF)
+            qk_grad = (dot(score_grad, q) + dot_tn(score_grad, q)) * SCALE
+            value_grad = dot(turned_ref[n], g)
+            msg_ref[:, n * 16 : (n + 1) * 16, :] = qk_grad.astype(BF).reshape(NG, 16, DIM)
+            rows = slice(256 + n * 16, 256 + (n + 1) * 16)
+            msg_ref[:, rows, :] = value_grad.astype(BF).reshape(NG, 16, DIM)
+    mark_ref[...] = shifts[0:8, :]
 
 
 def join(*refs):
@@ -286,9 +327,15 @@
 
 
 def project(place_ref, d_ref, *refs):
-    own_out, other_out, plane_ref, sem = refs[NZ:]
+    own_out, other_out, plane_ref, att_ref, sem, sems = refs[NZ:]
     fetch = pltpu.make_async_copy(d_ref.at[:, ROW_PLANE:ROWS_D, :], plane_ref, sem)
     fetch.start()
+    blocks = [
+        pltpu.make_async_copy(ref, att_ref.at[:, n * DIM : (n + 1) * DIM], sems.at[n])
+        for n, ref in enumerate(refs[:NZ])
+    ]
+    for block in blocks:
+        block.start()
     fetch.wait()
     weights = []
     for core in (place_ref[0], 1 - place_ref[0]):
@@ -299,15 +346,22 @@
             parts.append(plane_ref[pl.ds(core * (NG // 2), NG // 2), rows, :].reshape(NG * 8, DIM))
         weights.append(jnp.concatenate(parts, axis=1))
     weights = jnp.concatenate(weights, axis=0)
+    for block in blocks:
+        block.wait()
     for z in range(NZ):
         tokens = slice(z * TOK, (z + 1) * TOK)
-        rows = jnp.concatenate([ref[tokens, :] for ref in refs[:NZ]], axis=1)
-        both = dot_nt(rows, weights)
+        both = dot_nt(att_ref[tokens, :], weights)
         own_out[tokens, :] = both[:, :DIM]
         other_out[tokens, :] = both[:, DIM:]
 
 
-def gather_home(e_ref, slot_ref, own_ref, other_ref, msg_ref, y_ref):
+def gather_home(slot_in, own_in, other_in, e_ref, msg_ref, y_ref, slot_ref, own_ref, other_ref, sems):
+    fetches = [
+        pltpu.make_async_copy(source, dest, sems.at[n])
+        for n, (source, dest) in enumerate(((slot_in, slot_ref), (own_in, own_ref), (other_in, other_ref)))
+    ]
+    for fetch in fetches:
+        fetch.start()
     swap = swap_matrix()
     slot_lane = fiota((TOK, SLOTS), 1)
     for r in range(ROUNDS):
@@ -319,25 +373,27 @@
                 ],
                 axis=1,
             )
-            y_ref[r, :, o * 16 : (o + 1) * 16, :] = dot(swap, rows).astype(BF).reshape(NZ, 16, 2 * DIM)
+            at = r * SLOTS + o * 16
+            y_ref[:, at : at + 16, :] = dot(swap, rows).astype(BF).reshape(NZ, 16, 2 * DIM)
     total = jnp.zeros((TOK, DIM), F32)
     for o in range(NG):
         total = total + e_ref[o, ROW_GW:ROWS_E, :].astype(F32)
     total = total * (1.0 / math.sqrt(NX * NY * NZ * TOK))
     high = total.astype(BF)
     low = (total - high.astype(F32)).astype(BF)
+    fetches[0].wait()
     for z in range(NZ):
-        rows = jnp.zeros((TOK, 2 * DIM), F32)
-        for r in range(ROUNDS):
-            n = r * NZ + z
-            rows = rows + dot(ones_where(slot_lane == slot_ref[16:144, n : n + 1]), y_ref[r, z])
-        rows = rows.astype(BF)
+        picks = [ones_where(slot_lane == slot_ref[16:144, n : n + 1]) for n in (z, NZ + z)]
+        rows = dot(jnp.concatenate(picks, axis=1), y_ref[z]).astype(BF)
         msg_ref[z, 0:128, :] = rows[:, :DIM]
         msg_ref[z, 128:256, :] = rows[:, DIM:]
+        msg_ref[z, 384:400, :] = high[z * 16 : (z + 1) * 16, :]
+        msg_ref[z, 400:416, :] = low[z * 16 : (z + 1) * 16, :]
+    fetches[1].wait()
+    fetches[2].wait()
+    for z in range(NZ):
         tokens = slice(z * TOK, (z + 1) * TOK)
         msg_ref[z, 256:384, :] = (own_ref[tokens, :] + other_ref[tokens, :]).astype(BF)
-        msg_ref[z, 384:400, :] = high[z * 16 : (z + 1) * 16, :]
-        msg_ref[z, 400:416, :] = low[z * 16 : (z + 1) * 16, :]
 
 
 def unpack_ring(f_ref, qk_ref, v_ref, mixed_ref, gw_ref):
@@ -354,7 +410,7 @@
             mixed_ref[:, cols] = jnp.concatenate([first[:, part], second[:, part]], axis=1)
 
 
-def on_device(body, outs, scratch=(), scalars=0, hbm_in=0, hbm_out=0, vmem=24):
+def on_device(body, outs, scratch=(), scalars=0, hbm_in=0, hbm_out=0, vmem=24, cost=None, pin=True):
     shapes = [
         pltpu.HBM(shape, kind) if n < hbm_out else jax.ShapeDtypeStruct(shape, kind)
         for n, (shape, kind) in enumerate(outs)
@@ -362,6 +418,10 @@
     scratches = [pltpu.VMEM(*one) if isinstance(one, tuple) else one for one in scratch]
 
     def call(*operands):
+        operands = [
+            pltpu.with_memory_space_constraint(one, pltpu.HBM) if pin and scalars <= n < scalars + hbm_in else one
+            for n, one in enumerate(operands)
+        ]
         places = [pltpu.SMEM] * scalars + [pltpu.HBM] * hbm_in
         places += [pltpu.VMEM] * (len(operands) - len(places))
         return pl.pallas_call(
@@ -372,6 +432,9 @@
                 pl.BlockSpec(memory_space=pltpu.HBM if n < hbm_out else pltpu.VMEM) for n in range(len(shapes))
             ],
             scratch_shapes=scratches,
+            cost_estimate=None if cost is None else pl.CostEstimate(
+                flops=cost[0], bytes_accessed=cost[1], transcendentals=cost[2]
+            ),
             compiler_params=pltpu.CompilerParams(vmem_limit_bytes=vmem * 1024 * 1024),
         )(*operands)
 
@@ -409,13 +472,28 @@
     width = shared_qk.shape[1]
 
     (msg,) = on_device(
-        pack_ring, [((NZ, ROWS_A, DIM), BF)], [pltpu.SemaphoreType.DMA((NZ, 3))], hbm_in=3, vmem=56
+        pack_ring,
+        [((NZ, ROWS_A, DIM), BF)],
+        [
+            ((TOK, width), BF),
+            ((TOK, width), BF),
+            ((16, width), BF),
+            (buckets.shape, jnp.int32),
+            pltpu.SemaphoreType.DMA((4,)),
+        ],
+        hbm_in=4,
     )(shared_qk, values, out_weight, buckets)
     got_a = exchange(msg, RINGS)
-    msg, slots = on_device(
+    slots, msg = on_device(
         route,
-        [((NG, ROWS_B, DIM), BF), ((16 + TOK, TOK), F32)],
-        [((NZ, SLOTS, 2 * DIM), BF)],
+        [((16 + TOK, TOK), F32), ((NG, ROWS_B, DIM), BF)],
+        [
+            ((16 + TOK, TOK), F32),
+            ((ROUNDS, NZ, SLOTS, 2 * DIM), BF),
+            ((NG, ROWS_B, DIM), BF),
+            pltpu.SemaphoreType.DMA((NG + 1,)),
+        ],
+        hbm_out=2,
     )(got_a)
     late_grad, msg = lax.optimization_barrier((out_grad, msg))
     got_b = exchange(msg, PLANES)
@@ -425,22 +503,35 @@
     before4 = pass_on(before3, 1)
     blocks = [late_grad, before1, before2, before3, before4, after3, after2, after1]
     (ring_grad,) = on_device(
-        join, [((NZ * TOK, width), BF)], [pltpu.SemaphoreType.DMA((NZ,))], hbm_in=NZ, hbm_out=1
+        join, [((NZ * TOK, width), BF)], [pltpu.SemaphoreType.DMA((NZ,))], hbm_in=NZ, hbm_out=1, pin=False
     )(*blocks)
-    msg, state, head_weight = on_device(
-        attend, [((NG, ROWS_C, DIM), BF), ((SLOTS + 32, TOK), F32), ((2 * width, DIM), BF)]
+    state, msg, head_weight = on_device(
+        attend,
+        [((SLOTS + 32, TOK), F32), ((NG, ROWS_C, DIM), BF), ((2 * width, DIM), BF)],
+        [((SLOTS + 32, TOK), F32), pltpu.SemaphoreType.DMA],
+        hbm_out=1,
     )(got_b)
     got_c = exchange(msg, PLANES)
     other_grad = swap_cores(ring_grad)
     own_part = lax.dynamic_slice_in_dim(head_weight, core * width, width, 0)
     other_part = lax.dynamic_slice_in_dim(head_weight, (1 - core) * width, width, 0)
     attended_grad = dot(ring_grad, own_part) + dot(other_grad, other_part)
-    msg, attended, turned = on_device(
+    turned, msg, attended = on_device(
         combine,
-        [((NG, ROWS_D, DIM), BF), ((NZ * TOK, DIM), BF), ((NZ * TOK, DIM), BF)],
-        [((ROUNDS, NZ, SLOTS, DIM), BF), ((ROUNDS, NZ, SLOTS, DIM), BF)],
+        [((NZ * TOK, DIM), BF), ((NG, ROWS_D, DIM), BF), ((NZ * TOK, DIM), BF)],
+        [
+            ((NZ, SLOTS, 2 * DIM), BF),
+            ((NZ, SLOTS, 2 * DIM), BF),
+            ((16 + TOK, TOK), F32),
+            ((16, width), BF),
+            ((NZ * TOK, DIM), BF),
+            ((NG, ROWS_D, DIM), BF),
+            pltpu.SemaphoreType.DMA((NZ + 2 + NG,)),
+        ],
         scalars=1,
-    )(z_place.reshape(1), got_c, slots, attended_grad, out_weight)
+        hbm_in=2,
+        hbm_out=2,
+    )(z_place.reshape(1), slots, out_weight, got_c, attended_grad)
     got_d = exchange(msg, PLANES)
     att_before1, att_after1 = ring_round(attended, attended)
     att_before2, att_after2 = ring_round(att_before1, att_after1)
@@ -450,9 +541,19 @@
         [jnp.where(core == 0, own_gw, other_gw), jnp.where(core == 0, other_gw, own_gw)], axis=0
     )
     got_d, att_before2, att_after2 = lax.optimization_barrier((got_d, att_before2, att_after2))
-    msg, mark = on_device(attend_back, [((NG, ROWS_E, DIM), BF), ((8, TOK), F32)])(
-        got_b, got_d, state, both_gw
-    )
+    state, att_before2, att_after2 = lax.optimization_barrier((state, att_before2, att_after2))
+    buckets_here = ROUNDS * BUCKETS
+    probability, probability_turned, _ = on_device(
+        recall,
+        [((buckets_here, SLOTS, SLOTS), F32), ((buckets_here, SLOTS, SLOTS), BF), ((8, TOK), F32)],
+        cost=(2 * buckets_here * SLOTS * SLOTS * DIM, 8 << 20, buckets_here * SLOTS * SLOTS),
+    )(got_b, state)
+    msg, mark = on_device(
+        attend_back,
+        [((NG, ROWS_E, DIM), BF), ((8, TOK), F32)],
+        [((NG, ROWS_C, DIM), BF), pltpu.SemaphoreType.DMA((3,))],
+        hbm_in=1,
+    )(got_d, got_b, probability, probability_turned, both_gw)
     got_e = exchange(msg, PLANES)
     late_before2, late_after2 = after((att_before2, att_after2), mark)
     att_before3, att_after3 = ring_round(late_before2, late_after2)
@@ -462,14 +563,28 @@
     own_rows, other_rows = on_device(
         project,
         [((NZ * TOK, DIM), F32), ((NZ * TOK, DIM), F32)],
-        [((NG, ROWS_D - ROW_PLANE, DIM), BF), pltpu.SemaphoreType.DMA],
+        [
+            ((NG, ROWS_D - ROW_PLANE, DIM), BF),
+            ((NZ * TOK, width), BF),
+            pltpu.SemaphoreType.DMA,
+            pltpu.SemaphoreType.DMA((NZ,)),
+        ],
         scalars=1,
-        hbm_in=1,
+        hbm_in=1 + NZ,
     )(jnp.stack([core, z_place]), got_d, *all_attended)
     other_rows = swap_cores(other_rows)
     (msg,) = on_device(
-        gather_home, [((NZ, ROWS_F, DIM), BF)], [((ROUNDS, NZ, SLOTS, 2 * DIM), BF)]
-    )(got_e, slots, own_rows, other_rows)
+        gather_home,
+        [((NZ, ROWS_F, DIM), BF)],
+        [
+            ((NZ, ROUNDS * SLOTS, 2 * DIM), BF),
+            ((16 + TOK, TOK), F32),
+            ((NZ * TOK, DIM), F32),
+            ((NZ * TOK, DIM), F32),
+            pltpu.SemaphoreType.DMA((3,)),
+        ],
+        hbm_in=3,
+    )(slots, own_rows, other_rows, got_e)
     got_f = exchange(msg, RINGS)
     grad_qk, grad_values, mixed, grad_weight = on_device(
         unpack_ring,

time: 213 us -> 208 us (0.977)
  local copies, waits for them, and re-layouts: 13.6 us -> 5.62 us
    unnamed x44 -> x36, local copies, waits for them, and re-layouts: 13.6 us -> 5.62 us
    pallas_call x9 -> x10, Pallas kernels: 29 us -> 30.6 us  [call(): pl.pallas_call(body, out_shape=shapes, in_specs=[pl.BlockSpec(memory_spac...]
  transfers between devices with their start and end apart: 20 -> 20, of which waited for: 14 -> 14; matrix products, arithmetic and copies ran while one was open for 4% -> 4% of each run, Pallas kernels for 4% -> 5%
where the time goes in v3:
time: 208 us
  waiting for transfers between devices  59.5 us (29%)
  blocking collectives  54.2 us (26%)
  starting transfers between devices  49.4 us (24%)
  Pallas kernels  30.6 us (15%)
  matrix products  7.37 us (4%)
  local copies, waits for them, and re-layouts  5.62 us (3%)
    all_to_all x2, blocking collectives, exchange(): lax.all_to_all(message, 'ctx', split_axis=0, concat_axis=0, tiled=True, a...  54.2 us
    ppermute x14, waiting for transfers between devices, pass_on(): return lax.ppermute(block, 'ctx', turn)  38 us
    pallas_call x10, Pallas kernels, call(): pl.pallas_call(body, out_shape=shapes, in_specs=[pl.BlockSpec(memory_spac...  30.6 us
    all_to_all x4, starting transfers between devices, exchange(): lax.all_to_all(message, 'ctx', split_axis=0, concat_axis=0, tiled=True, a...  29.2 us
    ppermute x14, starting transfers between devices, pass_on(): return lax.ppermute(block, 'ctx', turn)  20.1 us
    all_to_all x4, waiting for transfers between devices, exchange(): lax.all_to_all(message, 'ctx', split_axis=0, concat_axis=0, tiled=True, a...  19.6 us
    unnamed x36, local copies, waits for them, and re-layouts  5.62 us
  transfers between devices with their start and end apart: 20, of which 14 were waited for; matrix products, arithmetic and copies ran while one was open for 4% of the time, Pallas kernels for 5%

profile of v3, /device:TPU:18, one launch (start us, length us, event | category | flops | bytes accessed | tf_op | source)
XLA Modules:
  0.0 207.7 jit_solution(7412343488729184044)
XLA Ops:
  1.8 27.2 %all_to_all.30.a_ref = bf16[8,288,128]{2,1,0:T(8,128)(2,1)S(1)} all-to-all(bf16[8,288,128]{2,1,0:T(8,128)(2,1)S(1)} %shard_map.84), channel_id=1, replica_groups={{0,8,16,24,32,40,48,56},{2,10,18,26,34,42,50,58},{4,12,20,28,36,44,52,6..., dimensions={0} | all-to-all | bytes 1179648 | tf_op jit(solution)/shard_map/all_to_all | solution.py:445
  29.0 3.1 %shard_map.85 = (f32[144,128]{1,0:T(8,128)}, bf16[16,656,128]{2,1,0:T(8,128)(2,1)}) custom-call(bf16[8,288,128]{2,1,0:T(8,128)(2,1)S(1)} %all_to_all.30.a_ref), custom_call_target="tpu_custom_call" | custom-call | tf_op jit(solution)/shard_map/pallas_call | solution.py:427
  32.7 7.3 %all-to-all-start.1 = ((bf16[16,656,128]{2,1,0:T(8,128)(2,1)}), bf16[16,656,128]{2,1,0:T(8,128)(2,1)S(1)}, u32[]{:S(2)}, u32[]{:S(2)}) async-start(bf16[16,656,128]{2,1,0:T(8,128)(2,1)} %get-tuple-element.33), calls=%async_computation.1 | async-start | bytes 5373952 | tf_op jit(solution)/shard_map/all_to_all | solution.py:445
  40.0 2.7 %collective-permute-start.4 = (bf16[128,1024]{1,0:T(8,128)(2,1)S(1)}, bf16[128,1024]{1,0:T(8,128)(2,1)S(1)}, u32[]{:S(2)}, u32[]{:S(2)}) collective-permute-start(bf16[128,1024]{1,0:T(8,128)(2,1)S(1)} %copy-done.4), channel_id=1, source_target_pairs={{0,56},{2,58},{4,60},{6,62},{8,0},{10,2},{12,4},{14,6},{16,8},{18,... | collective-permute-start | bytes 786440 | tf_op jit(solution)/shard_map/ppermute | solution.py:458
  42.6 4.4 %collective-permute-done.4.refs_7_ = bf16[128,1024]{1,0:T(8,128)(2,1)S(1)} collective-permute-done((bf16[128,1024]{1,0:T(8,128)(2,1)S(1)}, bf16[128,1024]{1,0:T(8,128)(2,1)S(1)}, u32[]{:S(2)}, u32[]{:S(2)}) %collective-permute-start.4) | collective-permute-done | bytes 262176 | tf_op jit(solution)/shard_map/ppermute | solution.py:458
  47.1 3.1 %collective-permute-start.5 = (bf16[128,1024]{1,0:T(8,128)(2,1)S(1)}, bf16[128,1024]{1,0:T(8,128)(2,1)S(1)}, u32[]{:S(2)}, u32[]{:S(2)}) collective-permute-start(bf16[128,1024]{1,0:T(8,128)(2,1)S(1)} %collective-permute-done.4.refs_7_), channel_id=1, source_target_pairs={{0,56},{2,58},{4,60},{6,62},{8,0},{10,2},{12,4},{14,6},{16,8},{18,... | collective-permute-start | bytes 786440 | tf_op jit(solution)/shard_map/ppermute | solution.py:458
  50.2 4.7 %collective-permute-done.5.refs_6_ = bf16[128,1024]{1,0:T(8,128)(2,1)S(1)} collective-permute-done((bf16[128,1024]{1,0:T(8,128)(2,1)S(1)}, bf16[128,1024]{1,0:T(8,128)(2,1)S(1)}, u32[]{:S(2)}, u32[]{:S(2)}) %collective-permute-start.5) | collective-permute-done | bytes 262176 | tf_op jit(solution)/shard_map/ppermute | solution.py:458
  54.9 3.7 %collective-permute-start.6 = (bf16[128,1024]{1,0:T(8,128)(2,1)S(1)}, bf16[128,1024]{1,0:T(8,128)(2,1)S(1)}, u32[]{:S(2)}, u32[]{:S(2)}) collective-permute-start(bf16[128,1024]{1,0:T(8,128)(2,1)S(1)} %collective-permute-done.5.refs_6_), channel_id=1, source_target_pairs={{0,56},{2,58},{4,60},{6,62},{8,0},{10,2},{12,4},{14,6},{16,8},{18,... | collective-permute-start | bytes 786440 | tf_op jit(solution)/shard_map/ppermute | solution.py:458
  58.6 3.9 %collective-permute-done.6.refs_5_ = bf16[128,1024]{1,0:T(8,128)(2,1)S(1)} collective-permute-done((bf16[128,1024]{1,0:T(8,128)(2,1)S(1)}, bf16[128,1024]{1,0:T(8,128)(2,1)S(1)}, u32[]{:S(2)}, u32[]{:S(2)}) %collective-permute-start.6) | collective-permute-done | bytes 262176 | tf_op jit(solution)/shard_map/ppermute | solution.py:458
  62.5 3.7 %collective-permute-done.3.refs_4_ = bf16[128,1024]{1,0:T(8,128)(2,1)S(1)} collective-permute-done((bf16[128,1024]{1,0:T(8,128)(2,1)S(1)}, bf16[128,1024]{1,0:T(8,128)(2,1)S(1)}, u32[]{:S(2)}, u32[]{:S(2)}) %collective-permute-start.3) | collective-permute-done | bytes 262176 | tf_op jit(solution)/shard_map/ppermute | solution.py:458
  67.8 3.9 %all-to-all-done.1.b_ref = bf16[16,656,128]{2,1,0:T(8,128)(2,1)S(1)} async-done(((bf16[16,656,128]{2,1,0:T(8,128)(2,1)}), bf16[16,656,128]{2,1,0:T(8,128)(2,1)S(1)}, u32[]{:S(2)}, u32[]{:S(2)}) %all-to-all-start.1) | async-done | bytes 2687008 | tf_op jit(solution)/shard_map/all_to_all | solution.py:445
  71.7 4.4 %shard_map.86 = (f32[288,128]{1,0:T(8,128)}, bf16[16,272,128]{2,1,0:T(8,128)(2,1)S(1)}, bf16[2048,128]{1,0:T(8,128)(2,1)S(1)}) custom-call(bf16[16,656,128]{2,1,0:T(8,128)(2,1)S(1)} %all-to-all-done.1.b_ref), custom_call_target="tpu_custom_call" | custom-call | tf_op jit(solution)/shard_map/pallas_call | solution.py:427
  77.1 7.2 %all-to-all-start.2 = ((bf16[16,272,128]{2,1,0:T(8,128)(2,1)}), bf16[16,272,128]{2,1,0:T(8,128)(2,1)}, u32[]{:S(2)}, u32[]{:S(2)}) async-start(bf16[16,272,128]{2,1,0:T(8,128)(2,1)} %copy-done.1), calls=%async_computation.2 | async-start | bytes 2228224 | tf_op jit(solution)/shard_map/all_to_all | solution.py:445
  84.3 2.4 %fusion = f32[1024,128]{1,0:T(8,128)S(1)} fusion(bf16[1024,1024]{1,0:T(8,128)(2,1)} %collective-permute-done.7, bf16[2048,128]{1,0:T(8,128)(2,1)S(1)} %get-tuple-element.36, s32[]{:T(128)S(6)} %select_n.25), kind=kOutput, calls=%fused_computation.4 | convolution fusion | flops 268435456 | bytes 2883588 | tf_op jit(solution)/shard_map/dot_general | solution.py:53
  88.4 8.9 %all-to-all-done.2.c_ref = bf16[16,272,128]{2,1,0:T(8,128)(2,1)} async-done(((bf16[16,272,128]{2,1,0:T(8,128)(2,1)}), bf16[16,272,128]{2,1,0:T(8,128)(2,1)}, u32[]{:S(2)}, u32[]{:S(2)}) %all-to-all-start.2) | async-done | bytes 1114144 | tf_op jit(solution)/shard_map/all_to_all | solution.py:445
  97.3 7.2 %shard_map.88 = (bf16[1024,128]{1,0:T(8,128)(2,1)}, bf16[16,400,128]{2,1,0:T(8,128)(2,1)}, bf16[1024,128]{1,0:T(8,128)(2,1)S(1)}) custom-call(s32[1]{0:T(128)} %bitcast.1.z_ref, f32[144,128]{1,0:T(8,128)} %get-tuple-element.31.slot_in, bf16[16,1024]{1,0:T(8,128)(2,1)} %weight_in.1, bf16[16,272,128]{2,1,0:T(8,128)(2,1)} %all-to-all-done.2.c_ref, ...), custom_call_target="tpu_custom_call" | custom-call | tf_op jit(solution)/shard_map/pallas_call | solution.py:427
  104.6 7.2 %all-to-all-start.3 = ((bf16[16,400,128]{2,1,0:T(8,128)(2,1)}), bf16[16,400,128]{2,1,0:T(8,128)(2,1)}, u32[]{:S(2)}, u32[]{:S(2)}) async-start(bf16[16,400,128]{2,1,0:T(8,128)(2,1)} %get-tuple-element.37), calls=%async_computation.3 | async-start | bytes 3276800 | tf_op jit(solution)/shard_map/all_to_all | solution.py:445
  111.8 3.0 %collective-permute-start.10 = (bf16[1024,128]{1,0:T(8,128)(2,1)S(1)}, bf16[1024,128]{1,0:T(8,128)(2,1)S(1)}, u32[]{:S(2)}, u32[]{:S(2)}) collective-permute-start(bf16[1024,128]{1,0:T(8,128)(2,1)S(1)} %get-tuple-element.38.refs_0_), channel_id=1, source_target_pairs={{0,56},{2,58},{4,60},{6,62},{8,0},{10,2},{12,4},{14,6},{16,8},{18,... | collective-permute-start | bytes 786440 | tf_op jit(solution)/shard_map/ppermute | solution.py:458
  114.8 2.5 %convolution_convert_fusion = bf16[1024,128]{1,0:T(8,128)(2,1)S(1)} fusion(bf16[1024,1024]{1,0:T(8,128)(2,1)} %collective-permute-done.7, bf16[1024,128]{1,0:T(8,128)(2,1)S(1)} %copy-done.14), kind=kOutput, calls=%fused_computation.1 | convolution fusion | flops 268566528 | bytes 2621440 | tf_op jit(solution)/shard_map/dot_general | solution.py:61
  117.3 2.1 collective-permute-done.10.refs_7_
  119.3 3.7 %collective-permute-start.11 = (bf16[1024,128]{1,0:T(8,128)(2,1)S(1)}, bf16[1024,128]{1,0:T(8,128)(2,1)S(1)}, u32[]{:S(2)}, u32[]{:S(2)}) collective-permute-start(bf16[1024,128]{1,0:T(8,128)(2,1)S(1)} %collective-permute-done.10.refs_7_), channel_id=1, source_target_pairs={{0,56},{2,58},{4,60},{6,62},{8,0},{10,2},{12,4},{14,6},{16,8},{18,... | collective-permute-start | bytes 786440 | tf_op jit(solution)/shard_map/ppermute | solution.py:458
  123.9 3.0 %collective-permute-done.11.refs_6_ = bf16[1024,128]{1,0:T(8,128)(2,1)S(1)} collective-permute-done((bf16[1024,128]{1,0:T(8,128)(2,1)S(1)}, bf16[1024,128]{1,0:T(8,128)(2,1)S(1)}, u32[]{:S(2)}, u32[]{:S(2)}) %collective-permute-start.11) | collective-permute-done | bytes 262176 | tf_op jit(solution)/shard_map/ppermute | solution.py:458
  127.6 3.1 %collective-permute-done.9.refs_2_ = bf16[1024,128]{1,0:T(8,128)(2,1)} collective-permute-done((bf16[1024,128]{1,0:T(8,128)(2,1)S(1)}, bf16[1024,128]{1,0:T(8,128)(2,1)}, u32[]{:S(2)}, u32[]{:S(2)}) %collective-permute-start.9) | collective-permute-done | bytes 262176 | tf_op jit(solution)/shard_map/ppermute | solution.py:458
  131.9 2.0 shard_map.90
  134.0 5.0 %shard_map.91 = (bf16[16,640,128]{2,1,0:T(8,128)(2,1)S(1)}, f32[8,128]{1,0:T(8,128)}) custom-call(bf16[16,400,128]{2,1,0:T(8,128)(2,1)} %all-to-all-done.3.d_ref.d_in, bf16[16,656,128]{2,1,0:T(8,128)(2,1)S(1)} %all-to-all-done.1.b_ref, f32[16,256,256]{2,1,0:T(8,128)S(1)} %get-tuple-element.50.prob_ref, ...), custom_call_target="tpu_custom_call" | custom-call | tf_op jit(solution)/shard_map/pallas_call | solution.py:427
  140.5 7.5 %all-to-all-start.4 = ((bf16[16,640,128]{2,1,0:T(8,128)(2,1)}), bf16[16,640,128]{2,1,0:T(8,128)(2,1)S(1)}, u32[]{:S(2)}, u32[]{:S(2)}) async-start(bf16[16,640,128]{2,1,0:T(8,128)(2,1)} %copy-done), calls=%async_computation.4 | async-start | bytes 5242880 | tf_op jit(solution)/shard_map/all_to_all | solution.py:445
  148.2 3.1 %collective-permute-start.14 = (bf16[1024,128]{1,0:T(8,128)(2,1)S(1)}, bf16[1024,128]{1,0:T(8,128)(2,1)S(1)}, u32[]{:S(2)}, u32[]{:S(2)}) collective-permute-start(bf16[1024,128]{1,0:T(8,128)(2,1)S(1)} %copy-done.13), channel_id=1, source_target_pairs={{0,56},{2,58},{4,60},{6,62},{8,0},{10,2},{12,4},{14,6},{16,8},{18,... | collective-permute-start | bytes 786440 | tf_op jit(solution)/shard_map/ppermute | solution.py:458
  151.2 5.6 %collective-permute-done.12.refs_3_ = bf16[1024,128]{1,0:T(8,128)(2,1)S(1)} collective-permute-done((bf16[1024,128]{1,0:T(8,128)(2,1)}, bf16[1024,128]{1,0:T(8,128)(2,1)S(1)}, u32[]{:S(2)}, u32[]{:S(2)}) %collective-permute-start.12) | collective-permute-done | bytes 262176 | tf_op jit(solution)/shard_map/ppermute | solution.py:458
  156.9 7.5 %collective-permute-done.13.refs_4_ = bf16[1024,128]{1,0:T(8,128)(2,1)S(1)} collective-permute-done((bf16[1024,128]{1,0:T(8,128)(2,1)S(1)}, bf16[1024,128]{1,0:T(8,128)(2,1)S(1)}, u32[]{:S(2)}, u32[]{:S(2)}) %collective-permute-start.13) | collective-permute-done | bytes 262176 | tf_op jit(solution)/shard_map/ppermute | solution.py:458
  165.1 3.8 %shard_map.89 = (f32[1024,128]{1,0:T(8,128)S(1)}, f32[1024,128]{1,0:T(8,128)S(1)}) custom-call(s32[2]{0:T(128)S(1)} %pad_add_fusion.place_ref, bf16[16,400,128]{2,1,0:T(8,128)(2,1)} %all-to-all-done.3.d_ref.d_in, bf16[1024,128]{1,0:T(8,128)(2,1)} %copy-done.5, bf16[1024,128]{1,0:T(8,128)(2,1)} %copy-done.11, ...), custom_call_target="tpu_custom_call" | custom-call | tf_op jit(solution)/shard_map/pallas_call | solution.py:427
  171.6 6.5 %all-to-all-done.4.e_ref = bf16[16,640,128]{2,1,0:T(8,128)(2,1)S(1)} async-done(((bf16[16,640,128]{2,1,0:T(8,128)(2,1)}), bf16[16,640,128]{2,1,0:T(8,128)(2,1)S(1)}, u32[]{:S(2)}, u32[]{:S(2)}) %all-to-all-start.4) | async-done | bytes 2621472 | tf_op jit(solution)/shard_map/all_to_all | solution.py:445
  179.6 27.1 %all_to_all.31.f_ref = bf16[8,416,128]{2,1,0:T(8,128)(2,1)S(1)} all-to-all(bf16[8,416,128]{2,1,0:T(8,128)(2,1)S(1)} %shard_map.92), channel_id=1, replica_groups={{0,8,16,24,32,40,48,56},{2,10,18,26,34,42,50,58},{4,12,20,28,36,44,52,6..., dimensions={0} | all-to-all | bytes 1703936 | tf_op jit(solution)/shard_map/all_to_all | solution.py:445
  (62 shorter events, 16.4 us)
Async XLA Ops:
  0.6 31.4 %copy-start.4 = (bf16[128,1024]{1,0:T(8,128)(2,1)S(1)}, bf16[128,1024]{1,0:T(8,128)(2,1)}, u32[]{:S(2)}) copy-start(bf16[128,1024]{1,0:T(8,128)(2,1)} %refs_0_) | copy-start | bytes 786436
  32.1 10.6 %collective-permute-start = (bf16[128,1024]{1,0:T(8,128)(2,1)S(1)}, bf16[128,1024]{1,0:T(8,128)(2,1)S(1)}, u32[]{:S(2)}, u32[]{:S(2)}) collective-permute-start(bf16[128,1024]{1,0:T(8,128)(2,1)S(1)} %copy-done.4), channel_id=1, source_target_pairs={{0,8},{2,10},{4,12},{6,14},{8,16},{10,18},{12,20},{14,22},{16,24},... | collective-permute-start | bytes 786440 | tf_op jit(solution)/shard_map/ppermute | solution.py:458
  32.7 38.9 %all-to-all-start.1 = ((bf16[16,656,128]{2,1,0:T(8,128)(2,1)}), bf16[16,656,128]{2,1,0:T(8,128)(2,1)S(1)}, u32[]{:S(2)}, u32[]{:S(2)}) async-start(bf16[16,656,128]{2,1,0:T(8,128)(2,1)} %get-tuple-element.33), calls=%async_computation.1 | async-start | bytes 5373952 | tf_op jit(solution)/shard_map/all_to_all | solution.py:445
  40.0 7.1 %collective-permute-start.4 = (bf16[128,1024]{1,0:T(8,128)(2,1)S(1)}, bf16[128,1024]{1,0:T(8,128)(2,1)S(1)}, u32[]{:S(2)}, u32[]{:S(2)}) collective-permute-start(bf16[128,1024]{1,0:T(8,128)(2,1)S(1)} %copy-done.4), channel_id=1, source_target_pairs={{0,56},{2,58},{4,60},{6,62},{8,0},{10,2},{12,4},{14,6},{16,8},{18,... | collective-permute-start | bytes 786440 | tf_op jit(solution)/shard_map/ppermute | solution.py:458
  42.6 7.6 %collective-permute-start.1 = (bf16[128,1024]{1,0:T(8,128)(2,1)S(1)}, bf16[128,1024]{1,0:T(8,128)(2,1)S(1)}, u32[]{:S(2)}, u32[]{:S(2)}) collective-permute-start(bf16[128,1024]{1,0:T(8,128)(2,1)S(1)} %collective-permute-done.refs_1_), channel_id=1, source_target_pairs={{0,8},{2,10},{4,12},{6,14},{8,16},{10,18},{12,20},{14,22},{16,24},... | collective-permute-start | bytes 786440 | tf_op jit(solution)/shard_map/ppermute | solution.py:458
  47.1 7.8 %collective-permute-start.5 = (bf16[128,1024]{1,0:T(8,128)(2,1)S(1)}, bf16[128,1024]{1,0:T(8,128)(2,1)S(1)}, u32[]{:S(2)}, u32[]{:S(2)}) collective-permute-start(bf16[128,1024]{1,0:T(8,128)(2,1)S(1)} %collective-permute-done.4.refs_7_), channel_id=1, source_target_pairs={{0,56},{2,58},{4,60},{6,62},{8,0},{10,2},{12,4},{14,6},{16,8},{18,... | collective-permute-start | bytes 786440 | tf_op jit(solution)/shard_map/ppermute | solution.py:458
  50.2 8.4 %collective-permute-start.2 = (bf16[128,1024]{1,0:T(8,128)(2,1)S(1)}, bf16[128,1024]{1,0:T(8,128)(2,1)S(1)}, u32[]{:S(2)}, u32[]{:S(2)}) collective-permute-start(bf16[128,1024]{1,0:T(8,128)(2,1)S(1)} %collective-permute-done.1.refs_2_), channel_id=1, source_target_pairs={{0,8},{2,10},{4,12},{6,14},{8,16},{10,18},{12,20},{14,22},{16,24},... | collective-permute-start | bytes 786440 | tf_op jit(solution)/shard_map/ppermute | solution.py:458
  54.9 7.6 %collective-permute-start.6 = (bf16[128,1024]{1,0:T(8,128)(2,1)S(1)}, bf16[128,1024]{1,0:T(8,128)(2,1)S(1)}, u32[]{:S(2)}, u32[]{:S(2)}) collective-permute-start(bf16[128,1024]{1,0:T(8,128)(2,1)S(1)} %collective-permute-done.5.refs_6_), channel_id=1, source_target_pairs={{0,56},{2,58},{4,60},{6,62},{8,0},{10,2},{12,4},{14,6},{16,8},{18,... | collective-permute-start | bytes 786440 | tf_op jit(solution)/shard_map/ppermute | solution.py:458
  58.6 7.6 %collective-permute-start.3 = (bf16[128,1024]{1,0:T(8,128)(2,1)S(1)}, bf16[128,1024]{1,0:T(8,128)(2,1)S(1)}, u32[]{:S(2)}, u32[]{:S(2)}) collective-permute-start(bf16[128,1024]{1,0:T(8,128)(2,1)S(1)} %collective-permute-done.2.refs_3_), channel_id=1, source_target_pairs={{0,8},{2,10},{4,12},{6,14},{8,16},{10,18},{12,20},{14,22},{16,24},... | collective-permute-start | bytes 786440 | tf_op jit(solution)/shard_map/ppermute | solution.py:458
  67.7 16.6 %collective-permute-start.7 = (bf16[1024,1024]{1,0:T(8,128)(2,1)}, bf16[1024,1024]{1,0:T(8,128)(2,1)}, u32[]{:S(2)}, u32[]{:S(2)}) collective-permute-start(bf16[1024,1024]{1,0:T(8,128)(2,1)} %shard_map.87), channel_id=1, source_target_pairs={{0,1},{1,0},{2,3},{3,2},{4,5},{5,4},{6,7},{7,6},{8,9},{9,8},{10,11... | collective-permute-start | bytes 6291464 | tf_op jit(solution)/shard_map/ppermute | solution.py:451
  77.1 7.2 %copy-start.2 = (bf16[2048,128]{1,0:T(8,128)(2,1)}, bf16[2048,128]{1,0:T(8,128)(2,1)S(1)}, u32[]{:S(2)}) copy-start(bf16[2048,128]{1,0:T(8,128)(2,1)S(1)} %get-tuple-element.36) | copy-start | bytes 1572868
  77.1 20.2 %all-to-all-start.2 = ((bf16[16,272,128]{2,1,0:T(8,128)(2,1)}), bf16[16,272,128]{2,1,0:T(8,128)(2,1)}, u32[]{:S(2)}, u32[]{:S(2)}) async-start(bf16[16,272,128]{2,1,0:T(8,128)(2,1)} %copy-done.1), calls=%async_computation.2 | async-start | bytes 2228224 | tf_op jit(solution)/shard_map/all_to_all | solution.py:445
  84.3 2.5 %copy-start.7 = (bf16[1024,1024]{1,0:T(8,128)(2,1)S(1)}, bf16[1024,1024]{1,0:T(8,128)(2,1)}, u32[]{:S(2)}) copy-start(bf16[1024,1024]{1,0:T(8,128)(2,1)} %shard_map.87) | copy-start | bytes 6291460
  104.5 12.7 %copy-start.5 = (bf16[1024,128]{1,0:T(8,128)(2,1)}, bf16[1024,128]{1,0:T(8,128)(2,1)S(1)}, u32[]{:S(2)}) copy-start(bf16[1024,128]{1,0:T(8,128)(2,1)S(1)} %get-tuple-element.38.refs_0_) | copy-start | bytes 786436
  104.5 10.2 %copy-start.14 = (bf16[1024,128]{1,0:T(8,128)(2,1)S(1)}, bf16[1024,128]{1,0:T(8,128)(2,1)}, u32[]{:S(2)}) copy-start(bf16[1024,128]{1,0:T(8,128)(2,1)} %get-tuple-element.52) | copy-start | bytes 786436
  104.6 26.4 %all-to-all-start.3 = ((bf16[16,400,128]{2,1,0:T(8,128)(2,1)}), bf16[16,400,128]{2,1,0:T(8,128)(2,1)}, u32[]{:S(2)}, u32[]{:S(2)}) async-start(bf16[16,400,128]{2,1,0:T(8,128)(2,1)} %get-tuple-element.37), calls=%async_computation.3 | async-start | bytes 3276800 | tf_op jit(solution)/shard_map/all_to_all | solution.py:445
  111.8 7.6 %collective-permute-start.10 = (bf16[1024,128]{1,0:T(8,128)(2,1)S(1)}, bf16[1024,128]{1,0:T(8,128)(2,1)S(1)}, u32[]{:S(2)}, u32[]{:S(2)}) collective-permute-start(bf16[1024,128]{1,0:T(8,128)(2,1)S(1)} %get-tuple-element.38.refs_0_), channel_id=1, source_target_pairs={{0,56},{2,58},{4,60},{6,62},{8,0},{10,2},{12,4},{14,6},{16,8},{18,... | collective-permute-start | bytes 786440 | tf_op jit(solution)/shard_map/ppermute | solution.py:458
  114.8 8.3 %collective-permute-start.8 = (bf16[1024,128]{1,0:T(8,128)(2,1)S(1)}, bf16[1024,128]{1,0:T(8,128)(2,1)S(1)}, u32[]{:S(2)}, u32[]{:S(2)}) collective-permute-start(bf16[1024,128]{1,0:T(8,128)(2,1)S(1)} %get-tuple-element.38.refs_0_), channel_id=1, source_target_pairs={{0,8},{2,10},{4,12},{6,14},{8,16},{10,18},{12,20},{14,22},{16,24},... | collective-permute-start | bytes 786440 | tf_op jit(solution)/shard_map/ppermute | solution.py:458
  114.8 8.3 %copy-start.8 = (bf16[1024,1024]{1,0:T(8,128)(2,1)S(1)}, bf16[1024,1024]{1,0:T(8,128)(2,1)}, u32[]{:S(2)}) copy-start(bf16[1024,1024]{1,0:T(8,128)(2,1)} %shard_map.87) | copy-start | bytes 6291460
  119.3 4.5 %copy-start.10 = (bf16[1024,128]{1,0:T(8,128)(2,1)}, bf16[1024,128]{1,0:T(8,128)(2,1)S(1)}, u32[]{:S(2)}) copy-start(bf16[1024,128]{1,0:T(8,128)(2,1)S(1)} %collective-permute-done.10.refs_7_) | copy-start | bytes 786436
  119.3 7.6 %collective-permute-start.11 = (bf16[1024,128]{1,0:T(8,128)(2,1)S(1)}, bf16[1024,128]{1,0:T(8,128)(2,1)S(1)}, u32[]{:S(2)}, u32[]{:S(2)}) collective-permute-start(bf16[1024,128]{1,0:T(8,128)(2,1)S(1)} %collective-permute-done.10.refs_7_), channel_id=1, source_target_pairs={{0,56},{2,58},{4,60},{6,62},{8,0},{10,2},{12,4},{14,6},{16,8},{18,... | collective-permute-start | bytes 786440 | tf_op jit(solution)/shard_map/ppermute | solution.py:458
  123.0 7.7 %collective-permute-start.9 = (bf16[1024,128]{1,0:T(8,128)(2,1)S(1)}, bf16[1024,128]{1,0:T(8,128)(2,1)}, u32[]{:S(2)}, u32[]{:S(2)}) collective-permute-start(bf16[1024,128]{1,0:T(8,128)(2,1)S(1)} %collective-permute-done.8.refs_1_), channel_id=1, source_target_pairs={{0,8},{2,10},{4,12},{6,14},{8,16},{10,18},{12,20},{14,22},{16,24},... | collective-permute-start | bytes 786440 | tf_op jit(solution)/shard_map/ppermute | solution.py:458
  139.0 1.5 copy-start
  140.5 7.7 %copy-start.13 = (bf16[1024,128]{1,0:T(8,128)(2,1)S(1)}, bf16[1024,128]{1,0:T(8,128)(2,1)}, u32[]{:S(2)}) copy-start(bf16[1024,128]{1,0:T(8,128)(2,1)} %copy-done.12) | copy-start | bytes 786436
  140.5 37.6 %all-to-all-start.4 = ((bf16[16,640,128]{2,1,0:T(8,128)(2,1)}), bf16[16,640,128]{2,1,0:T(8,128)(2,1)S(1)}, u32[]{:S(2)}, u32[]{:S(2)}) async-start(bf16[16,640,128]{2,1,0:T(8,128)(2,1)} %copy-done), calls=%async_computation.4 | async-start | bytes 5242880 | tf_op jit(solution)/shard_map/all_to_all | solution.py:445
  148.0 8.8 %collective-permute-start.12 = (bf16[1024,128]{1,0:T(8,128)(2,1)}, bf16[1024,128]{1,0:T(8,128)(2,1)S(1)}, u32[]{:S(2)}, u32[]{:S(2)}) collective-permute-start(bf16[1024,128]{1,0:T(8,128)(2,1)} %collective-permute-done.9.refs_2_), channel_id=1, source_target_pairs={{0,8},{2,10},{4,12},{6,14},{8,16},{10,18},{12,20},{14,22},{16,24},... | collective-permute-start | bytes 786440 | tf_op jit(solution)/shard_map/ppermute | solution.py:458
  148.2 8.8 %collective-permute-start.14 = (bf16[1024,128]{1,0:T(8,128)(2,1)S(1)}, bf16[1024,128]{1,0:T(8,128)(2,1)S(1)}, u32[]{:S(2)}, u32[]{:S(2)}) collective-permute-start(bf16[1024,128]{1,0:T(8,128)(2,1)S(1)} %copy-done.13), channel_id=1, source_target_pairs={{0,56},{2,58},{4,60},{6,62},{8,0},{10,2},{12,4},{14,6},{16,8},{18,... | collective-permute-start | bytes 786440 | tf_op jit(solution)/shard_map/ppermute | solution.py:458
  156.8 7.6 %copy-start.15 = (bf16[1024,128]{1,0:T(8,128)(2,1)}, bf16[1024,128]{1,0:T(8,128)(2,1)S(1)}, u32[]{:S(2)}) copy-start(bf16[1024,128]{1,0:T(8,128)(2,1)S(1)} %collective-permute-done.12.refs_3_) | copy-start | bytes 786436
  156.8 7.6 %collective-permute-start.13 = (bf16[1024,128]{1,0:T(8,128)(2,1)S(1)}, bf16[1024,128]{1,0:T(8,128)(2,1)S(1)}, u32[]{:S(2)}, u32[]{:S(2)}) collective-permute-start(bf16[1024,128]{1,0:T(8,128)(2,1)S(1)} %collective-permute-done.12.refs_3_), channel_id=1, source_target_pairs={{0,8},{2,10},{4,12},{6,14},{8,16},{10,18},{12,20},{14,22},{16,24},... | collective-permute-start | bytes 786440 | tf_op jit(solution)/shard_map/ppermute | solution.py:458
  156.9 7.5 %copy-start.16 = (bf16[1024,128]{1,0:T(8,128)(2,1)}, bf16[1024,128]{1,0:T(8,128)(2,1)S(1)}, u32[]{:S(2)}) copy-start(bf16[1024,128]{1,0:T(8,128)(2,1)S(1)} %collective-permute-done.14.refs_5_) | copy-start | bytes 786436
  169.7 1.9 collective-permute-start.15
  171.6 6.5 %copy-start.9 = (f32[1024,128]{1,0:T(8,128)}, f32[1024,128]{1,0:T(8,128)S(1)}, u32[]{:S(2)}) copy-start(f32[1024,128]{1,0:T(8,128)S(1)} %collective-permute-done.15.other_in) | copy-start | bytes 1572868
  (6 other events, 4.9 us)

commit v4 on v3

--- a/solution.py
+++ b/solution.py
@@ -534,14 +534,13 @@
     )(z_place.reshape(1), slots, out_weight, got_c, attended_grad)
     got_d = exchange(msg, PLANES)
     att_before1, att_after1 = ring_round(attended, attended)
-    att_before2, att_after2 = ring_round(att_before1, att_after1)
     own_gw = dot_tn(ring_grad, turned).astype(BF)
     other_gw = dot_tn(other_grad, turned).astype(BF)
     both_gw = jnp.concatenate(
         [jnp.where(core == 0, own_gw, other_gw), jnp.where(core == 0, other_gw, own_gw)], axis=0
     )
-    got_d, att_before2, att_after2 = lax.optimization_barrier((got_d, att_before2, att_after2))
-    state, att_before2, att_after2 = lax.optimization_barrier((state, att_before2, att_after2))
+    got_d, att_before1, att_after1 = lax.optimization_barrier((got_d, att_before1, att_after1))
+    state, att_before1, att_after1 = lax.optimization_barrier((state, att_before1, att_after1))
     buckets_here = ROUNDS * BUCKETS
     probability, probability_turned, _ = on_device(
         recall,
@@ -555,8 +554,9 @@
         hbm_in=1,
     )(got_d, got_b, probability, probability_turned, both_gw)
     got_e = exchange(msg, PLANES)
-    late_before2, late_after2 = after((att_before2, att_after2), mark)
-    att_before3, att_after3 = ring_round(late_before2, late_after2)
+    late_before1, late_after1 = after((att_before1, att_after1), mark)
+    att_before2, att_after2 = ring_round(late_before1, late_after1)
+    att_before3, att_after3 = ring_round(att_before2, att_after2)
     att_before4 = pass_on(att_before3, 1)
     all_attended = [attended, att_before1, att_before2, att_before3, att_before4]
     all_attended += [att_after3, att_after2, att_after1]

time: 208 us -> 213 us (1.024)
  waiting for transfers between devices: 59.5 us -> 62.2 us
    all_to_all x4, waiting for transfers between devices: 19.6 us -> 23.7 us  [exchange(): lax.all_to_all(message, 'ctx', split_axis=0, concat_axis=0, tiled=True, a...]
  transfers between devices with their start and end apart: 20 -> 20, of which waited for: 14 -> 13; matrix products, arithmetic and copies ran while one was open for 4% -> 4% of each run, Pallas kernels for 5% -> 5%
where the time goes in v4:
time: 213 us; the launch traced here: 212 us
  waiting for transfers between devices  62.2 us (29%)
  blocking collectives  54.6 us (26%)
  starting transfers between devices  49.6 us (23%)
  Pallas kernels  30.6 us (14%)
  matrix products  7.37 us (3%)
  local copies, waits for them, and re-layouts  6.38 us (3%)
    all_to_all x2, blocking collectives, exchange(): lax.all_to_all(message, 'ctx', split_axis=0, concat_axis=0, tiled=True, a...  54.6 us
    ppermute x14, waiting for transfers between devices, pass_on(): return lax.ppermute(block, 'ctx', turn)  36.5 us
    pallas_call x10, Pallas kernels, call(): pl.pallas_call(body, out_shape=shapes, in_specs=[pl.BlockSpec(memory_spac...  30.6 us
    all_to_all x4, starting transfers between devices, exchange(): lax.all_to_all(message, 'ctx', split_axis=0, concat_axis=0, tiled=True, a...  29.2 us
    all_to_all x4, waiting for transfers between devices, exchange(): lax.all_to_all(message, 'ctx', split_axis=0, concat_axis=0, tiled=True, a...  23.7 us
    ppermute x14, starting transfers between devices, pass_on(): return lax.ppermute(block, 'ctx', turn)  20.3 us
    unnamed x36, local copies, waits for them, and re-layouts  6.38 us
  transfers between devices with their start and end apart: 20, of which 13 were waited for; matrix products, arithmetic and copies ran while one was open for 4% of the time, Pallas kernels for 5%

profile of v4, /device:TPU:18, one launch (start us, length us, event | category | flops | bytes accessed | tf_op | source)
XLA Modules:
  0.0 211.8 jit_solution(17119478574147085349)
XLA Ops:
  1.8 27.2 %all_to_all.30.a_ref = bf16[8,288,128]{2,1,0:T(8,128)(2,1)S(1)} all-to-all(bf16[8,288,128]{2,1,0:T(8,128)(2,1)S(1)} %shard_map.84), channel_id=1, replica_groups={{0,8,16,24,32,40,48,56},{2,10,18,26,34,42,50,58},{4,12,20,28,36,44,52,6..., dimensions={0} | all-to-all | bytes 1179648 | tf_op jit(solution)/shard_map/all_to_all | solution.py:445
  29.0 3.1 %shard_map.85 = (f32[144,128]{1,0:T(8,128)}, bf16[16,656,128]{2,1,0:T(8,128)(2,1)}) custom-call(bf16[8,288,128]{2,1,0:T(8,128)(2,1)S(1)} %all_to_all.30.a_ref), custom_call_target="tpu_custom_call" | custom-call | tf_op jit(solution)/shard_map/pallas_call | solution.py:427
  32.7 7.3 %all-to-all-start.1 = ((bf16[16,656,128]{2,1,0:T(8,128)(2,1)}), bf16[16,656,128]{2,1,0:T(8,128)(2,1)S(1)}, u32[]{:S(2)}, u32[]{:S(2)}) async-start(bf16[16,656,128]{2,1,0:T(8,128)(2,1)} %get-tuple-element.33), calls=%async_computation.1 | async-start | bytes 5373952 | tf_op jit(solution)/shard_map/all_to_all | solution.py:445
  40.0 2.7 %collective-permute-start.4 = (bf16[128,1024]{1,0:T(8,128)(2,1)S(1)}, bf16[128,1024]{1,0:T(8,128)(2,1)S(1)}, u32[]{:S(2)}, u32[]{:S(2)}) collective-permute-start(bf16[128,1024]{1,0:T(8,128)(2,1)S(1)} %copy-done.4), channel_id=1, source_target_pairs={{0,56},{2,58},{4,60},{6,62},{8,0},{10,2},{12,4},{14,6},{16,8},{18,... | collective-permute-start | bytes 786440 | tf_op jit(solution)/shard_map/ppermute | solution.py:458
  42.6 4.4 %collective-permute-done.4.refs_7_ = bf16[128,1024]{1,0:T(8,128)(2,1)S(1)} collective-permute-done((bf16[128,1024]{1,0:T(8,128)(2,1)S(1)}, bf16[128,1024]{1,0:T(8,128)(2,1)S(1)}, u32[]{:S(2)}, u32[]{:S(2)}) %collective-permute-start.4) | collective-permute-done | bytes 262176 | tf_op jit(solution)/shard_map/ppermute | solution.py:458
  47.1 3.1 %collective-permute-start.5 = (bf16[128,1024]{1,0:T(8,128)(2,1)S(1)}, bf16[128,1024]{1,0:T(8,128)(2,1)S(1)}, u32[]{:S(2)}, u32[]{:S(2)}) collective-permute-start(bf16[128,1024]{1,0:T(8,128)(2,1)S(1)} %collective-permute-done.4.refs_7_), channel_id=1, source_target_pairs={{0,56},{2,58},{4,60},{6,62},{8,0},{10,2},{12,4},{14,6},{16,8},{18,... | collective-permute-start | bytes 786440 | tf_op jit(solution)/shard_map/ppermute | solution.py:458
  50.3 4.7 %collective-permute-done.5.refs_6_ = bf16[128,1024]{1,0:T(8,128)(2,1)S(1)} collective-permute-done((bf16[128,1024]{1,0:T(8,128)(2,1)S(1)}, bf16[128,1024]{1,0:T(8,128)(2,1)S(1)}, u32[]{:S(2)}, u32[]{:S(2)}) %collective-permute-start.5) | collective-permute-done | bytes 262176 | tf_op jit(solution)/shard_map/ppermute | solution.py:458
  54.9 3.7 %collective-permute-start.6 = (bf16[128,1024]{1,0:T(8,128)(2,1)S(1)}, bf16[128,1024]{1,0:T(8,128)(2,1)S(1)}, u32[]{:S(2)}, u32[]{:S(2)}) collective-permute-start(bf16[128,1024]{1,0:T(8,128)(2,1)S(1)} %collective-permute-done.5.refs_6_), channel_id=1, source_target_pairs={{0,56},{2,58},{4,60},{6,62},{8,0},{10,2},{12,4},{14,6},{16,8},{18,... | collective-permute-start | bytes 786440 | tf_op jit(solution)/shard_map/ppermute | solution.py:458
  58.6 3.9 %collective-permute-done.6.refs_5_ = bf16[128,1024]{1,0:T(8,128)(2,1)S(1)} collective-permute-done((bf16[128,1024]{1,0:T(8,128)(2,1)S(1)}, bf16[128,1024]{1,0:T(8,128)(2,1)S(1)}, u32[]{:S(2)}, u32[]{:S(2)}) %collective-permute-start.6) | collective-permute-done | bytes 262176 | tf_op jit(solution)/shard_map/ppermute | solution.py:458
  62.5 3.7 %collective-permute-done.3.refs_4_ = bf16[128,1024]{1,0:T(8,128)(2,1)S(1)} collective-permute-done((bf16[128,1024]{1,0:T(8,128)(2,1)S(1)}, bf16[128,1024]{1,0:T(8,128)(2,1)S(1)}, u32[]{:S(2)}, u32[]{:S(2)}) %collective-permute-start.3) | collective-permute-done | bytes 262176 | tf_op jit(solution)/shard_map/ppermute | solution.py:458
  67.7 3.9 %all-to-all-done.1.b_ref = bf16[16,656,128]{2,1,0:T(8,128)(2,1)S(1)} async-done(((bf16[16,656,128]{2,1,0:T(8,128)(2,1)}), bf16[16,656,128]{2,1,0:T(8,128)(2,1)S(1)}, u32[]{:S(2)}, u32[]{:S(2)}) %all-to-all-start.1) | async-done | bytes 2687008 | tf_op jit(solution)/shard_map/all_to_all | solution.py:445
  71.7 4.4 %shard_map.86 = (f32[288,128]{1,0:T(8,128)}, bf16[16,272,128]{2,1,0:T(8,128)(2,1)S(1)}, bf16[2048,128]{1,0:T(8,128)(2,1)S(1)}) custom-call(bf16[16,656,128]{2,1,0:T(8,128)(2,1)S(1)} %all-to-all-done.1.b_ref), custom_call_target="tpu_custom_call" | custom-call | tf_op jit(solution)/shard_map/pallas_call | solution.py:427
  77.1 7.2 %all-to-all-start.2 = ((bf16[16,272,128]{2,1,0:T(8,128)(2,1)}), bf16[16,272,128]{2,1,0:T(8,128)(2,1)}, u32[]{:S(2)}, u32[]{:S(2)}) async-start(bf16[16,272,128]{2,1,0:T(8,128)(2,1)} %copy-done.1), calls=%async_computation.2 | async-start | bytes 2228224 | tf_op jit(solution)/shard_map/all_to_all | solution.py:445
  84.3 2.4 %fusion = f32[1024,128]{1,0:T(8,128)S(1)} fusion(bf16[1024,1024]{1,0:T(8,128)(2,1)} %collective-permute-done.7, bf16[2048,128]{1,0:T(8,128)(2,1)S(1)} %get-tuple-element.36, s32[]{:T(128)S(6)} %select_n.25), kind=kOutput, calls=%fused_computation.4 | convolution fusion | flops 268435456 | bytes 2883588 | tf_op jit(solution)/shard_map/dot_general | solution.py:53
  86.7 1.7 convolution_add_fusion.grad_ref
  88.4 8.9 %all-to-all-done.2.c_ref = bf16[16,272,128]{2,1,0:T(8,128)(2,1)} async-done(((bf16[16,272,128]{2,1,0:T(8,128)(2,1)}), bf16[16,272,128]{2,1,0:T(8,128)(2,1)}, u32[]{:S(2)}, u32[]{:S(2)}) %all-to-all-start.2) | async-done | bytes 1114144 | tf_op jit(solution)/shard_map/all_to_all | solution.py:445
  97.3 7.2 %shard_map.88 = (bf16[1024,128]{1,0:T(8,128)(2,1)}, bf16[16,400,128]{2,1,0:T(8,128)(2,1)}, bf16[1024,128]{1,0:T(8,128)(2,1)S(1)}) custom-call(s32[1]{0:T(128)} %bitcast.1.z_ref, f32[144,128]{1,0:T(8,128)} %get-tuple-element.31.slot_in, bf16[16,1024]{1,0:T(8,128)(2,1)} %weight_in.1, bf16[16,272,128]{2,1,0:T(8,128)(2,1)} %all-to-all-done.2.c_ref, ...), custom_call_target="tpu_custom_call" | custom-call | tf_op jit(solution)/shard_map/pallas_call | solution.py:427
  104.5 7.2 %all-to-all-start.3 = ((bf16[16,400,128]{2,1,0:T(8,128)(2,1)}), bf16[16,400,128]{2,1,0:T(8,128)(2,1)}, u32[]{:S(2)}, u32[]{:S(2)}) async-start(bf16[16,400,128]{2,1,0:T(8,128)(2,1)} %get-tuple-element.37), calls=%async_computation.3 | async-start | bytes 3276800 | tf_op jit(solution)/shard_map/all_to_all | solution.py:445
  112.2 2.8 %collective-permute-start.9 = (bf16[1024,128]{1,0:T(8,128)(2,1)S(1)}, bf16[1024,128]{1,0:T(8,128)(2,1)}, u32[]{:S(2)}, u32[]{:S(2)}) collective-permute-start(bf16[1024,128]{1,0:T(8,128)(2,1)S(1)} %get-tuple-element.38.refs_0_), channel_id=1, source_target_pairs={{0,56},{2,58},{4,60},{6,62},{8,0},{10,2},{12,4},{14,6},{16,8},{18,... | collective-permute-start | bytes 786440 | tf_op jit(solution)/shard_map/ppermute | solution.py:458
  115.0 2.5 %convolution_convert_fusion = bf16[1024,128]{1,0:T(8,128)(2,1)S(1)} fusion(bf16[1024,1024]{1,0:T(8,128)(2,1)} %collective-permute-done.7, bf16[1024,128]{1,0:T(8,128)(2,1)S(1)} %copy-done.15), kind=kOutput, calls=%fused_computation.1 | convolution fusion | flops 268566528 | bytes 2621440 | tf_op jit(solution)/shard_map/dot_general | solution.py:61
  120.1 10.9 %all-to-all-done.3.d_ref.d_in = bf16[16,400,128]{2,1,0:T(8,128)(2,1)} async-done(((bf16[16,400,128]{2,1,0:T(8,128)(2,1)}), bf16[16,400,128]{2,1,0:T(8,128)(2,1)}, u32[]{:S(2)}, u32[]{:S(2)}) %all-to-all-start.3) | async-done | bytes 1638432 | tf_op jit(solution)/shard_map/all_to_all | solution.py:445
  131.9 2.0 shard_map.90
  133.9 5.0 %shard_map.91 = (bf16[16,640,128]{2,1,0:T(8,128)(2,1)S(1)}, f32[8,128]{1,0:T(8,128)}) custom-call(bf16[16,400,128]{2,1,0:T(8,128)(2,1)} %all-to-all-done.3.d_ref.d_in, bf16[16,656,128]{2,1,0:T(8,128)(2,1)S(1)} %all-to-all-done.1.b_ref, f32[16,256,256]{2,1,0:T(8,128)S(1)} %get-tuple-element.50.prob_ref, ...), custom_call_target="tpu_custom_call" | custom-call | tf_op jit(solution)/shard_map/pallas_call | solution.py:427
  140.4 7.6 %all-to-all-start.4 = ((bf16[16,640,128]{2,1,0:T(8,128)(2,1)}), bf16[16,640,128]{2,1,0:T(8,128)(2,1)S(1)}, u32[]{:S(2)}, u32[]{:S(2)}) async-start(bf16[16,640,128]{2,1,0:T(8,128)(2,1)} %copy-done), calls=%async_computation.4 | async-start | bytes 5242880 | tf_op jit(solution)/shard_map/all_to_all | solution.py:445
  148.1 3.2 %collective-permute-start.13 = (bf16[1024,128]{1,0:T(8,128)(2,1)}, bf16[1024,128]{1,0:T(8,128)(2,1)S(1)}, u32[]{:S(2)}, u32[]{:S(2)}) collective-permute-start(bf16[1024,128]{1,0:T(8,128)(2,1)} %collective-permute-done.9.refs_7_), channel_id=1, source_target_pairs={{0,56},{2,58},{4,60},{6,62},{8,0},{10,2},{12,4},{14,6},{16,8},{18,... | collective-permute-start | bytes 786440 | tf_op jit(solution)/shard_map/ppermute | solution.py:458
  151.3 5.4 %collective-permute-done.10.refs_2_ = bf16[1024,128]{1,0:T(8,128)(2,1)S(1)} collective-permute-done((bf16[1024,128]{1,0:T(8,128)(2,1)S(1)}, bf16[1024,128]{1,0:T(8,128)(2,1)S(1)}, u32[]{:S(2)}, u32[]{:S(2)}) %collective-permute-start.10) | collective-permute-done | bytes 262176 | tf_op jit(solution)/shard_map/ppermute | solution.py:458
  156.8 3.6 %collective-permute-start.14 = (bf16[1024,128]{1,0:T(8,128)(2,1)S(1)}, bf16[1024,128]{1,0:T(8,128)(2,1)S(1)}, u32[]{:S(2)}, u32[]{:S(2)}) collective-permute-start(bf16[1024,128]{1,0:T(8,128)(2,1)S(1)} %collective-permute-done.13.refs_6_), channel_id=1, source_target_pairs={{0,56},{2,58},{4,60},{6,62},{8,0},{10,2},{12,4},{14,6},{16,8},{18,... | collective-permute-start | bytes 786440 | tf_op jit(solution)/shard_map/ppermute | solution.py:458
  160.4 5.8 %collective-permute-done.11.refs_3_ = bf16[1024,128]{1,0:T(8,128)(2,1)S(1)} collective-permute-done((bf16[1024,128]{1,0:T(8,128)(2,1)S(1)}, bf16[1024,128]{1,0:T(8,128)(2,1)S(1)}, u32[]{:S(2)}, u32[]{:S(2)}) %collective-permute-start.11) | collective-permute-done | bytes 262176 | tf_op jit(solution)/shard_map/ppermute | solution.py:458
  166.3 7.5 %collective-permute-done.12.refs_4_ = bf16[1024,128]{1,0:T(8,128)(2,1)S(1)} collective-permute-done((bf16[1024,128]{1,0:T(8,128)(2,1)S(1)}, bf16[1024,128]{1,0:T(8,128)(2,1)S(1)}, u32[]{:S(2)}, u32[]{:S(2)}) %collective-permute-start.12) | collective-permute-done | bytes 262176 | tf_op jit(solution)/shard_map/ppermute | solution.py:458
  174.5 3.8 %shard_map.89 = (f32[1024,128]{1,0:T(8,128)S(1)}, f32[1024,128]{1,0:T(8,128)S(1)}) custom-call(s32[2]{0:T(128)S(1)} %pad_add_fusion.place_ref, bf16[16,400,128]{2,1,0:T(8,128)(2,1)} %all-to-all-done.3.d_ref.d_in, bf16[1024,128]{1,0:T(8,128)(2,1)} %copy-done.5, bf16[1024,128]{1,0:T(8,128)(2,1)} %copy-done.10, bf16[1024,128]{1,0:T(8,128)(2,1)} %copy-done.12, ...), custom_call_target="tpu_custom_call" | custom-call | tf_op jit(solution)/shard_map/pallas_call | solution.py:427
  179.0 1.9 collective-permute-done.15.other_in
  183.3 27.5 %all_to_all.31.f_ref = bf16[8,416,128]{2,1,0:T(8,128)(2,1)S(1)} all-to-all(bf16[8,416,128]{2,1,0:T(8,128)(2,1)S(1)} %shard_map.92), channel_id=1, replica_groups={{0,8,16,24,32,40,48,56},{2,10,18,26,34,42,50,58},{4,12,20,28,36,44,52,6..., dimensions={0} | all-to-all | bytes 1703936 | tf_op jit(solution)/shard_map/all_to_all | solution.py:445
  (62 shorter events, 14.9 us)
Async XLA Ops:
  0.6 31.4 %copy-start.4 = (bf16[128,1024]{1,0:T(8,128)(2,1)S(1)}, bf16[128,1024]{1,0:T(8,128)(2,1)}, u32[]{:S(2)}) copy-start(bf16[128,1024]{1,0:T(8,128)(2,1)} %refs_0_) | copy-start | bytes 786436
  32.1 10.6 %collective-permute-start = (bf16[128,1024]{1,0:T(8,128)(2,1)S(1)}, bf16[128,1024]{1,0:T(8,128)(2,1)S(1)}, u32[]{:S(2)}, u32[]{:S(2)}) collective-permute-start(bf16[128,1024]{1,0:T(8,128)(2,1)S(1)} %copy-done.4), channel_id=1, source_target_pairs={{0,8},{2,10},{4,12},{6,14},{8,16},{10,18},{12,20},{14,22},{16,24},... | collective-permute-start | bytes 786440 | tf_op jit(solution)/shard_map/ppermute | solution.py:458
  32.7 38.9 %all-to-all-start.1 = ((bf16[16,656,128]{2,1,0:T(8,128)(2,1)}), bf16[16,656,128]{2,1,0:T(8,128)(2,1)S(1)}, u32[]{:S(2)}, u32[]{:S(2)}) async-start(bf16[16,656,128]{2,1,0:T(8,128)(2,1)} %get-tuple-element.33), calls=%async_computation.1 | async-start | bytes 5373952 | tf_op jit(solution)/shard_map/all_to_all | solution.py:445
  40.0 7.1 %collective-permute-start.4 = (bf16[128,1024]{1,0:T(8,128)(2,1)S(1)}, bf16[128,1024]{1,0:T(8,128)(2,1)S(1)}, u32[]{:S(2)}, u32[]{:S(2)}) collective-permute-start(bf16[128,1024]{1,0:T(8,128)(2,1)S(1)} %copy-done.4), channel_id=1, source_target_pairs={{0,56},{2,58},{4,60},{6,62},{8,0},{10,2},{12,4},{14,6},{16,8},{18,... | collective-permute-start | bytes 786440 | tf_op jit(solution)/shard_map/ppermute | solution.py:458
  42.6 7.6 %collective-permute-start.1 = (bf16[128,1024]{1,0:T(8,128)(2,1)S(1)}, bf16[128,1024]{1,0:T(8,128)(2,1)S(1)}, u32[]{:S(2)}, u32[]{:S(2)}) collective-permute-start(bf16[128,1024]{1,0:T(8,128)(2,1)S(1)} %collective-permute-done.refs_1_), channel_id=1, source_target_pairs={{0,8},{2,10},{4,12},{6,14},{8,16},{10,18},{12,20},{14,22},{16,24},... | collective-permute-start | bytes 786440 | tf_op jit(solution)/shard_map/ppermute | solution.py:458
  47.1 7.8 %collective-permute-start.5 = (bf16[128,1024]{1,0:T(8,128)(2,1)S(1)}, bf16[128,1024]{1,0:T(8,128)(2,1)S(1)}, u32[]{:S(2)}, u32[]{:S(2)}) collective-permute-start(bf16[128,1024]{1,0:T(8,128)(2,1)S(1)} %collective-permute-done.4.refs_7_), channel_id=1, source_target_pairs={{0,56},{2,58},{4,60},{6,62},{8,0},{10,2},{12,4},{14,6},{16,8},{18,... | collective-permute-start | bytes 786440 | tf_op jit(solution)/shard_map/ppermute | solution.py:458
  50.2 8.4 %collective-permute-start.2 = (bf16[128,1024]{1,0:T(8,128)(2,1)S(1)}, bf16[128,1024]{1,0:T(8,128)(2,1)S(1)}, u32[]{:S(2)}, u32[]{:S(2)}) collective-permute-start(bf16[128,1024]{1,0:T(8,128)(2,1)S(1)} %collective-permute-done.1.refs_2_), channel_id=1, source_target_pairs={{0,8},{2,10},{4,12},{6,14},{8,16},{10,18},{12,20},{14,22},{16,24},... | collective-permute-start | bytes 786440 | tf_op jit(solution)/shard_map/ppermute | solution.py:458
  54.9 7.6 %collective-permute-start.6 = (bf16[128,1024]{1,0:T(8,128)(2,1)S(1)}, bf16[128,1024]{1,0:T(8,128)(2,1)S(1)}, u32[]{:S(2)}, u32[]{:S(2)}) collective-permute-start(bf16[128,1024]{1,0:T(8,128)(2,1)S(1)} %collective-permute-done.5.refs_6_), channel_id=1, source_target_pairs={{0,56},{2,58},{4,60},{6,62},{8,0},{10,2},{12,4},{14,6},{16,8},{18,... | collective-permute-start | bytes 786440 | tf_op jit(solution)/shard_map/ppermute | solution.py:458
  58.6 7.6 %collective-permute-start.3 = (bf16[128,1024]{1,0:T(8,128)(2,1)S(1)}, bf16[128,1024]{1,0:T(8,128)(2,1)S(1)}, u32[]{:S(2)}, u32[]{:S(2)}) collective-permute-start(bf16[128,1024]{1,0:T(8,128)(2,1)S(1)} %collective-permute-done.2.refs_3_), channel_id=1, source_target_pairs={{0,8},{2,10},{4,12},{6,14},{8,16},{10,18},{12,20},{14,22},{16,24},... | collective-permute-start | bytes 786440 | tf_op jit(solution)/shard_map/ppermute | solution.py:458
  67.6 16.6 %collective-permute-start.7 = (bf16[1024,1024]{1,0:T(8,128)(2,1)}, bf16[1024,1024]{1,0:T(8,128)(2,1)}, u32[]{:S(2)}, u32[]{:S(2)}) collective-permute-start(bf16[1024,1024]{1,0:T(8,128)(2,1)} %shard_map.87), channel_id=1, source_target_pairs={{0,1},{1,0},{2,3},{3,2},{4,5},{5,4},{6,7},{7,6},{8,9},{9,8},{10,11... | collective-permute-start | bytes 6291464 | tf_op jit(solution)/shard_map/ppermute | solution.py:451
  77.1 7.2 %copy-start.2 = (bf16[2048,128]{1,0:T(8,128)(2,1)}, bf16[2048,128]{1,0:T(8,128)(2,1)S(1)}, u32[]{:S(2)}) copy-start(bf16[2048,128]{1,0:T(8,128)(2,1)S(1)} %get-tuple-element.36) | copy-start | bytes 1572868
  77.1 20.2 %all-to-all-start.2 = ((bf16[16,272,128]{2,1,0:T(8,128)(2,1)}), bf16[16,272,128]{2,1,0:T(8,128)(2,1)}, u32[]{:S(2)}, u32[]{:S(2)}) async-start(bf16[16,272,128]{2,1,0:T(8,128)(2,1)} %copy-done.1), calls=%async_computation.2 | async-start | bytes 2228224 | tf_op jit(solution)/shard_map/all_to_all | solution.py:445
  84.2 2.5 %copy-start.7 = (bf16[1024,1024]{1,0:T(8,128)(2,1)S(1)}, bf16[1024,1024]{1,0:T(8,128)(2,1)}, u32[]{:S(2)}) copy-start(bf16[1024,1024]{1,0:T(8,128)(2,1)} %shard_map.87) | copy-start | bytes 6291460
  104.5 13.0 %copy-start.5 = (bf16[1024,128]{1,0:T(8,128)(2,1)}, bf16[1024,128]{1,0:T(8,128)(2,1)S(1)}, u32[]{:S(2)}) copy-start(bf16[1024,128]{1,0:T(8,128)(2,1)S(1)} %get-tuple-element.38.refs_0_) | copy-start | bytes 786436
  104.5 10.5 %copy-start.15 = (bf16[1024,128]{1,0:T(8,128)(2,1)S(1)}, bf16[1024,128]{1,0:T(8,128)(2,1)}, u32[]{:S(2)}) copy-start(bf16[1024,128]{1,0:T(8,128)(2,1)} %get-tuple-element.52) | copy-start | bytes 786436
  104.5 26.4 %all-to-all-start.3 = ((bf16[16,400,128]{2,1,0:T(8,128)(2,1)}), bf16[16,400,128]{2,1,0:T(8,128)(2,1)}, u32[]{:S(2)}, u32[]{:S(2)}) async-start(bf16[16,400,128]{2,1,0:T(8,128)(2,1)} %get-tuple-element.37), calls=%async_computation.3 | async-start | bytes 3276800 | tf_op jit(solution)/shard_map/all_to_all | solution.py:445
  111.8 7.6 %collective-permute-start.8 = (bf16[1024,128]{1,0:T(8,128)(2,1)S(1)}, bf16[1024,128]{1,0:T(8,128)(2,1)S(1)}, u32[]{:S(2)}, u32[]{:S(2)}) collective-permute-start(bf16[1024,128]{1,0:T(8,128)(2,1)S(1)} %get-tuple-element.38.refs_0_), channel_id=1, source_target_pairs={{0,8},{2,10},{4,12},{6,14},{8,16},{10,18},{12,20},{14,22},{16,24},... | collective-permute-start | bytes 786440 | tf_op jit(solution)/shard_map/ppermute | solution.py:458
  112.2 7.8 %collective-permute-start.9 = (bf16[1024,128]{1,0:T(8,128)(2,1)S(1)}, bf16[1024,128]{1,0:T(8,128)(2,1)}, u32[]{:S(2)}, u32[]{:S(2)}) collective-permute-start(bf16[1024,128]{1,0:T(8,128)(2,1)S(1)} %get-tuple-element.38.refs_0_), channel_id=1, source_target_pairs={{0,56},{2,58},{4,60},{6,62},{8,0},{10,2},{12,4},{14,6},{16,8},{18,... | collective-permute-start | bytes 786440 | tf_op jit(solution)/shard_map/ppermute | solution.py:458
  115.0 2.5 %copy-start.8 = (bf16[1024,1024]{1,0:T(8,128)(2,1)S(1)}, bf16[1024,1024]{1,0:T(8,128)(2,1)}, u32[]{:S(2)}) copy-start(bf16[1024,1024]{1,0:T(8,128)(2,1)} %shard_map.87) | copy-start | bytes 6291460
  138.9 1.5 copy-start
  140.4 7.6 %copy-start.11 = (bf16[1024,128]{1,0:T(8,128)(2,1)S(1)}, bf16[1024,128]{1,0:T(8,128)(2,1)}, u32[]{:S(2)}) copy-start(bf16[1024,128]{1,0:T(8,128)(2,1)} %copy-done.10) | copy-start | bytes 786436
  140.4 40.5 %all-to-all-start.4 = ((bf16[16,640,128]{2,1,0:T(8,128)(2,1)}), bf16[16,640,128]{2,1,0:T(8,128)(2,1)S(1)}, u32[]{:S(2)}, u32[]{:S(2)}) async-start(bf16[16,640,128]{2,1,0:T(8,128)(2,1)} %copy-done), calls=%async_computation.4 | async-start | bytes 5242880 | tf_op jit(solution)/shard_map/all_to_all | solution.py:445
  148.0 8.7 %collective-permute-start.10 = (bf16[1024,128]{1,0:T(8,128)(2,1)S(1)}, bf16[1024,128]{1,0:T(8,128)(2,1)S(1)}, u32[]{:S(2)}, u32[]{:S(2)}) collective-permute-start(bf16[1024,128]{1,0:T(8,128)(2,1)S(1)} %copy-done.11), channel_id=1, source_target_pairs={{0,8},{2,10},{4,12},{6,14},{8,16},{10,18},{12,20},{14,22},{16,24},... | collective-permute-start | bytes 786440 | tf_op jit(solution)/shard_map/ppermute | solution.py:458
  148.1 8.7 %collective-permute-start.13 = (bf16[1024,128]{1,0:T(8,128)(2,1)}, bf16[1024,128]{1,0:T(8,128)(2,1)S(1)}, u32[]{:S(2)}, u32[]{:S(2)}) collective-permute-start(bf16[1024,128]{1,0:T(8,128)(2,1)} %collective-permute-done.9.refs_7_), channel_id=1, source_target_pairs={{0,56},{2,58},{4,60},{6,62},{8,0},{10,2},{12,4},{14,6},{16,8},{18,... | collective-permute-start | bytes 786440 | tf_op jit(solution)/shard_map/ppermute | solution.py:458
  156.7 17.1 %copy-start.12 = (bf16[1024,128]{1,0:T(8,128)(2,1)}, bf16[1024,128]{1,0:T(8,128)(2,1)S(1)}, u32[]{:S(2)}) copy-start(bf16[1024,128]{1,0:T(8,128)(2,1)S(1)} %collective-permute-done.10.refs_2_) | copy-start | bytes 786436
  156.7 9.5 %collective-permute-start.11 = (bf16[1024,128]{1,0:T(8,128)(2,1)S(1)}, bf16[1024,128]{1,0:T(8,128)(2,1)S(1)}, u32[]{:S(2)}, u32[]{:S(2)}) collective-permute-start(bf16[1024,128]{1,0:T(8,128)(2,1)S(1)} %collective-permute-done.10.refs_2_), channel_id=1, source_target_pairs={{0,8},{2,10},{4,12},{6,14},{8,16},{10,18},{12,20},{14,22},{16,24},... | collective-permute-start | bytes 786440 | tf_op jit(solution)/shard_map/ppermute | solution.py:458
  156.8 16.9 %copy-start.13 = (bf16[1024,128]{1,0:T(8,128)(2,1)}, bf16[1024,128]{1,0:T(8,128)(2,1)S(1)}, u32[]{:S(2)}) copy-start(bf16[1024,128]{1,0:T(8,128)(2,1)S(1)} %collective-permute-done.13.refs_6_) | copy-start | bytes 786436
  156.8 9.4 %collective-permute-start.14 = (bf16[1024,128]{1,0:T(8,128)(2,1)S(1)}, bf16[1024,128]{1,0:T(8,128)(2,1)S(1)}, u32[]{:S(2)}, u32[]{:S(2)}) collective-permute-start(bf16[1024,128]{1,0:T(8,128)(2,1)S(1)} %collective-permute-done.13.refs_6_), channel_id=1, source_target_pairs={{0,56},{2,58},{4,60},{6,62},{8,0},{10,2},{12,4},{14,6},{16,8},{18,... | collective-permute-start | bytes 786440 | tf_op jit(solution)/shard_map/ppermute | solution.py:458
  166.2 7.6 %copy-start.14 = (bf16[1024,128]{1,0:T(8,128)(2,1)}, bf16[1024,128]{1,0:T(8,128)(2,1)S(1)}, u32[]{:S(2)}) copy-start(bf16[1024,128]{1,0:T(8,128)(2,1)S(1)} %collective-permute-done.11.refs_3_) | copy-start | bytes 786436
  166.2 7.6 %collective-permute-start.12 = (bf16[1024,128]{1,0:T(8,128)(2,1)S(1)}, bf16[1024,128]{1,0:T(8,128)(2,1)S(1)}, u32[]{:S(2)}, u32[]{:S(2)}) collective-permute-start(bf16[1024,128]{1,0:T(8,128)(2,1)S(1)} %collective-permute-done.11.refs_3_), channel_id=1, source_target_pairs={{0,8},{2,10},{4,12},{6,14},{8,16},{10,18},{12,20},{14,22},{16,24},... | collective-permute-start | bytes 786440 | tf_op jit(solution)/shard_map/ppermute | solution.py:458
  166.3 7.5 %copy-start.16 = (bf16[1024,128]{1,0:T(8,128)(2,1)}, bf16[1024,128]{1,0:T(8,128)(2,1)S(1)}, u32[]{:S(2)}) copy-start(bf16[1024,128]{1,0:T(8,128)(2,1)S(1)} %collective-permute-done.14.refs_5_) | copy-start | bytes 786436
  179.0 1.9 collective-permute-start.15
  (6 other events, 4.9 us)

commit v5 on v3

--- a/solution.py
+++ b/solution.py
@@ -355,10 +355,10 @@
         other_out[tokens, :] = both[:, DIM:]
 
 
-def gather_home(slot_in, own_in, other_in, e_ref, msg_ref, y_ref, slot_ref, own_ref, other_ref, sems):
+def gather_home(slot_in, mixed_in, e_ref, msg_ref, y_ref, slot_ref, mixed_ref, sems):
     fetches = [
         pltpu.make_async_copy(source, dest, sems.at[n])
-        for n, (source, dest) in enumerate(((slot_in, slot_ref), (own_in, own_ref), (other_in, other_ref)))
+        for n, (source, dest) in enumerate(((slot_in, slot_ref), (mixed_in, mixed_ref)))
     ]
     for fetch in fetches:
         fetch.start()
@@ -390,10 +390,8 @@
         msg_ref[z, 384:400, :] = high[z * 16 : (z + 1) * 16, :]
         msg_ref[z, 400:416, :] = low[z * 16 : (z + 1) * 16, :]
     fetches[1].wait()
-    fetches[2].wait()
     for z in range(NZ):
-        tokens = slice(z * TOK, (z + 1) * TOK)
-        msg_ref[z, 256:384, :] = (own_ref[tokens, :] + other_ref[tokens, :]).astype(BF)
+        msg_ref[z, 256:384, :] = mixed_ref[z * TOK : (z + 1) * TOK, :]
 
 
 def unpack_ring(f_ref, qk_ref, v_ref, mixed_ref, gw_ref):
@@ -572,19 +570,18 @@
         scalars=1,
         hbm_in=1 + NZ,
     )(jnp.stack([core, z_place]), got_d, *all_attended)
-    other_rows = swap_cores(other_rows)
+    mixed_rows = (own_rows + swap_cores(other_rows)).astype(BF)
     (msg,) = on_device(
         gather_home,
         [((NZ, ROWS_F, DIM), BF)],
         [
             ((NZ, ROUNDS * SLOTS, 2 * DIM), BF),
             ((16 + TOK, TOK), F32),
-            ((NZ * TOK, DIM), F32),
-            ((NZ * TOK, DIM), F32),
-            pltpu.SemaphoreType.DMA((3,)),
+            ((NZ * TOK, DIM), BF),
+            pltpu.SemaphoreType.DMA((2,)),
         ],
-        hbm_in=3,
-    )(slots, own_rows, other_rows, got_e)
+        hbm_in=2,
+    )(slots, mixed_rows, got_e)
     got_f = exchange(msg, RINGS)
     grad_qk, grad_values, mixed, grad_weight = on_device(
         unpack_ring,

time: 208 us -> 208 us (level)
    unnamed x36 -> x32, local copies, waits for them, and re-layouts: 5.62 us -> 4.88 us
where the time goes in v5:
time: 208 us
  waiting for transfers between devices  59.4 us (29%)
  blocking collectives  54.2 us (26%)
  starting transfers between devices  49.5 us (24%)
  Pallas kernels  30.6 us (15%)
  matrix products  7.37 us (4%)
  local copies, waits for them, and re-layouts  4.88 us (2%)
    all_to_all x2, blocking collectives, exchange(): lax.all_to_all(message, 'ctx', split_axis=0, concat_axis=0, tiled=True, a...  54.2 us
    ppermute x14, waiting for transfers between devices, pass_on(): return lax.ppermute(block, 'ctx', turn)  38 us
    pallas_call x10, Pallas kernels, call(): pl.pallas_call(body, out_shape=shapes, in_specs=[pl.BlockSpec(memory_spac...  30.6 us
    all_to_all x4, starting transfers between devices, exchange(): lax.all_to_all(message, 'ctx', split_axis=0, concat_axis=0, tiled=True, a...  29.2 us
    ppermute x14, starting transfers between devices, pass_on(): return lax.ppermute(block, 'ctx', turn)  20.1 us
    all_to_all x4, waiting for transfers between devices, exchange(): lax.all_to_all(message, 'ctx', split_axis=0, concat_axis=0, tiled=True, a...  19.5 us
    unnamed x32, local copies, waits for them, and re-layouts  4.88 us
  transfers between devices with their start and end apart: 20, of which 14 were waited for; matrix products, arithmetic and copies ran while one was open for 4% of the time, Pallas kernels for 5%

profile of v5, /device:TPU:18, one launch (start us, length us, event | category | flops | bytes accessed | tf_op | source)
XLA Modules:
  0.0 207.7 jit_solution(13922582688667498004)
XLA Ops:
  1.8 27.2 %all_to_all.30.a_ref = bf16[8,288,128]{2,1,0:T(8,128)(2,1)S(1)} all-to-all(bf16[8,288,128]{2,1,0:T(8,128)(2,1)S(1)} %shard_map.84), channel_id=1, replica_groups={{0,8,16,24,32,40,48,56},{2,10,18,26,34,42,50,58},{4,12,20,28,36,44,52,6..., dimensions={0} | all-to-all | bytes 1179648 | tf_op jit(solution)/shard_map/all_to_all | solution.py:443
  29.0 3.1 %shard_map.85 = (f32[144,128]{1,0:T(8,128)}, bf16[16,656,128]{2,1,0:T(8,128)(2,1)}) custom-call(bf16[8,288,128]{2,1,0:T(8,128)(2,1)S(1)} %all_to_all.30.a_ref), custom_call_target="tpu_custom_call" | custom-call | tf_op jit(solution)/shard_map/pallas_call | solution.py:425
  32.7 7.3 %all-to-all-start.1 = ((bf16[16,656,128]{2,1,0:T(8,128)(2,1)}), bf16[16,656,128]{2,1,0:T(8,128)(2,1)S(1)}, u32[]{:S(2)}, u32[]{:S(2)}) async-start(bf16[16,656,128]{2,1,0:T(8,128)(2,1)} %get-tuple-element.33), calls=%async_computation.1 | async-start | bytes 5373952 | tf_op jit(solution)/shard_map/all_to_all | solution.py:443
  40.0 2.7 %collective-permute-start.4 = (bf16[128,1024]{1,0:T(8,128)(2,1)S(1)}, bf16[128,1024]{1,0:T(8,128)(2,1)S(1)}, u32[]{:S(2)}, u32[]{:S(2)}) collective-permute-start(bf16[128,1024]{1,0:T(8,128)(2,1)S(1)} %copy-done.3), channel_id=1, source_target_pairs={{0,56},{2,58},{4,60},{6,62},{8,0},{10,2},{12,4},{14,6},{16,8},{18,... | collective-permute-start | bytes 786440 | tf_op jit(solution)/shard_map/ppermute | solution.py:456
  42.7 4.4 %collective-permute-done.4.refs_7_ = bf16[128,1024]{1,0:T(8,128)(2,1)S(1)} collective-permute-done((bf16[128,1024]{1,0:T(8,128)(2,1)S(1)}, bf16[128,1024]{1,0:T(8,128)(2,1)S(1)}, u32[]{:S(2)}, u32[]{:S(2)}) %collective-permute-start.4) | collective-permute-done | bytes 262176 | tf_op jit(solution)/shard_map/ppermute | solution.py:456
  47.1 3.1 %collective-permute-start.5 = (bf16[128,1024]{1,0:T(8,128)(2,1)S(1)}, bf16[128,1024]{1,0:T(8,128)(2,1)S(1)}, u32[]{:S(2)}, u32[]{:S(2)}) collective-permute-start(bf16[128,1024]{1,0:T(8,128)(2,1)S(1)} %collective-permute-done.4.refs_7_), channel_id=1, source_target_pairs={{0,56},{2,58},{4,60},{6,62},{8,0},{10,2},{12,4},{14,6},{16,8},{18,... | collective-permute-start | bytes 786440 | tf_op jit(solution)/shard_map/ppermute | solution.py:456
  50.3 4.7 %collective-permute-done.5.refs_6_ = bf16[128,1024]{1,0:T(8,128)(2,1)S(1)} collective-permute-done((bf16[128,1024]{1,0:T(8,128)(2,1)S(1)}, bf16[128,1024]{1,0:T(8,128)(2,1)S(1)}, u32[]{:S(2)}, u32[]{:S(2)}) %collective-permute-start.5) | collective-permute-done | bytes 262176 | tf_op jit(solution)/shard_map/ppermute | solution.py:456
  55.0 3.7 %collective-permute-start.6 = (bf16[128,1024]{1,0:T(8,128)(2,1)S(1)}, bf16[128,1024]{1,0:T(8,128)(2,1)S(1)}, u32[]{:S(2)}, u32[]{:S(2)}) collective-permute-start(bf16[128,1024]{1,0:T(8,128)(2,1)S(1)} %collective-permute-done.5.refs_6_), channel_id=1, source_target_pairs={{0,56},{2,58},{4,60},{6,62},{8,0},{10,2},{12,4},{14,6},{16,8},{18,... | collective-permute-start | bytes 786440 | tf_op jit(solution)/shard_map/ppermute | solution.py:456
  58.7 3.9 %collective-permute-done.6.refs_5_ = bf16[128,1024]{1,0:T(8,128)(2,1)S(1)} collective-permute-done((bf16[128,1024]{1,0:T(8,128)(2,1)S(1)}, bf16[128,1024]{1,0:T(8,128)(2,1)S(1)}, u32[]{:S(2)}, u32[]{:S(2)}) %collective-permute-start.6) | collective-permute-done | bytes 262176 | tf_op jit(solution)/shard_map/ppermute | solution.py:456
  62.5 3.7 %collective-permute-done.3.refs_4_ = bf16[128,1024]{1,0:T(8,128)(2,1)S(1)} collective-permute-done((bf16[128,1024]{1,0:T(8,128)(2,1)S(1)}, bf16[128,1024]{1,0:T(8,128)(2,1)S(1)}, u32[]{:S(2)}, u32[]{:S(2)}) %collective-permute-start.3) | collective-permute-done | bytes 262176 | tf_op jit(solution)/shard_map/ppermute | solution.py:456
  67.8 3.9 %all-to-all-done.1.b_ref = bf16[16,656,128]{2,1,0:T(8,128)(2,1)S(1)} async-done(((bf16[16,656,128]{2,1,0:T(8,128)(2,1)}), bf16[16,656,128]{2,1,0:T(8,128)(2,1)S(1)}, u32[]{:S(2)}, u32[]{:S(2)}) %all-to-all-start.1) | async-done | bytes 2687008 | tf_op jit(solution)/shard_map/all_to_all | solution.py:443
  71.7 4.4 %shard_map.86 = (f32[288,128]{1,0:T(8,128)}, bf16[16,272,128]{2,1,0:T(8,128)(2,1)S(1)}, bf16[2048,128]{1,0:T(8,128)(2,1)S(1)}) custom-call(bf16[16,656,128]{2,1,0:T(8,128)(2,1)S(1)} %all-to-all-done.1.b_ref), custom_call_target="tpu_custom_call" | custom-call | tf_op jit(solution)/shard_map/pallas_call | solution.py:425
  77.1 7.2 %all-to-all-start.2 = ((bf16[16,272,128]{2,1,0:T(8,128)(2,1)}), bf16[16,272,128]{2,1,0:T(8,128)(2,1)}, u32[]{:S(2)}, u32[]{:S(2)}) async-start(bf16[16,272,128]{2,1,0:T(8,128)(2,1)} %copy-done.1), calls=%async_computation.2 | async-start | bytes 2228224 | tf_op jit(solution)/shard_map/all_to_all | solution.py:443
  84.3 2.4 %fusion = f32[1024,128]{1,0:T(8,128)S(1)} fusion(bf16[1024,1024]{1,0:T(8,128)(2,1)} %collective-permute-done.7, bf16[2048,128]{1,0:T(8,128)(2,1)S(1)} %get-tuple-element.36, s32[]{:T(128)S(6)} %select_n.25), kind=kOutput, calls=%fused_computation.5 | convolution fusion | flops 268435456 | bytes 2883588 | tf_op jit(solution)/shard_map/dot_general | solution.py:53
  88.5 8.9 %all-to-all-done.2.c_ref = bf16[16,272,128]{2,1,0:T(8,128)(2,1)} async-done(((bf16[16,272,128]{2,1,0:T(8,128)(2,1)}), bf16[16,272,128]{2,1,0:T(8,128)(2,1)}, u32[]{:S(2)}, u32[]{:S(2)}) %all-to-all-start.2) | async-done | bytes 1114144 | tf_op jit(solution)/shard_map/all_to_all | solution.py:443
  97.4 7.2 %shard_map.88 = (bf16[1024,128]{1,0:T(8,128)(2,1)}, bf16[16,400,128]{2,1,0:T(8,128)(2,1)}, bf16[1024,128]{1,0:T(8,128)(2,1)S(1)}) custom-call(s32[1]{0:T(128)} %bitcast.1.z_ref, f32[144,128]{1,0:T(8,128)} %get-tuple-element.31.slot_in, bf16[16,1024]{1,0:T(8,128)(2,1)} %weight_in.1, bf16[16,272,128]{2,1,0:T(8,128)(2,1)} %all-to-all-done.2.c_ref, ...), custom_call_target="tpu_custom_call" | custom-call | tf_op jit(solution)/shard_map/pallas_call | solution.py:425
  104.6 7.2 %all-to-all-start.3 = ((bf16[16,400,128]{2,1,0:T(8,128)(2,1)}), bf16[16,400,128]{2,1,0:T(8,128)(2,1)}, u32[]{:S(2)}, u32[]{:S(2)}) async-start(bf16[16,400,128]{2,1,0:T(8,128)(2,1)} %get-tuple-element.37), calls=%async_computation.3 | async-start | bytes 3276800 | tf_op jit(solution)/shard_map/all_to_all | solution.py:443
  111.8 3.0 %collective-permute-start.10 = (bf16[1024,128]{1,0:T(8,128)(2,1)S(1)}, bf16[1024,128]{1,0:T(8,128)(2,1)S(1)}, u32[]{:S(2)}, u32[]{:S(2)}) collective-permute-start(bf16[1024,128]{1,0:T(8,128)(2,1)S(1)} %get-tuple-element.38.refs_0_), channel_id=1, source_target_pairs={{0,56},{2,58},{4,60},{6,62},{8,0},{10,2},{12,4},{14,6},{16,8},{18,... | collective-permute-start | bytes 786440 | tf_op jit(solution)/shard_map/ppermute | solution.py:456
  114.8 2.5 %convolution_convert_fusion = bf16[1024,128]{1,0:T(8,128)(2,1)S(1)} fusion(bf16[1024,1024]{1,0:T(8,128)(2,1)} %collective-permute-done.7, bf16[1024,128]{1,0:T(8,128)(2,1)S(1)} %copy-done.12), kind=kOutput, calls=%fused_computation.1 | convolution fusion | flops 268566528 | bytes 2621440 | tf_op jit(solution)/shard_map/dot_general | solution.py:61
  117.3 2.1 collective-permute-done.10.refs_7_
  119.4 3.7 %collective-permute-start.11 = (bf16[1024,128]{1,0:T(8,128)(2,1)S(1)}, bf16[1024,128]{1,0:T(8,128)(2,1)S(1)}, u32[]{:S(2)}, u32[]{:S(2)}) collective-permute-start(bf16[1024,128]{1,0:T(8,128)(2,1)S(1)} %collective-permute-done.10.refs_7_), channel_id=1, source_target_pairs={{0,56},{2,58},{4,60},{6,62},{8,0},{10,2},{12,4},{14,6},{16,8},{18,... | collective-permute-start | bytes 786440 | tf_op jit(solution)/shard_map/ppermute | solution.py:456
  123.9 3.0 %collective-permute-done.11.refs_6_ = bf16[1024,128]{1,0:T(8,128)(2,1)S(1)} collective-permute-done((bf16[1024,128]{1,0:T(8,128)(2,1)S(1)}, bf16[1024,128]{1,0:T(8,128)(2,1)S(1)}, u32[]{:S(2)}, u32[]{:S(2)}) %collective-permute-start.11) | collective-permute-done | bytes 262176 | tf_op jit(solution)/shard_map/ppermute | solution.py:456
  127.7 3.1 %collective-permute-done.9.refs_2_ = bf16[1024,128]{1,0:T(8,128)(2,1)} collective-permute-done((bf16[1024,128]{1,0:T(8,128)(2,1)S(1)}, bf16[1024,128]{1,0:T(8,128)(2,1)}, u32[]{:S(2)}, u32[]{:S(2)}) %collective-permute-start.9) | collective-permute-done | bytes 262176 | tf_op jit(solution)/shard_map/ppermute | solution.py:456
  132.0 2.0 shard_map.90
  134.0 5.0 %shard_map.91 = (bf16[16,640,128]{2,1,0:T(8,128)(2,1)S(1)}, f32[8,128]{1,0:T(8,128)}) custom-call(bf16[16,400,128]{2,1,0:T(8,128)(2,1)} %all-to-all-done.3.d_ref.d_in, bf16[16,656,128]{2,1,0:T(8,128)(2,1)S(1)} %all-to-all-done.1.b_ref, f32[16,256,256]{2,1,0:T(8,128)S(1)} %get-tuple-element.50.prob_ref, ...), custom_call_target="tpu_custom_call" | custom-call | tf_op jit(solution)/shard_map/pallas_call | solution.py:425
  140.5 7.6 %all-to-all-start.4 = ((bf16[16,640,128]{2,1,0:T(8,128)(2,1)}), bf16[16,640,128]{2,1,0:T(8,128)(2,1)S(1)}, u32[]{:S(2)}, u32[]{:S(2)}) async-start(bf16[16,640,128]{2,1,0:T(8,128)(2,1)} %copy-done), calls=%async_computation.4 | async-start | bytes 5242880 | tf_op jit(solution)/shard_map/all_to_all | solution.py:443
  148.2 3.2 %collective-permute-start.14 = (bf16[1024,128]{1,0:T(8,128)(2,1)S(1)}, bf16[1024,128]{1,0:T(8,128)(2,1)S(1)}, u32[]{:S(2)}, u32[]{:S(2)}) collective-permute-start(bf16[1024,128]{1,0:T(8,128)(2,1)S(1)} %copy-done.11), channel_id=1, source_target_pairs={{0,56},{2,58},{4,60},{6,62},{8,0},{10,2},{12,4},{14,6},{16,8},{18,... | collective-permute-start | bytes 786440 | tf_op jit(solution)/shard_map/ppermute | solution.py:456
  151.3 5.6 %collective-permute-done.12.refs_3_ = bf16[1024,128]{1,0:T(8,128)(2,1)S(1)} collective-permute-done((bf16[1024,128]{1,0:T(8,128)(2,1)}, bf16[1024,128]{1,0:T(8,128)(2,1)S(1)}, u32[]{:S(2)}, u32[]{:S(2)}) %collective-permute-start.12) | collective-permute-done | bytes 262176 | tf_op jit(solution)/shard_map/ppermute | solution.py:456
  157.0 7.5 %collective-permute-done.13.refs_4_ = bf16[1024,128]{1,0:T(8,128)(2,1)S(1)} collective-permute-done((bf16[1024,128]{1,0:T(8,128)(2,1)S(1)}, bf16[1024,128]{1,0:T(8,128)(2,1)S(1)}, u32[]{:S(2)}, u32[]{:S(2)}) %collective-permute-start.13) | collective-permute-done | bytes 262176 | tf_op jit(solution)/shard_map/ppermute | solution.py:456
  165.2 3.7 %shard_map.89 = (f32[1024,128]{1,0:T(8,128)S(1)}, f32[1024,128]{1,0:T(8,128)S(1)}) custom-call(s32[2]{0:T(128)S(1)} %pad_add_fusion.place_ref, bf16[16,400,128]{2,1,0:T(8,128)(2,1)} %all-to-all-done.3.d_ref.d_in, bf16[1024,128]{1,0:T(8,128)(2,1)} %copy-done.4, bf16[1024,128]{1,0:T(8,128)(2,1)} %copy-done.9, ...), custom_call_target="tpu_custom_call" | custom-call | tf_op jit(solution)/shard_map/pallas_call | solution.py:425
  171.8 6.4 %all-to-all-done.4.e_ref = bf16[16,640,128]{2,1,0:T(8,128)(2,1)S(1)} async-done(((bf16[16,640,128]{2,1,0:T(8,128)(2,1)}), bf16[16,640,128]{2,1,0:T(8,128)(2,1)S(1)}, u32[]{:S(2)}, u32[]{:S(2)}) %all-to-all-start.4) | async-done | bytes 2621472 | tf_op jit(solution)/shard_map/all_to_all | solution.py:443
  179.6 27.0 %all_to_all.31.f_ref = bf16[8,416,128]{2,1,0:T(8,128)(2,1)S(1)} all-to-all(bf16[8,416,128]{2,1,0:T(8,128)(2,1)S(1)} %shard_map.92), channel_id=1, replica_groups={{0,8,16,24,32,40,48,56},{2,10,18,26,34,42,50,58},{4,12,20,28,36,44,52,6..., dimensions={0} | all-to-all | bytes 1703936 | tf_op jit(solution)/shard_map/all_to_all | solution.py:443
  (59 shorter events, 16.4 us)
Async XLA Ops:
  0.6 31.5 %copy-start.3 = (bf16[128,1024]{1,0:T(8,128)(2,1)S(1)}, bf16[128,1024]{1,0:T(8,128)(2,1)}, u32[]{:S(2)}) copy-start(bf16[128,1024]{1,0:T(8,128)(2,1)} %refs_0_) | copy-start | bytes 786436
  32.1 10.6 %collective-permute-start = (bf16[128,1024]{1,0:T(8,128)(2,1)S(1)}, bf16[128,1024]{1,0:T(8,128)(2,1)S(1)}, u32[]{:S(2)}, u32[]{:S(2)}) collective-permute-start(bf16[128,1024]{1,0:T(8,128)(2,1)S(1)} %copy-done.3), channel_id=1, source_target_pairs={{0,8},{2,10},{4,12},{6,14},{8,16},{10,18},{12,20},{14,22},{16,24},... | collective-permute-start | bytes 786440 | tf_op jit(solution)/shard_map/ppermute | solution.py:456
  32.7 38.9 %all-to-all-start.1 = ((bf16[16,656,128]{2,1,0:T(8,128)(2,1)}), bf16[16,656,128]{2,1,0:T(8,128)(2,1)S(1)}, u32[]{:S(2)}, u32[]{:S(2)}) async-start(bf16[16,656,128]{2,1,0:T(8,128)(2,1)} %get-tuple-element.33), calls=%async_computation.1 | async-start | bytes 5373952 | tf_op jit(solution)/shard_map/all_to_all | solution.py:443
  40.0 7.1 %collective-permute-start.4 = (bf16[128,1024]{1,0:T(8,128)(2,1)S(1)}, bf16[128,1024]{1,0:T(8,128)(2,1)S(1)}, u32[]{:S(2)}, u32[]{:S(2)}) collective-permute-start(bf16[128,1024]{1,0:T(8,128)(2,1)S(1)} %copy-done.3), channel_id=1, source_target_pairs={{0,56},{2,58},{4,60},{6,62},{8,0},{10,2},{12,4},{14,6},{16,8},{18,... | collective-permute-start | bytes 786440 | tf_op jit(solution)/shard_map/ppermute | solution.py:456
  42.7 7.6 %collective-permute-start.1 = (bf16[128,1024]{1,0:T(8,128)(2,1)S(1)}, bf16[128,1024]{1,0:T(8,128)(2,1)S(1)}, u32[]{:S(2)}, u32[]{:S(2)}) collective-permute-start(bf16[128,1024]{1,0:T(8,128)(2,1)S(1)} %collective-permute-done.refs_1_), channel_id=1, source_target_pairs={{0,8},{2,10},{4,12},{6,14},{8,16},{10,18},{12,20},{14,22},{16,24},... | collective-permute-start | bytes 786440 | tf_op jit(solution)/shard_map/ppermute | solution.py:456
  47.1 7.8 %collective-permute-start.5 = (bf16[128,1024]{1,0:T(8,128)(2,1)S(1)}, bf16[128,1024]{1,0:T(8,128)(2,1)S(1)}, u32[]{:S(2)}, u32[]{:S(2)}) collective-permute-start(bf16[128,1024]{1,0:T(8,128)(2,1)S(1)} %collective-permute-done.4.refs_7_), channel_id=1, source_target_pairs={{0,56},{2,58},{4,60},{6,62},{8,0},{10,2},{12,4},{14,6},{16,8},{18,... | collective-permute-start | bytes 786440 | tf_op jit(solution)/shard_map/ppermute | solution.py:456
  50.3 8.4 %collective-permute-start.2 = (bf16[128,1024]{1,0:T(8,128)(2,1)S(1)}, bf16[128,1024]{1,0:T(8,128)(2,1)S(1)}, u32[]{:S(2)}, u32[]{:S(2)}) collective-permute-start(bf16[128,1024]{1,0:T(8,128)(2,1)S(1)} %collective-permute-done.1.refs_2_), channel_id=1, source_target_pairs={{0,8},{2,10},{4,12},{6,14},{8,16},{10,18},{12,20},{14,22},{16,24},... | collective-permute-start | bytes 786440 | tf_op jit(solution)/shard_map/ppermute | solution.py:456
  55.0 7.6 %collective-permute-start.6 = (bf16[128,1024]{1,0:T(8,128)(2,1)S(1)}, bf16[128,1024]{1,0:T(8,128)(2,1)S(1)}, u32[]{:S(2)}, u32[]{:S(2)}) collective-permute-start(bf16[128,1024]{1,0:T(8,128)(2,1)S(1)} %collective-permute-done.5.refs_6_), channel_id=1, source_target_pairs={{0,56},{2,58},{4,60},{6,62},{8,0},{10,2},{12,4},{14,6},{16,8},{18,... | collective-permute-start | bytes 786440 | tf_op jit(solution)/shard_map/ppermute | solution.py:456
  58.7 7.6 %collective-permute-start.3 = (bf16[128,1024]{1,0:T(8,128)(2,1)S(1)}, bf16[128,1024]{1,0:T(8,128)(2,1)S(1)}, u32[]{:S(2)}, u32[]{:S(2)}) collective-permute-start(bf16[128,1024]{1,0:T(8,128)(2,1)S(1)} %collective-permute-done.2.refs_3_), channel_id=1, source_target_pairs={{0,8},{2,10},{4,12},{6,14},{8,16},{10,18},{12,20},{14,22},{16,24},... | collective-permute-start | bytes 786440 | tf_op jit(solution)/shard_map/ppermute | solution.py:456
  67.7 16.6 %collective-permute-start.7 = (bf16[1024,1024]{1,0:T(8,128)(2,1)}, bf16[1024,1024]{1,0:T(8,128)(2,1)}, u32[]{:S(2)}, u32[]{:S(2)}) collective-permute-start(bf16[1024,1024]{1,0:T(8,128)(2,1)} %shard_map.87), channel_id=1, source_target_pairs={{0,1},{1,0},{2,3},{3,2},{4,5},{5,4},{6,7},{7,6},{8,9},{9,8},{10,11... | collective-permute-start | bytes 6291464 | tf_op jit(solution)/shard_map/ppermute | solution.py:449
  76.1 1.0 copy-start.1
  77.1 7.2 %copy-start.2 = (bf16[2048,128]{1,0:T(8,128)(2,1)}, bf16[2048,128]{1,0:T(8,128)(2,1)S(1)}, u32[]{:S(2)}) copy-start(bf16[2048,128]{1,0:T(8,128)(2,1)S(1)} %get-tuple-element.36) | copy-start | bytes 1572868
  77.1 20.2 %all-to-all-start.2 = ((bf16[16,272,128]{2,1,0:T(8,128)(2,1)}), bf16[16,272,128]{2,1,0:T(8,128)(2,1)}, u32[]{:S(2)}, u32[]{:S(2)}) async-start(bf16[16,272,128]{2,1,0:T(8,128)(2,1)} %copy-done.1), calls=%async_computation.2 | async-start | bytes 2228224 | tf_op jit(solution)/shard_map/all_to_all | solution.py:443
  84.3 2.5 %copy-start.6 = (bf16[1024,1024]{1,0:T(8,128)(2,1)S(1)}, bf16[1024,1024]{1,0:T(8,128)(2,1)}, u32[]{:S(2)}) copy-start(bf16[1024,1024]{1,0:T(8,128)(2,1)} %shard_map.87) | copy-start | bytes 6291460
  104.6 12.7 %copy-start.4 = (bf16[1024,128]{1,0:T(8,128)(2,1)}, bf16[1024,128]{1,0:T(8,128)(2,1)S(1)}, u32[]{:S(2)}) copy-start(bf16[1024,128]{1,0:T(8,128)(2,1)S(1)} %get-tuple-element.38.refs_0_) | copy-start | bytes 786436
  104.6 10.2 %copy-start.12 = (bf16[1024,128]{1,0:T(8,128)(2,1)S(1)}, bf16[1024,128]{1,0:T(8,128)(2,1)}, u32[]{:S(2)}) copy-start(bf16[1024,128]{1,0:T(8,128)(2,1)} %get-tuple-element.52) | copy-start | bytes 786436
  104.6 26.5 %all-to-all-start.3 = ((bf16[16,400,128]{2,1,0:T(8,128)(2,1)}), bf16[16,400,128]{2,1,0:T(8,128)(2,1)}, u32[]{:S(2)}, u32[]{:S(2)}) async-start(bf16[16,400,128]{2,1,0:T(8,128)(2,1)} %get-tuple-element.37), calls=%async_computation.3 | async-start | bytes 3276800 | tf_op jit(solution)/shard_map/all_to_all | solution.py:443
  111.8 7.6 %collective-permute-start.10 = (bf16[1024,128]{1,0:T(8,128)(2,1)S(1)}, bf16[1024,128]{1,0:T(8,128)(2,1)S(1)}, u32[]{:S(2)}, u32[]{:S(2)}) collective-permute-start(bf16[1024,128]{1,0:T(8,128)(2,1)S(1)} %get-tuple-element.38.refs_0_), channel_id=1, source_target_pairs={{0,56},{2,58},{4,60},{6,62},{8,0},{10,2},{12,4},{14,6},{16,8},{18,... | collective-permute-start | bytes 786440 | tf_op jit(solution)/shard_map/ppermute | solution.py:456
  114.8 8.3 %collective-permute-start.8 = (bf16[1024,128]{1,0:T(8,128)(2,1)S(1)}, bf16[1024,128]{1,0:T(8,128)(2,1)S(1)}, u32[]{:S(2)}, u32[]{:S(2)}) collective-permute-start(bf16[1024,128]{1,0:T(8,128)(2,1)S(1)} %get-tuple-element.38.refs_0_), channel_id=1, source_target_pairs={{0,8},{2,10},{4,12},{6,14},{8,16},{10,18},{12,20},{14,22},{16,24},... | collective-permute-start | bytes 786440 | tf_op jit(solution)/shard_map/ppermute | solution.py:456
  114.8 8.3 %copy-start.7 = (bf16[1024,1024]{1,0:T(8,128)(2,1)S(1)}, bf16[1024,1024]{1,0:T(8,128)(2,1)}, u32[]{:S(2)}) copy-start(bf16[1024,1024]{1,0:T(8,128)(2,1)} %shard_map.87) | copy-start | bytes 6291460
  119.4 4.5 %copy-start.8 = (bf16[1024,128]{1,0:T(8,128)(2,1)}, bf16[1024,128]{1,0:T(8,128)(2,1)S(1)}, u32[]{:S(2)}) copy-start(bf16[1024,128]{1,0:T(8,128)(2,1)S(1)} %collective-permute-done.10.refs_7_) | copy-start | bytes 786436
  119.4 7.6 %collective-permute-start.11 = (bf16[1024,128]{1,0:T(8,128)(2,1)S(1)}, bf16[1024,128]{1,0:T(8,128)(2,1)S(1)}, u32[]{:S(2)}, u32[]{:S(2)}) collective-permute-start(bf16[1024,128]{1,0:T(8,128)(2,1)S(1)} %collective-permute-done.10.refs_7_), channel_id=1, source_target_pairs={{0,56},{2,58},{4,60},{6,62},{8,0},{10,2},{12,4},{14,6},{16,8},{18,... | collective-permute-start | bytes 786440 | tf_op jit(solution)/shard_map/ppermute | solution.py:456
  123.1 7.7 %collective-permute-start.9 = (bf16[1024,128]{1,0:T(8,128)(2,1)S(1)}, bf16[1024,128]{1,0:T(8,128)(2,1)}, u32[]{:S(2)}, u32[]{:S(2)}) collective-permute-start(bf16[1024,128]{1,0:T(8,128)(2,1)S(1)} %collective-permute-done.8.refs_1_), channel_id=1, source_target_pairs={{0,8},{2,10},{4,12},{6,14},{8,16},{10,18},{12,20},{14,22},{16,24},... | collective-permute-start | bytes 786440 | tf_op jit(solution)/shard_map/ppermute | solution.py:456
  139.0 1.5 copy-start
  140.5 7.6 %copy-start.11 = (bf16[1024,128]{1,0:T(8,128)(2,1)S(1)}, bf16[1024,128]{1,0:T(8,128)(2,1)}, u32[]{:S(2)}) copy-start(bf16[1024,128]{1,0:T(8,128)(2,1)} %copy-done.10) | copy-start | bytes 786436
  140.5 37.6 %all-to-all-start.4 = ((bf16[16,640,128]{2,1,0:T(8,128)(2,1)}), bf16[16,640,128]{2,1,0:T(8,128)(2,1)S(1)}, u32[]{:S(2)}, u32[]{:S(2)}) async-start(bf16[16,640,128]{2,1,0:T(8,128)(2,1)} %copy-done), calls=%async_computation.4 | async-start | bytes 5242880 | tf_op jit(solution)/shard_map/all_to_all | solution.py:443
  148.1 8.8 %collective-permute-start.12 = (bf16[1024,128]{1,0:T(8,128)(2,1)}, bf16[1024,128]{1,0:T(8,128)(2,1)S(1)}, u32[]{:S(2)}, u32[]{:S(2)}) collective-permute-start(bf16[1024,128]{1,0:T(8,128)(2,1)} %collective-permute-done.9.refs_2_), channel_id=1, source_target_pairs={{0,8},{2,10},{4,12},{6,14},{8,16},{10,18},{12,20},{14,22},{16,24},... | collective-permute-start | bytes 786440 | tf_op jit(solution)/shard_map/ppermute | solution.py:456
  148.2 8.8 %collective-permute-start.14 = (bf16[1024,128]{1,0:T(8,128)(2,1)S(1)}, bf16[1024,128]{1,0:T(8,128)(2,1)S(1)}, u32[]{:S(2)}, u32[]{:S(2)}) collective-permute-start(bf16[1024,128]{1,0:T(8,128)(2,1)S(1)} %copy-done.11), channel_id=1, source_target_pairs={{0,56},{2,58},{4,60},{6,62},{8,0},{10,2},{12,4},{14,6},{16,8},{18,... | collective-permute-start | bytes 786440 | tf_op jit(solution)/shard_map/ppermute | solution.py:456
  156.9 7.6 %copy-start.13 = (bf16[1024,128]{1,0:T(8,128)(2,1)}, bf16[1024,128]{1,0:T(8,128)(2,1)S(1)}, u32[]{:S(2)}) copy-start(bf16[1024,128]{1,0:T(8,128)(2,1)S(1)} %collective-permute-done.12.refs_3_) | copy-start | bytes 786436
  156.9 7.6 %collective-permute-start.13 = (bf16[1024,128]{1,0:T(8,128)(2,1)S(1)}, bf16[1024,128]{1,0:T(8,128)(2,1)S(1)}, u32[]{:S(2)}, u32[]{:S(2)}) collective-permute-start(bf16[1024,128]{1,0:T(8,128)(2,1)S(1)} %collective-permute-done.12.refs_3_), channel_id=1, source_target_pairs={{0,8},{2,10},{4,12},{6,14},{8,16},{10,18},{12,20},{14,22},{16,24},... | collective-permute-start | bytes 786440 | tf_op jit(solution)/shard_map/ppermute | solution.py:456
  157.0 7.5 %copy-start.14 = (bf16[1024,128]{1,0:T(8,128)(2,1)}, bf16[1024,128]{1,0:T(8,128)(2,1)S(1)}, u32[]{:S(2)}) copy-start(bf16[1024,128]{1,0:T(8,128)(2,1)S(1)} %collective-permute-done.14.refs_5_) | copy-start | bytes 786436
  169.0 2.0 collective-permute-start.15
  (4 other events, 3.1 us)
